TPU v7x, 32 devices: a whole 2x2x4 slice. The times are simulated.
32 devices in a mesh: cls: 4 (over y, x), dom: 8 (over z, core).
Axes of the slice: x: 2, y: 2, z: 4, core: 2. Of those that a mesh axis runs over, the one named last changes fastest.
Arguments:
- particles: bfloat16 [8192, 4096], P('dom', 'cls'), may hold values from -6 to 8
- candidates: int32 [8192, 2], P('dom'), may hold values from 0 to 7, all different within a row; in each aligned block of 1024 rows (0 to 1023, 1024 to 2047, ...) at most 512 rows name the same one
- defocus: int32 [8192], P('dom'), may hold values from 0 to 31
- ctf_table: float32 [32, 4096], P(None, 'cls'), may hold values from -1 to 1
- references: bfloat16 [32, 4096], P('dom', 'cls'), may hold values from -5 to 5
- rotations: bfloat16 [64, 64, 64], replicated, may hold values from -0.4 to 1.1
Outputs:
- class_sums: bfloat16 [32, 4096], P('dom', 'cls')
- class_weights: float32 [32, 4096], P('dom', 'cls')
- log_evidence: float32 [8192], P('dom')
Inputs may be any that keep to these rules, and one draw needn't show every extreme that they name: The two candidates of a particle differ; among the 1024 particles of one index of dom no group is named by more than 512 entries, a bound that some block reaches.
All inputs are finite; a program needn't handle non-finite values.
Results may differ from a plain program's by a relative error of at most 0.0054.
Values may be sent and summed in bfloat16 or wider, within the bound.
No kernel may reach another device: no remote copies, remote signals or barrier semaphores. Data moves between devices by JAX's collectives and lax.ppermute only.
A program may use at most 128 MiB of HBM per device.

v0:
```python
import math

import jax
import jax.numpy as jnp
from jax import lax
from jax.sharding import PartitionSpec as P

highest = lax.Precision.HIGHEST


def route_slots(candidates, owners):
    entries = candidates.reshape(-1)
    owner_ids = lax.broadcasted_iota(jnp.int32, (entries.shape[0], owners), 1)
    onehot_owner = (entries[:, None] == owner_ids).astype(jnp.int32)
    entry_rank = jnp.cumsum(onehot_owner, axis=0) - onehot_owner
    slot_of = jnp.sum(entry_rank * onehot_owner, axis=1)
    return (entries, slot_of)


def local(particles, candidates, defocus, ctf_table, references, rotations):
    local_count, pixel_share = particles.shape
    owners = lax.axis_size("dom")
    capacity = 4 * local_count // owners
    slot_count = owners * capacity
    entries, slot_of = route_slots(candidates, owners)
    entry_ids = jnp.arange(entries.shape[0], dtype=jnp.int32)
    slot_entry = jnp.full((owners, capacity), -1, jnp.int32).at[entries, slot_of].set(entry_ids)
    send_live = slot_entry >= 0
    send_rows = jnp.maximum(slot_entry, 0) // 2
    send_pixels = jnp.where(
        send_live[:, :, None], particles[send_rows], jnp.zeros((), jnp.bfloat16)
    )
    send_defocus = jnp.where(send_live, defocus[send_rows], -1)
    arrived, arrived_defocus = (
        lax.all_to_all(send_pixels, "dom", split_axis=0, concat_axis=0, tiled=True),
        lax.all_to_all(send_defocus, "dom", split_axis=0, concat_axis=0, tiled=True),
    )
    defocus_kinds = ctf_table.shape[0]
    class_count = references.shape[0]
    turn_count = rotations.shape[0]
    angles = rotations.shape[1]
    cycle_share = pixel_share // angles
    pair_count = class_count * turn_count
    flat_defocus = arrived_defocus.reshape(slot_count)
    owner_live = flat_defocus >= 0
    kind_ids = lax.broadcasted_iota(jnp.int32, (slot_count, defocus_kinds), 1)
    picked = (flat_defocus[:, None] == kind_ids).astype(jnp.float32)
    rotated = jnp.einsum(
        "cla,rba->crlb",
        references.reshape(class_count, cycle_share, angles),
        rotations,
        preferred_element_type=jnp.float32,
    )
    rotated = rotated.astype(jnp.bfloat16).reshape(pair_count, pixel_share)
    block_rows = min(512, slot_count)
    block_count = slot_count // block_rows

    def score_block(packed):
        pixel_rows, picked_rows = packed
        ctf_rows = jnp.dot(picked_rows, ctf_table, precision=highest)
        weighted = (pixel_rows.astype(jnp.float32) * ctf_rows).astype(jnp.bfloat16)
        cross_term = lax.dot_general(
            weighted, rotated, (((1,), (1,)), ((), ())), preferred_element_type=jnp.float32
        )
        return (weighted, cross_term)

    weighted, cross_term = lax.map(
        score_block,
        (
            arrived.reshape(block_count, block_rows, pixel_share),
            picked.reshape(block_count, block_rows, defocus_kinds),
        ),
    )
    weighted = weighted.reshape(slot_count, pixel_share)
    cross_term = cross_term.reshape(slot_count, pair_count)
    ctf_power = ctf_table * ctf_table
    square = rotated.astype(jnp.float32) ** 2
    energy = lax.dot_general(ctf_power, square, (((1,), (1,)), ((), ())), precision=highest)
    partial_value = cross_term - 0.5 * jnp.dot(picked, energy, precision=highest)
    inverse_noise = 4.0 / math.sqrt(pixel_share * lax.axis_size("cls"))
    score_share = inverse_noise * lax.psum_scatter(
        partial_value, "cls", scatter_dimension=0, tiled=True
    )
    share_rows = score_share.shape[0]
    share_max = jnp.max(score_share, axis=1)
    share_sum = jnp.sum(jnp.exp(score_share - share_max[:, None]), axis=1)
    slot_max, slot_sum = (
        lax.all_gather(share_max, "cls", axis=0, tiled=True),
        lax.all_gather(share_sum, "cls", axis=0, tiled=True),
    )
    back_max = lax.all_to_all(
        slot_max.reshape(owners, capacity), "dom", split_axis=0, concat_axis=0, tiled=True
    )
    back_sum = lax.all_to_all(
        slot_sum.reshape(owners, capacity), "dom", split_axis=0, concat_axis=0, tiled=True
    )
    pair_max = back_max[entries, slot_of].reshape(local_count, 2)
    pair_sum = back_sum[entries, slot_of].reshape(local_count, 2)
    pair_best = jnp.max(pair_max, axis=1, keepdims=True)
    log_evidence = pair_best[:, 0] + jnp.log(
        jnp.sum(pair_sum * jnp.exp(pair_max - pair_best), axis=1)
    )
    send_log = jnp.where(send_live, log_evidence[send_rows], 0.0)
    slot_log = lax.all_to_all(send_log, "dom", split_axis=0, concat_axis=0, tiled=True)
    log_evidence, slot_log = (log_evidence, slot_log.reshape(slot_count))
    offset = lax.axis_index("cls") * share_rows
    share_log = lax.dynamic_slice_in_dim(slot_log, offset, share_rows)
    share_live = lax.dynamic_slice_in_dim(owner_live, offset, share_rows)
    share_weights = jnp.where(
        share_live[:, None], jnp.exp(score_share - share_log[:, None]), 0.0
    ).astype(jnp.bfloat16)
    weights = lax.all_gather(share_weights, "cls", axis=0, tiled=True)
    rot_sum = lax.dot_general(
        weights, weighted, (((0,), (0,)), ((), ())), preferred_element_type=jnp.float32
    )
    pair_kind = lax.dot_general(
        weights,
        picked.astype(jnp.bfloat16),
        (((0,), (0,)), ((), ())),
        preferred_element_type=jnp.float32,
    )
    rot_weight = jnp.dot(pair_kind, ctf_power, precision=highest)
    turn_maps = rotations.astype(jnp.float32)
    back_sum = jnp.einsum(
        "crlb,rba->cla",
        rot_sum.reshape(class_count, turn_count, cycle_share, angles),
        turn_maps,
        precision=highest,
    )
    back_weight = jnp.einsum(
        "crlb,rba->cla",
        rot_weight.reshape(class_count, turn_count, cycle_share, angles),
        turn_maps,
        precision=highest,
    )
    class_sums = back_sum.reshape(class_count, pixel_share).astype(jnp.bfloat16)
    class_weights = back_weight.reshape(class_count, pixel_share)
    return (class_sums, class_weights, log_evidence)


def solution(mesh):
    in_specs = (P("dom", "cls"), P("dom", None), P("dom"), P(None, "cls"), P("dom", "cls"), P())
    out_specs = (P("dom", "cls"), P("dom", "cls"), P("dom"))
    return jax.shard_map(local, mesh=mesh, in_specs=in_specs, out_specs=out_specs, check_vma=False)
```

profile of v0, /device:TPU:0, one launch (start us, length us, event | category | flops | bytes accessed | tf_op | source)
XLA Modules:
  0.0 513.9 jit_solution(14782615724169570176)
XLA Ops:
  13.6 8.1 %scatter_custom_fusion = s32[4096]{0:T(1024)S(1)} fusion(s32[2048]{0:T(1024)S(1)} %broadcast_select_fusion.2, s32[2048]{0:T(1024)S(1)} %iota.22, s32[]{:T(128)} %constant.23.clone.1), kind=kCustom, calls=%fused_computation.72 | custom fusion | bytes 16388
  21.8 16.7 %gather_fusion = s32[4096]{0:T(1024)S(1)} fusion(s32[1024]{0:T(1024)S(1)} %copy-done.3, s32[4096]{0:T(1024)S(1)} %broadcast_clamp_fusion), kind=kCustom, calls=%fused_computation | custom fusion | bytes 49152 | tf_op jit(solution)/shard_map/gather | solution.py:33
  39.2 6.3 %all-to-all-start = ((s32[8,1,512]{2,1,0:T(1,128)}), s32[8,1,512]{2,1,0:T(1,128)S(1)}, u32[]{:S(2)}, u32[]{:S(2)}) async-start(s32[8,1,512]{2,1,0:T(1,128)} %all_to_all.31), calls=%async_computation | async-start | bytes 32768 | tf_op jit(solution)/shard_map/all_to_all | solution.py:36
  45.5 18.3 %gather_fusion.1 = bf16[4096,1024]{1,0:T(8,128)(2,1)} fusion(bf16[1024,1024]{1,0:T(8,128)(2,1)S(1)} %copy-done, s32[4096]{0:T(1024)S(1)} %broadcast_clamp_fusion), kind=kCustom, calls=%fused_computation.1 | custom fusion | bytes 16793600 | tf_op jit(solution)/shard_map/gather | solution.py:31
  63.8 7.2 %broadcast_select_fusion = bf16[8,512,1024]{2,1,0:T(8,128)(2,1)} fusion(bf16[8,512,1024]{2,1,0:T(8,128)(2,1)} %bitcast.114, pred[8,512]{1,0:T(8,128)(4,1)S(1)} %reshape.148), kind=kLoop, calls=%fused_computation.14 | loop fusion | flops 4194304 | bytes 16781312 | tf_op jit(solution)/shard_map/jit(_where)/select_n | solution.py:30
  71.0 5.2 %all-to-all-start.1 = ((bf16[8,512,1024]{2,1,0:T(8,128)(2,1)}), bf16[8,512,1024]{2,1,0:T(8,128)(2,1)}, u32[]{:S(2)}, u32[]{:S(2)}) async-start(bf16[8,512,1024]{2,1,0:T(8,128)(2,1)} %broadcast_select_fusion), calls=%async_computation.1 | async-start | bytes 16777216 | tf_op jit(solution)/shard_map/all_to_all | solution.py:35
  83.4 176.8 %all-to-all-done.1 = bf16[8,512,1024]{2,1,0:T(8,128)(2,1)} async-done(((bf16[8,512,1024]{2,1,0:T(8,128)(2,1)}), bf16[8,512,1024]{2,1,0:T(8,128)(2,1)}, u32[]{:S(2)}, u32[]{:S(2)}) %all-to-all-start.1) | async-done | bytes 8388640 | tf_op jit(solution)/shard_map/all_to_all | solution.py:35
  260.2 4.3 broadcast_in_dim.64
  264.5 43.3 %while.12 = (s32[]{:T(128)}, bf16[8,512,1024]{2,1,0:T(8,128)(2,1)}, f32[8,512,256]{2,1,0:T(8,128)}, bf16[8,512,1024]{2,1,0:T(8,128)(2,1)}, f32[8,512,32]{2,1,0:T...) while((s32[]{:T(128)}, bf16[8,512,1024]{2,1,0:T(8,128)(2,1)}, ...), condition=%wide.region_5.6_spmd, body=%wide.region_4.5_spmd.sunk | while | flops 471334912 | bytes 5637717 | solution.py:67
  264.5 4.2 bitcast_dynamic-update-slice_fusion.2
  270.0 4.1 bitcast_dynamic-update-slice_fusion.2
  275.4 4.1 bitcast_dynamic-update-slice_fusion.2
  280.8 4.1 bitcast_dynamic-update-slice_fusion.2
  286.2 4.2 bitcast_dynamic-update-slice_fusion.2
  291.6 4.1 bitcast_dynamic-update-slice_fusion.2
  297.0 4.1 bitcast_dynamic-update-slice_fusion.2
  302.4 4.1 bitcast_dynamic-update-slice_fusion.2
  307.8 6.0 %fusion.5 = f32[4096,256]{1,0:T(8,128)} fusion(f32[4096,256]{1,0:T(8,128)} %bitcast.118, f32[32,256]{1,0:T(8,128)S(1)} %fusion.19, s32[4096]{0:T(1024)S(1)} %bitcast.120), kind=kOutput, calls=%fused_computation.16 | convolution fusion | flops 404881408 | bytes 8437760 | tf_op jit(solution)/shard_map/dot_general | solution.py:79
  313.8 51.7 %reduce-scatter.2.cloned.1.call-done = f32[1024,256]{1,0:T(8,128)} async-done(((f32[4096,256]{1,0:T(8,128)}), f32[1024,256]{1,0:T(8,128)}) %reduce-scatter.2.cloned.1.call-update) | async-done | bytes 1048592 | tf_op jit(solution)/shard_map/reduce_scatter | solution.py:81
  368.6 8.7 %all_gather.10 = f32[4096]{0:T(1024)} all-gather(f32[1024]{0:T(1024)S(1)} %exponential_reduce_fusion), channel_id=1, replica_groups=mesh['cls'=4,'dom'=8] {'cls'}, dimensions={0}, use_global_device_ids=true | all-gather | bytes 20480 | tf_op jit(solution)/shard_map/all_gather | solution.py:89
  377.3 4.6 all-to-all-start.3
  381.9 8.1 %all_gather.9 = f32[4096]{0:T(1024)} all-gather(f32[1024]{0:T(1024)S(1)} %multiply_reduce_fusion), channel_id=1, replica_groups=mesh['cls'=4,'dom'=8] {'cls'}, dimensions={0}, use_global_device_ids=true | all-gather | bytes 20480 | tf_op jit(solution)/shard_map/all_gather | solution.py:88
  390.0 5.1 all-to-all-start.2
  395.1 13.0 %gather_fusion.3 = f32[2048]{0:T(1024)S(1)} fusion(f32[8,512]{1,0:T(8,128)S(1)} %bitcast.110, s32[2048]{0:T(1024)S(1)} %bitcast.112), kind=kCustom, calls=%fused_computation.3 | custom fusion | bytes 32768 | tf_op jit(solution)/shard_map/gather | solution.py:98
  408.6 13.0 %gather_fusion.2 = f32[2048]{0:T(1024)S(1)} fusion(f32[8,512]{1,0:T(8,128)S(1)} %bitcast.111, s32[2048]{0:T(1024)S(1)} %bitcast.113), kind=kCustom, calls=%fused_computation.2 | custom fusion | bytes 32768 | tf_op jit(solution)/shard_map/gather | solution.py:97
  422.7 16.7 %gather_fusion.4 = f32[4096]{0:T(1024)S(1)} fusion(f32[1024]{0:T(1024)S(1)} %log_add_fusion, s32[4096]{0:T(1024)S(1)} %broadcast_clamp_fusion), kind=kCustom, calls=%fused_computation.4 | custom fusion | bytes 49152 | tf_op jit(solution)/shard_map/gather | solution.py:103
  440.0 5.1 all-to-all-start.4
  445.2 5.6 %all-to-all-done.4 = f32[8,1,512]{2,1,0:T(1,128)S(1)} async-done(((f32[8,1,512]{2,1,0:T(1,128)}), f32[8,1,512]{2,1,0:T(1,128)S(1)}, u32[]{:S(2)}, u32[]{:S(2)}) %all-to-all-start.4) | async-done | bytes 16416 | tf_op jit(solution)/shard_map/all_to_all | solution.py:104
  451.9 11.5 %copy.42 = bf16[4096,1024]{0,1:T(8,128)(2,1)} copy(bf16[4096,1024]{1,0:T(8,128)(2,1)} %bitcast.115) | data formatting | bytes 16777216 | tf_op jit(solution)/shard_map/reshape | solution.py:74
  463.4 21.2 %all-gather.2.cloned.1.call-done = bf16[4096,256]{1,0:T(8,128)(2,1)} async-done(((bf16[1024,256]{1,0:T(8,128)(2,1)}), bf16[4096,256]{1,0:T(8,128)(2,1)}) %all-gather.2.cloned.1.call-update) | async-done | bytes 2097168 | tf_op jit(solution)/shard_map/all_gather | solution.py:112
  492.3 4.1 copy.35
  496.4 7.7 %fusion.36 = f32[4,64,16,64]{3,1,2,0:T(8,128)S(1)} fusion(bf16[4,64,4096,1]{2,1,3,0:T(8,128)(2,1)} %bitcast.119, bf16[16,64,4096,1]{2,1,0,3:T(8,128)(2,1)} %bitcast.116), kind=kOutput, calls=%fused_computation.78 | convolution fusion | flops 2147483648 | bytes 11534336 | tf_op jit(solution)/shard_map/dot_general | solution.py:113
  (87 shorter events, 41.4 us)
Async XLA Ops:
  7.2 38.3 %copy-start = (bf16[1024,1024]{1,0:T(8,128)(2,1)S(1)}, bf16[1024,1024]{1,0:T(8,128)(2,1)}, u32[]{:S(2)}) copy-start(bf16[1024,1024]{1,0:T(8,128)(2,1)} %param.8) | copy-start | bytes 6291460
  7.2 14.6 %copy-start.3 = (s32[1024]{0:T(1024)S(1)}, s32[1024]{0:T(1024)}, u32[]{:S(2)}) copy-start(s32[1024]{0:T(1024)} %param.10) | copy-start | bytes 12292
  39.2 31.8 %all-to-all-start = ((s32[8,1,512]{2,1,0:T(1,128)}), s32[8,1,512]{2,1,0:T(1,128)S(1)}, u32[]{:S(2)}, u32[]{:S(2)}) async-start(s32[8,1,512]{2,1,0:T(1,128)} %all_to_all.31), calls=%async_computation | async-start | bytes 32768 | tf_op jit(solution)/shard_map/all_to_all | solution.py:36
  71.0 5.3 %copy-start.7 = (bf16[4,1024]{1,0:T(4,128)(2,1)S(1)}, bf16[4,1024]{1,0:T(4,128)(2,1)}, u32[]{:S(2)}) copy-start(bf16[4,1024]{1,0:T(4,128)(2,1)} %param.12) | copy-start | bytes 24580
  71.0 5.4 %copy-start.5 = (bf16[64,64,64]{2,1,0:T(8,128)(2,1)S(1)}, bf16[64,64,64]{2,1,0:T(8,128)(2,1)}, u32[]{:S(2)}) copy-start(bf16[64,64,64]{2,1,0:T(8,128)(2,1)} %param.13) | copy-start | bytes 1572868
  71.0 189.2 %all-to-all-start.1 = ((bf16[8,512,1024]{2,1,0:T(8,128)(2,1)}), bf16[8,512,1024]{2,1,0:T(8,128)(2,1)}, u32[]{:S(2)}, u32[]{:S(2)}) async-start(bf16[8,512,1024]{2,1,0:T(8,128)(2,1)} %broadcast_select_fusion), calls=%async_computation.1 | async-start | bytes 16777216 | tf_op jit(solution)/shard_map/all_to_all | solution.py:35
  76.2 4.4 copy-start.6
  76.2 289.3 %reduce-scatter.2.cloned.1.call-start = ((), (), s32[]{:S(2)}) async-start(), calls=%async_computation.6 | async-start | bytes 5242880 | tf_op jit(solution)/shard_map/reduce_scatter | solution.py:81
  377.3 12.7 %all-to-all-start.3 = ((f32[8,1,512]{2,1,0:T(1,128)}), f32[8,1,512]{2,1,0:T(1,128)S(1)}, u32[]{:S(2)}, u32[]{:S(2)}) async-start(f32[8,1,512]{2,1,0:T(1,128)} %bitcast.14), calls=%async_computation.4 | async-start | bytes 32768 | tf_op jit(solution)/shard_map/all_to_all | solution.py:94
  390.0 18.6 %all-to-all-start.2 = ((f32[8,1,512]{2,1,0:T(1,128)}), f32[8,1,512]{2,1,0:T(1,128)S(1)}, u32[]{:S(2)}, u32[]{:S(2)}) async-start(f32[8,1,512]{2,1,0:T(1,128)} %bitcast.12), calls=%async_computation.3 | async-start | bytes 32768 | tf_op jit(solution)/shard_map/all_to_all | solution.py:91
  422.6 16.7 %copy-start.2 = (f32[1024]{0:T(1024)}, f32[1024]{0:T(1024)S(1)}, u32[]{:S(2)}) copy-start(f32[1024]{0:T(1024)S(1)} %log_add_fusion) | copy-start | bytes 12292
  422.7 28.1 %copy-start.4 = (f32[1024,256]{1,0:T(8,128)S(1)}, f32[1024,256]{1,0:T(8,128)}, u32[]{:S(2)}) copy-start(f32[1024,256]{1,0:T(8,128)} %reduce-scatter.2.cloned.1.call-done) | copy-start | bytes 3145732
  440.0 10.7 %all-to-all-start.4 = ((f32[8,1,512]{2,1,0:T(1,128)}), f32[8,1,512]{2,1,0:T(1,128)S(1)}, u32[]{:S(2)}, u32[]{:S(2)}) async-start(f32[8,1,512]{2,1,0:T(1,128)} %copy.34), calls=%async_computation.5 | async-start | bytes 32768 | tf_op jit(solution)/shard_map/all_to_all | solution.py:104
  445.1 39.6 %all-gather.2.cloned.1.call-start = ((), (), s32[]{:S(2)}) async-start(), calls=%async_computation.7 | async-start | bytes 2621440 | tf_op jit(solution)/shard_map/all_gather | solution.py:112
  496.4 10.6 %copy-start.1 = (bf16[1024,1024]{1,0:T(8,128)(2,1)S(1)}, bf16[1024,1024]{1,0:T(8,128)(2,1)}, u32[]{:S(2)}) copy-start(bf16[1024,1024]{1,0:T(8,128)(2,1)} %param.8) | copy-start | bytes 6291460
Sparse Core Ops, SparseCore 0:
  313.9 51.5 reduce-scatter.1
  452.0 32.5 all-gather.1
where the time goes:
time: 515 us; the launch traced here: 514 us
  waiting for transfers between devices  255 us (50%)
  local copies, waits for them, and re-layouts  116 us (23%)
  matrix products  66.6 us (13%)
  starting transfers between devices  26.4 us (5%)
  other arithmetic  17.9 us (3%)
  blocking collectives  16.7 us (3%)
  between operations  14.4 us (3%)
    all_to_all x1, waiting for transfers between devices, local(): lax.all_to_all(send_pixels, 'dom', split_axis=0, concat_axis=0, tiled=True)  177 us
    reduce_scatter x1, waiting for transfers between devices, local(): lax.psum_scatter(partial_value, 'cls', scatter_dimension=0, tiled=True)  51.7 us
    dot_general x8, matrix products, score_block(): ctf_rows = jnp.dot(picked_rows, ctf_table, precision=highest)  33.1 us
    all_gather x1, waiting for transfers between devices, local(): weights = lax.all_gather(share_weights, 'cls', axis=0, tiled=True)  21.2 us
    gather x1, local copies, waits for them, and re-layouts, local(): particles[send_rows]  18.3 us
    gather x2, local copies, waits for them, and re-layouts, local(): send_defocus = jnp.where(send_live, defocus[send_rows], -1)  16.7 us
    gather x2, local copies, waits for them, and re-layouts, local(): send_log = jnp.where(send_live, log_evidence[send_rows], 0.0)  16.7 us
    gather x1, local copies, waits for them, and re-layouts, local(): pair_sum = back_sum[entries, slot_of].reshape(local_count, 2)  13 us
  transfers between devices with their start and end apart: 7, of which 4 were waited for; matrix products, arithmetic and copies ran while one was open for 11% of the time, Pallas kernels for 0%

commit v1 on v0

v1 whole, which is shorter than its diff:
```python
import functools
import math

import jax
import jax.numpy as jnp
from jax import lax
from jax.experimental import pallas as pl
from jax.experimental.pallas import tpu as pltpu
from jax.sharding import PartitionSpec as P

f32, bf16 = jnp.float32, jnp.bfloat16
VMEM = pl.BlockSpec(memory_space=pltpu.VMEM)
SMEM = pl.BlockSpec(memory_space=pltpu.SMEM)
BLOCK = 32
NN = (((1,), (0,)), ((), ()))
NT = (((1,), (1,)), ((), ()))
TN = (((0,), (0,)), ((), ()))


def dot(a, b, dims):
    return lax.dot_general(a, b, dims, preferred_element_type=f32)


def split3(x):
    hi = x.astype(bf16)
    rest = x - hi.astype(f32)
    mid = rest.astype(bf16)
    return hi, mid, (rest - mid.astype(f32)).astype(bf16)


def one_hot(row, kinds, copies):
    ids = lax.broadcasted_iota(jnp.int32, (kinds, row.shape[1]), 0)
    hit = jnp.where(ids == row, 1.0, 0.0).astype(bf16)
    return jnp.concatenate([hit] * copies, axis=0)


def diagonal(turn2, angles, width):
    wide = jnp.concatenate([turn2] * (width // (2 * angles)), axis=1)
    tall = jnp.concatenate([wide] * (width // angles), axis=0)
    row = lax.broadcasted_iota(jnp.int32, (width, width), 0) // angles
    col = lax.broadcasted_iota(jnp.int32, (width, width), 1) // angles
    return jnp.where(row == col, tall, jnp.zeros((), bf16))


def weigh_kernel(pixels, kind, table, out):
    table3 = jnp.concatenate(split3(table[...]), axis=0)
    hit3 = one_hot(kind[...], table.shape[0], 3)
    rows = dot(hit3, table3, TN)
    out[...] = (pixels[...].astype(f32) * rows).astype(bf16)


def weigh(particles, kind, table):
    count, pixels = particles.shape
    rows = math.gcd(count, 256)
    return pl.pallas_call(
        weigh_kernel,
        grid=(count // rows,),
        in_specs=[
            pl.BlockSpec((rows, pixels), lambda i: (i, 0)),
            pl.BlockSpec((1, rows), lambda i: (0, i)),
            pl.BlockSpec(table.shape, lambda i: (0, 0)),
        ],
        out_specs=pl.BlockSpec((rows, pixels), lambda i: (i, 0)),
        out_shape=jax.ShapeDtypeStruct((count, pixels), bf16),
        compiler_params=pltpu.CompilerParams(vmem_limit_bytes=40 << 20),
        cost_estimate=pl.CostEstimate(
            flops=2 * count * pixels * 96, bytes_accessed=4 * count * pixels, transcendentals=0
        ),
        name="weigh",
    )(particles, kind, table)


def rotate_kernel(refs, turns, table, rotated, energy, mean, wide, center):
    classes, pixels = refs.shape
    turn_count, angles, _ = turns.shape
    width = min(256, pixels)
    quads = pixels // width
    lhs = jnp.concatenate([refs[:, q * width:(q + 1) * width] for q in range(quads)], axis=0)

    def turn(r, carry):
        matrix = diagonal(turns[r], angles, width)
        product = dot(lhs, matrix, NT)
        for q in range(quads):
            for t in range(width // 128):
                wide[q * (width // 128) + t, pl.ds(r, classes, stride=turn_count), :] = product[
                    q * classes:(q + 1) * classes, t * 128:(t + 1) * 128
                ]
        return carry

    lax.fori_loop(0, turn_count, turn, 0, unroll=4)
    power = table[...] * table[...]
    kinds = power.shape[0]
    power2 = jnp.concatenate(split3(power)[:2], axis=0)
    pairs = classes * turn_count
    rows = 256

    def part(i, carry):
        at = pl.ds(pl.multiple_of(i * rows, rows), rows)
        total = jnp.zeros((rows, 2 * kinds), f32)
        for t in range(pixels // 128):
            value = wide[t, at, :].astype(bf16)
            rotated[at, t * 128:(t + 1) * 128] = value
        for q in range(quads):
            value = rotated[at, q * width:(q + 1) * width].astype(f32)
            square = value * value
            hi = square.astype(bf16)
            lo = (square - hi.astype(f32)).astype(bf16)
            own = power2[:, q * width:(q + 1) * width]
            total = total + dot(hi, own, NT) + dot(lo, own, NT)
        total = -0.5 * (total[:, :kinds] + total[:, kinds:])
        energy[at, :] = total
        return carry + jnp.sum(total, axis=0, keepdims=True)

    summed = lax.fori_loop(0, pairs // rows, part, jnp.zeros((1, kinds), f32))

    @pl.when(pl.program_id(0) == 0)
    def _():
        center[...] = summed * (1.0 / pairs)

    mean[...] = center[...]


def rotate(refs, turns2, table):
    classes, pixels = refs.shape
    turn_count = turns2.shape[0]
    kinds = table.shape[0]
    block = min(BLOCK, classes)
    pairs = block * turn_count
    return pl.pallas_call(
        rotate_kernel,
        grid=(classes // block,),
        in_specs=[
            pl.BlockSpec((block, pixels), lambda i: (i, 0)),
            pl.BlockSpec(turns2.shape, lambda i: (0, 0, 0)),
            pl.BlockSpec(table.shape, lambda i: (0, 0)),
        ],
        out_specs=[
            pl.BlockSpec((pairs, pixels), lambda i: (i, 0)),
            pl.BlockSpec((pairs, kinds), lambda i: (i, 0)),
            pl.BlockSpec((1, kinds), lambda i: (0, 0)),
        ],
        out_shape=[
            jax.ShapeDtypeStruct((classes * turn_count, pixels), bf16),
            jax.ShapeDtypeStruct((classes * turn_count, kinds), f32),
            jax.ShapeDtypeStruct((1, kinds), f32),
        ],
        scratch_shapes=[
            pltpu.VMEM((pixels // 128, pairs, 128), f32),
            pltpu.VMEM((1, kinds), f32),
        ],
        compiler_params=pltpu.CompilerParams(vmem_limit_bytes=50 << 20),
        cost_estimate=pl.CostEstimate(
            flops=8 * classes * turn_count * pixels * 64,
            bytes_accessed=2 * classes * turn_count * pixels,
            transcendentals=0,
        ),
        name="rotate",
    )(refs, turns2, table)


def score_kernel(groups, scale, me, weighted, kind, names, rotated, energy, mean, own, *rest):
    others, acc = rest[:-1], rest[-1]
    step = pl.program_id(0)
    count = weighted.shape[0]
    kinds = energy.shape[1]
    pairs = rotated.shape[0] // groups
    span = min(256, count)
    for n in range(count // span):
        cols = pl.ds(n * span, span)
        hit3 = one_hot(kind[:, cols], kinds, 3)
        first, second = names[0:1, cols], names[1:2, cols]
        pix = weighted[cols, :]
        for g in range(groups):
            at = pl.ds(g * pairs, pairs)
            shift = jnp.concatenate(split3(energy[at, :] - mean[...]), axis=1)
            value = scale * (dot(rotated[at, :], pix, NT) + dot(shift, hit3, NN))
            group = step * groups + g
            for k, name in enumerate((first, second)):
                rows = pl.ds(k * pairs, pairs)
                if g == 0:
                    base = jnp.where(step == 0, jnp.zeros_like(value), acc[rows, cols])
                    acc[rows, cols] = jnp.where(name == group, value, base)
                else:
                    acc[rows, cols] = jnp.where(name == group, value, acc[rows, cols])

    @pl.when(step == pl.num_programs(0) - 1)
    def _():
        share = own.shape[1]
        for k, out in enumerate((own,) + others):
            start = pl.multiple_of((me[0] ^ k) * share, share)
            out[...] = acc[:, pl.ds(start, share)]


def score(weighted, kind, names, rotated, energy, mean, me, peers, group_pairs, scale):
    count, pixels = weighted.shape
    kinds = energy.shape[1]
    groups_all = rotated.shape[0] // group_pairs
    groups = math.gcd(groups_all, 8)
    share = count // peers
    rows = 2 * group_pairs
    out = pl.BlockSpec((rows, share), lambda i: (0, 0))
    return pl.pallas_call(
        functools.partial(score_kernel, groups, scale),
        grid=(groups_all // groups,),
        in_specs=[
            SMEM,
            pl.BlockSpec((count, pixels), lambda i: (0, 0)),
            pl.BlockSpec((1, count), lambda i: (0, 0)),
            pl.BlockSpec((2, count), lambda i: (0, 0)),
            pl.BlockSpec((groups * group_pairs, pixels), lambda i: (i, 0)),
            pl.BlockSpec((groups * group_pairs, kinds), lambda i: (i, 0)),
            pl.BlockSpec((1, kinds), lambda i: (0, 0)),
        ],
        out_specs=[out] * peers,
        out_shape=[jax.ShapeDtypeStruct((rows, share), f32)] * peers,
        scratch_shapes=[pltpu.VMEM((rows, count), f32)],
        compiler_params=pltpu.CompilerParams(vmem_limit_bytes=50 << 20),
        cost_estimate=pl.CostEstimate(
            flops=2 * rotated.shape[0] * pixels * count,
            bytes_accessed=2 * rotated.shape[0] * pixels,
            transcendentals=0,
        ),
        name="score",
    )(me, weighted, kind, names, rotated, energy, mean)


def soften_kernel(scores, mean, out):
    value = scores[...]
    rows, share = value.shape
    top = jnp.max(value, axis=0, keepdims=True)
    grown = jnp.exp(value - top)
    total = jnp.sum(grown, axis=0, keepdims=True)
    out[:rows, :] = (grown * (1.0 / total)).astype(bf16)
    kinds = mean.shape[1]
    centers = mean[...]
    if kinds < share:
        centers = jnp.concatenate([centers, jnp.zeros((1, share - kinds), f32)], axis=1)
    tail = jnp.zeros((16, share), f32)
    at = lax.broadcasted_iota(jnp.int32, tail.shape, 0)
    for i, row in enumerate(split3(top + jnp.log(total)) + split3(centers)):
        tail = jnp.where(at == i, row.astype(f32), tail)
    out[rows:, :] = tail.astype(bf16)


def soften(scores, mean):
    rows, share = scores.shape
    return pl.pallas_call(
        soften_kernel,
        in_specs=[VMEM, VMEM],
        out_specs=VMEM,
        out_shape=jax.ShapeDtypeStruct((rows + 16, share), bf16),
        cost_estimate=pl.CostEstimate(
            flops=4 * rows * share, bytes_accessed=6 * rows * share, transcendentals=rows * share
        ),
        name="soften",
    )(scores, mean)


def collect_kernel(groups, scale, peers, chunks, me, kind, names, weighted, turns, table, *rest):
    blocks = rest[:peers * chunks]
    sums, logs, weights, rot_sum, rot_weight = rest[peers * chunks:]
    step = pl.program_id(0)
    count, pixels = weighted.shape
    kinds = table.shape[0]
    turn_count, angles, _ = turns.shape
    share = blocks[0].shape[1]
    rows = weights.shape[0]
    pairs = rows // 2
    classes = groups * pairs // turn_count
    tiles = pixels // 128

    @pl.when(step == 0)
    def _():
        center = jnp.zeros((1, share), f32)
        for k in range(peers):
            for c in range(chunks):
                block = blocks[c * peers + k]
                start = pl.multiple_of((c * peers + (me[0] ^ k)) * share, share)
                weights[:, pl.ds(start, share)] = block[:rows, :]
                tail = block[rows:, :].astype(f32)
                logs[0:1, pl.ds(start, share)] = tail[0:1] + tail[1:2] + tail[2:3]
                if c == 0:
                    center = center + (tail[3:4] + tail[4:5] + tail[5:6])
        center3 = jnp.concatenate([part.astype(f32) for part in split3(center[:, :kinds])], axis=0)
        center3 = jnp.concatenate([center3, jnp.zeros((13, kinds), f32)], axis=0).astype(bf16)
        moved = dot(center3, one_hot(kind[...], kinds, 1), NN)
        logs[...] = logs[...] + scale * jnp.sum(moved, axis=0, keepdims=True)

    hit = one_hot(kind[...], kinds, 1)
    power = table[...] * table[...]
    power3 = jnp.concatenate(split3(power)[:2], axis=0)
    first, second = names[0:1, :], names[1:2, :]
    zero = jnp.zeros((), bf16)
    for g in range(groups):
        group = step * groups + g
        dense = jnp.where(first == group, weights[:pairs, :], zero) + jnp.where(
            second == group, weights[pairs:, :], zero
        )
        at = pl.ds(g * pairs, pairs)
        by_kind = dot(dense, hit, NT)
        hi = by_kind.astype(bf16)
        lo = (by_kind - hi.astype(f32)).astype(bf16)
        value = dot(dense, weighted[...], NN)
        for t in range(tiles):
            rot_sum[t, at, :] = value[:, t * 128:(t + 1) * 128]
        value = dot(jnp.concatenate([hi, hi], axis=1), power3, NN) + dot(lo, power3[:kinds], NN)
        for t in range(tiles):
            rot_weight[t, at, :] = value[:, t * 128:(t + 1) * 128]

    width = min(256, pixels)
    quads = pixels // width
    per = width // 128

    def turn(r, carry):
        matrix = diagonal(turns[r], angles, width)
        at = pl.ds(r, classes, stride=turn_count)
        parts = []
        for source in (rot_sum, rot_weight):
            for q in range(quads):
                parts.append(jnp.concatenate([source[q * per + t, at, :] for t in range(per)], axis=1))
        lhs = jnp.concatenate(parts, axis=0)
        hi = lhs.astype(bf16)
        lo = (lhs - hi.astype(f32)).astype(bf16)
        return carry + dot(hi, matrix, NN) + dot(lo, matrix, NN)

    total = lax.fori_loop(0, turn_count, turn, jnp.zeros((2 * quads * classes, width), f32), unroll=2)
    for q in range(2 * quads):
        sums[:, q * width:(q + 1) * width] = total[q * classes:(q + 1) * classes, :]


def collect(blocks, chunks, kind, names, weighted, turns2, table, me, group_pairs, groups_all, scale):
    count, pixels = weighted.shape
    turn_count = turns2.shape[0]
    peers = len(blocks) // chunks
    groups = math.gcd(groups_all, 8)
    classes = groups * group_pairs // turn_count
    whole = lambda a: pl.BlockSpec(a.shape, lambda i: (0,) * a.ndim)
    return pl.pallas_call(
        functools.partial(collect_kernel, groups, scale, peers, chunks),
        grid=(groups_all // groups,),
        in_specs=[SMEM] + [whole(a) for a in (kind, names, weighted, turns2, table)] + [whole(b) for b in blocks],
        out_specs=[
            pl.BlockSpec((classes, 2 * pixels), lambda i: (i, 0)),
            pl.BlockSpec((1, count), lambda i: (0, 0)),
        ],
        out_shape=[
            jax.ShapeDtypeStruct((groups_all * group_pairs // turn_count, 2 * pixels), f32),
            jax.ShapeDtypeStruct((1, count), f32),
        ],
        scratch_shapes=[
            pltpu.VMEM((2 * group_pairs, count), bf16),
            pltpu.VMEM((pixels // 128, groups * group_pairs, 128), f32),
            pltpu.VMEM((pixels // 128, groups * group_pairs, 128), f32),
        ],
        compiler_params=pltpu.CompilerParams(vmem_limit_bytes=56 << 20),
        cost_estimate=pl.CostEstimate(
            flops=4 * groups_all * group_pairs * pixels * count,
            bytes_accessed=4 * count * pixels,
            transcendentals=0,
        ),
        name="collect",
    )(me, kind, names, weighted, turns2, table, *blocks)


def swap(x, axis, k):
    return lax.ppermute(x, axis, [(i, i ^ k) for i in range(lax.axis_size(axis))])


def gather_dom(x):
    size = lax.axis_size("dom")
    if size & (size - 1) or size > 8:
        return lax.all_gather(x, "dom", axis=0, tiled=True)
    here = lax.axis_index("dom")
    out = jnp.zeros((size,) + x.shape, x.dtype)
    for k in range(size):
        out = lax.dynamic_update_index_in_dim(out, swap(x, "dom", k) if k else x, here ^ k, 0)
    return out.reshape((size * x.shape[0],) + x.shape[1:])


def scatter_dom(x):
    size = lax.axis_size("dom")
    if size & (size - 1) or size > 8:
        return lax.psum_scatter(x, "dom", scatter_dimension=0, tiled=True)
    here = lax.axis_index("dom")
    x = x.reshape((size, x.shape[0] // size) + x.shape[1:])
    pick = lambda k: lax.dynamic_index_in_dim(x, here ^ k, 0, keepdims=False)
    total = pick(0)
    for k in range(1, size):
        total = total + swap(pick(k), "dom", k)
    return total


def local(particles, candidates, defocus, ctf_table, references, rotations):
    count, pixels = particles.shape
    peers = lax.axis_size("cls")
    turn_count = rotations.shape[0]
    group_pairs = references.shape[0] * turn_count
    groups = lax.axis_size("dom")
    scale = 4.0 / math.sqrt(pixels * peers)
    me = lax.axis_index("cls").astype(jnp.int32).reshape(1)
    kind = defocus.reshape(1, count)
    names = candidates.T
    turns2 = jnp.concatenate([rotations, rotations], axis=2)
    all_refs = gather_dom(references)
    weighted = weigh(particles, kind, ctf_table)
    rotated, energy, mean = rotate(all_refs, turns2, ctf_table)
    chunks = 2
    size = count // chunks
    blocks = []
    for c in range(chunks):
        at = slice(c * size, (c + 1) * size)
        cut = score(
            weighted[at], kind[:, at], names[:, at], rotated, energy, mean, me, peers, group_pairs, scale
        )
        total = cut[0]
        for k in range(1, peers):
            total = total + swap(cut[k].astype(jnp.float16), "cls", k).astype(f32)
        own = soften(total, mean)
        blocks.extend([own] + [swap(own, "cls", k) for k in range(1, peers)])
    sums, logs = collect(
        blocks, chunks, kind, names, weighted, turns2, ctf_table, me, group_pairs, groups, scale
    )
    total = scatter_dom(sums)
    return total[:, :pixels].astype(bf16), total[:, pixels:], logs.reshape(count)


def solution(mesh):
    in_specs = (P("dom", "cls"), P("dom", None), P("dom"), P(None, "cls"), P("dom", "cls"), P())
    out_specs = (P("dom", "cls"), P("dom", "cls"), P("dom"))
    return jax.shard_map(local, mesh=mesh, in_specs=in_specs, out_specs=out_specs, check_vma=False)
```

time: 515 us -> 121 us (0.23)
  waiting for transfers between devices: 255 us -> 14.6 us
  local copies, waits for them, and re-layouts: 116 us -> 9.46 us
  matrix products: 66.6 us -> 0 us
  Pallas kernels: 0 us -> 59.6 us
  blocking collectives: 16.7 us -> 0 us
  other arithmetic: 17.9 us -> 4 us
  between operations: 14.4 us -> 0.95 us
  starting transfers between devices: 26.4 us -> 31.9 us
    all_to_all x5 -> x0, waiting for transfers between devices: 182 us -> none  [the longest x1 177 us: local(): lax.all_to_all(send_pixels, 'dom', split_axis=0, concat_axis=0, tiled=True)]
    gather x7 -> x0, local copies, waits for them, and re-layouts: 77.6 us -> none  [the longest x1 18.3 us: local(): particles[send_rows]]
    dot_general x24 -> x0, matrix products: 66.6 us -> none  [the longest x8 33.1 us: score_block(): ctf_rows = jnp.dot(picked_rows, ctf_table, precision=highest)]
    pallas_call x0 -> x7, Pallas kernels: none -> 59.6 us  [the longest x1 29.1 us: collect(): pl.pallas_call(functools.partial(collect_kernel, groups, scale, peers, ch...]
    reduce_scatter x1 -> x0, waiting for transfers between devices: 51.7 us -> none  [local(): lax.psum_scatter(partial_value, 'cls', scatter_dimension=0, tiled=True)]
    ppermute x0 -> x26, starting transfers between devices: none -> 31.9 us  [swap(): lax.ppermute(x, axis, [(i, i ^ k) for i in range(lax.axis_size(axis))])]
    all_to_all x5 -> x0, starting transfers between devices: 26.4 us -> none  [the longest x1 6.33 us: local(): lax.all_to_all(send_defocus, 'dom', split_axis=0, concat_axis=0, tiled=True)]
    all_gather x1 -> x0, waiting for transfers between devices: 21.2 us -> none  [local(): weights = lax.all_gather(share_weights, 'cls', axis=0, tiled=True)]
  transfers between devices with their start and end apart: 7 -> 26, of which waited for: 4 -> 10; matrix products, arithmetic and copies ran while one was open for 11% -> 6% of each run, Pallas kernels for 0% -> 8%
where the time goes in v1:
time: 121 us; the launch traced here: 120 us
  Pallas kernels  59.6 us (49%)
  starting transfers between devices  31.9 us (26%)
  waiting for transfers between devices  14.6 us (12%)
  local copies, waits for them, and re-layouts  9.46 us (8%)
  other arithmetic  4 us (3%)
    ppermute x26, starting transfers between devices, swap(): lax.ppermute(x, axis, [(i, i ^ k) for i in range(lax.axis_size(axis))])  31.9 us
    pallas_call x1, Pallas kernels, collect(): pl.pallas_call(functools.partial(collect_kernel, groups, scale, peers, ch...  29.1 us
    pallas_call x1, Pallas kernels, rotate(): pl.pallas_call(rotate_kernel, grid=(classes // block,), in_specs=[pl.Bloc...  15.1 us
    ppermute x26, waiting for transfers between devices, swap(): lax.ppermute(x, axis, [(i, i ^ k) for i in range(lax.axis_size(axis))])  14.6 us
    pallas_call x2, Pallas kernels, score(): pl.pallas_call(functools.partial(score_kernel, groups, scale), grid=(grou...  10.5 us
    unnamed x30, local copies, waits for them, and re-layouts  4.25 us
    pallas_call x2, Pallas kernels, soften(): pl.pallas_call(soften_kernel, in_specs=[VMEM, VMEM], out_specs=VMEM, out_...  3.49 us
  transfers between devices with their start and end apart: 26, of which 10 were waited for; matrix products, arithmetic and copies ran while one was open for 6% of the time, Pallas kernels for 8%

profile of v1, /device:TPU:0, one launch (start us, length us, event | category | flops | bytes accessed | tf_op | source)
XLA Modules:
  0.0 120.4 jit_solution(5052233429438915845)
XLA Ops:
  0.6 3.5 %collective-permute-start.4 = (bf16[4,1024]{1,0:T(4,128)(2,1)}, bf16[4,1024]{1,0:T(4,128)(2,1)S(1)}, u32[]{:S(2)}, u32[]{:S(2)}) collective-permute-start(bf16[4,1024]{1,0:T(4,128)(2,1)} %param.10), channel_id=1, source_target_pairs={{0,5},{1,4},{2,7},{3,6},{4,1},{5,0},{6,3},{7,2},{8,13},{9,12},{10,... | collective-permute-start | bytes 24584 | tf_op jit(solution)/shard_map/ppermute | solution.py:366
  4.8 1.3 %collective-permute-start.2 = (bf16[4,1024]{1,0:T(4,128)(2,1)}, bf16[4,1024]{1,0:T(4,128)(2,1)S(1)}, u32[]{:S(2)}, u32[]{:S(2)}) collective-permute-start(bf16[4,1024]{1,0:T(4,128)(2,1)} %param.10), channel_id=1, source_target_pairs={{0,3},{1,2},{2,1},{3,0},{4,7},{5,6},{6,5},{7,4},{8,11},{9,10},{10,... | collective-permute-start | bytes 24584 | tf_op jit(solution)/shard_map/ppermute | solution.py:366
  8.1 1.6 %copy-done.1 = bf16[1024,1024]{1,0:T(8,128)(2,1)S(1)} copy-done((bf16[1024,1024]{1,0:T(8,128)(2,1)S(1)}, bf16[1024,1024]{1,0:T(8,128)(2,1)}, u32[]{:S(2)}) %copy-start.1) | copy-done | bytes 2097176
  9.7 0.9 copy-done.4
  11.3 1.3 %weigh.1.weighted = bf16[1024,1024]{1,0:T(8,128)(2,1)S(1)} custom-call(bf16[1024,1024]{1,0:T(8,128)(2,1)S(1)} %copy-done.1, s32[1,1024]{1,0:T(1,128)S(1)} %bitcast.50, f32[32,1024]{1,0:T(8,128)S(1)} %copy-done.4), custom_call_target="tpu_custom_call" | custom-call | flops 201326592 | bytes 4194304 | tf_op jit(solution)/shard_map/weigh/pallas_call | solution.py:55
  12.6 1.4 %fusion.6 = (bf16[512,1024]{1,0:T(8,128)(2,1)}, bf16[512,1024]{1,0:T(8,128)(2,1)S(1)}) fusion(bf16[1024,1024]{1,0:T(8,128)(2,1)S(1)} %weigh.1.weighted), kind=kLoop, calls=%fused_computation.26 | loop fusion | bytes 4194304 | tf_op jit(solution)/shard_map/slice | solution.py:413
  14.4 2.3 %pad_maximum_fusion.turns = bf16[64,64,128]{2,1,0:T(8,128)(2,1)S(1)} fusion(bf16[64,64,64]{2,1,0:T(8,128)(2,1)} %param.11), kind=kLoop, calls=%fused_computation | loop fusion | flops 2097152 | bytes 1572864 | tf_op jit(solution)/shard_map/concatenate | solution.py:403
  16.8 3.7 %collective-permute-start.6 = (bf16[4,1024]{1,0:T(4,128)(2,1)S(1)}, bf16[4,1024]{1,0:T(4,128)(2,1)S(1)}, u32[]{:S(2)}, u32[]{:S(2)}) collective-permute-start(bf16[4,1024]{1,0:T(4,128)(2,1)S(1)} %copy-done.8), channel_id=1, source_target_pairs={{0,7},{1,6},{2,5},{3,4},{4,3},{5,2},{6,1},{7,0},{8,15},{9,14},{10,... | collective-permute-start | bytes 24584 | tf_op jit(solution)/shard_map/ppermute | solution.py:366
  20.8 5.2 %collective-permute-done.5 = bf16[4,1024]{1,0:T(4,128)(2,1)S(1)} collective-permute-done((bf16[4,1024]{1,0:T(4,128)(2,1)S(1)}, bf16[4,1024]{1,0:T(4,128)(2,1)S(1)}, u32[]{:S(2)}, u32[]{:S(2)}) %collective-permute-start.5) | collective-permute-done | bytes 8224 | tf_op jit(solution)/shard_map/ppermute | solution.py:366
  26.1 15.1 %rotate.1 = (bf16[2048,1024]{1,0:T(8,128)(2,1)}, f32[2048,32]{1,0:T(8,128)S(1)}, f32[1,32]{1,0:T(1,128)S(1)}) custom-call(bf16[32,1024]{1,0:T(8,128)(2,1)S(1)} %reshape.23.refs, bf16[64,64,128]{2,1,0:T(8,128)(2,1)S(1)} %pad_maximum_fusion.turns, f32[32,1024]{1,0:T(8,128)S(1)} %copy-done.5), custom_call_target="tpu_custom_call" | custom-call | flops 1073741824 | bytes 4194304 | tf_op jit(solution)/shard_map/rotate/pallas_call | solution.py:129
  41.2 5.3 %score.3 = (f32[512,128]{1,0:T(8,128)S(1)}, f32[512,128]{1,0:T(8,128)S(1)}, f32[512,128]{1,0:T(8,128)S(1)}, f32[512,128]{1,0:T(8,128)S(1)}) custom-call(s32[1]{0:T(128)} %bitcast.me, bf16[512,1024]{1,0:T(8,128)(2,1)S(1)} %copy-done.3, s32[1,512]{1,0:T(1,128)S(1)} %get-tuple-element.40.kind, s32[2,512]{1,0:T(2,128)S(1)} %get-tuple-element.38.names, ...), custom_call_target="tpu_custom_call" | custom-call | flops 2147483648 | bytes 4194304 | tf_op jit(solution)/shard_map/score/pallas_call | solution.py:202
  46.5 2.5 %collective-permute-start.15 = (f16[512,128]{1,0:T(8,128)(2,1)S(1)}, f16[512,128]{1,0:T(8,128)(2,1)S(1)}, u32[]{:S(2)}, u32[]{:S(2)}) collective-permute-start(f16[512,128]{1,0:T(8,128)(2,1)S(1)} %convert_element_type.47), channel_id=1, source_target_pairs={{0,24},{8,16},{16,8},{24,0},{1,25},{9,17},{17,9},{25,1},{2,26},{10... | collective-permute-start | bytes 393224 | tf_op jit(solution)/shard_map/ppermute | solution.py:366
  50.1 5.3 %score.2 = (f32[512,128]{1,0:T(8,128)S(1)}, f32[512,128]{1,0:T(8,128)S(1)}, f32[512,128]{1,0:T(8,128)S(1)}, f32[512,128]{1,0:T(8,128)S(1)}) custom-call(s32[1]{0:T(128)} %bitcast.me, bf16[512,1024]{1,0:T(8,128)(2,1)S(1)} %get-tuple-element.30.weighted, s32[1,512]{1,0:T(1,128)S(1)} %get-tuple-element.41.kind, s32[2,512]{1,0:T(2,128)S(1)} %get-tuple-element.39.names, ...), custom_call_target="tpu_custom_call" | custom-call | flops 2147483648 | bytes 4194304 | tf_op jit(solution)/shard_map/score/pallas_call | solution.py:202
  55.4 2.5 %collective-permute-start.9 = (f16[512,128]{1,0:T(8,128)(2,1)S(1)}, f16[512,128]{1,0:T(8,128)(2,1)S(1)}, u32[]{:S(2)}, u32[]{:S(2)}) collective-permute-start(f16[512,128]{1,0:T(8,128)(2,1)S(1)} %convert_element_type.41), channel_id=1, source_target_pairs={{0,24},{8,16},{16,8},{24,0},{1,25},{9,17},{17,9},{25,1},{2,26},{10... | collective-permute-start | bytes 393224 | tf_op jit(solution)/shard_map/ppermute | solution.py:366
  59.0 0.8 convert_add_fusion.scores
  59.8 1.7 %soften.3.rest_4_ = bf16[528,128]{1,0:T(8,128)(2,1)} custom-call(f32[512,128]{1,0:T(8,128)} %convert_add_fusion.scores, f32[1,32]{1,0:T(1,128)} %copy-done.7), custom_call_target="tpu_custom_call" | custom-call | flops 262144 | bytes 393216 | tf_op jit(solution)/shard_map/soften/pallas_call | solution.py:247
  61.5 2.4 %collective-permute-start.18 = (bf16[528,128]{1,0:T(8,128)(2,1)}, bf16[528,128]{1,0:T(8,128)(2,1)S(1)}, u32[]{:S(2)}, u32[]{:S(2)}) collective-permute-start(bf16[528,128]{1,0:T(8,128)(2,1)} %soften.3.rest_4_), channel_id=1, source_target_pairs={{0,24},{8,16},{16,8},{24,0},{1,25},{9,17},{17,9},{25,1},{2,26},{10... | collective-permute-start | bytes 405512 | tf_op jit(solution)/shard_map/ppermute | solution.py:366
  64.5 1.2 collective-permute-done.8
  65.6 0.8 convert_add_fusion.1.scores
  66.4 1.7 %soften.2.rest_0_ = bf16[528,128]{1,0:T(8,128)(2,1)} custom-call(f32[512,128]{1,0:T(8,128)} %convert_add_fusion.1.scores, f32[1,32]{1,0:T(1,128)} %copy-done.7), custom_call_target="tpu_custom_call" | custom-call | flops 262144 | bytes 393216 | tf_op jit(solution)/shard_map/soften/pallas_call | solution.py:247
  68.2 1.8 %collective-permute-start.12 = (bf16[528,128]{1,0:T(8,128)(2,1)}, bf16[528,128]{1,0:T(8,128)(2,1)S(1)}, u32[]{:S(2)}, u32[]{:S(2)}) collective-permute-start(bf16[528,128]{1,0:T(8,128)(2,1)} %soften.2.rest_0_), channel_id=1, source_target_pairs={{0,24},{8,16},{16,8},{24,0},{1,25},{9,17},{17,9},{25,1},{2,26},{10... | collective-permute-start | bytes 405512 | tf_op jit(solution)/shard_map/ppermute | solution.py:366
  70.0 1.7 %collective-permute-start.11 = (bf16[528,128]{1,0:T(8,128)(2,1)}, bf16[528,128]{1,0:T(8,128)(2,1)S(1)}, u32[]{:S(2)}, u32[]{:S(2)}) collective-permute-start(bf16[528,128]{1,0:T(8,128)(2,1)} %soften.2.rest_0_), channel_id=1, source_target_pairs={{0,16},{8,24},{16,0},{24,8},{1,17},{9,25},{17,1},{25,9},{2,18},{10... | collective-permute-start | bytes 405512 | tf_op jit(solution)/shard_map/ppermute | solution.py:366
  71.7 0.9 collective-permute-done.17.rest_6_
  72.5 1.9 %collective-permute-done.12.rest_3_ = bf16[528,128]{1,0:T(8,128)(2,1)S(1)} collective-permute-done((bf16[528,128]{1,0:T(8,128)(2,1)}, bf16[528,128]{1,0:T(8,128)(2,1)S(1)}, u32[]{:S(2)}, u32[]{:S(2)}) %collective-permute-start.12) | collective-permute-done | bytes 135200 | tf_op jit(solution)/shard_map/ppermute | solution.py:366
  74.4 1.4 %collective-permute-done.11.rest_2_ = bf16[528,128]{1,0:T(8,128)(2,1)S(1)} collective-permute-done((bf16[528,128]{1,0:T(8,128)(2,1)}, bf16[528,128]{1,0:T(8,128)(2,1)S(1)}, u32[]{:S(2)}, u32[]{:S(2)}) %collective-permute-start.11) | collective-permute-done | bytes 135200 | tf_op jit(solution)/shard_map/ppermute | solution.py:366
  75.8 1.1 collective-permute-done.10.rest_1_
  77.6 29.1 %collect.1 = (f32[32,2048]{1,0:T(8,128)}, f32[1,1024]{1,0:T(1,128)}) custom-call(s32[1]{0:T(128)} %bitcast.me, s32[1,1024]{1,0:T(1,128)} %bitcast.49, s32[2,1024]{1,0:T(2,128)} %bitcast.52, bf16[1024,1024]{1,0:T(8,128)(2,1)} %copy-done, bf16[64,64,128]{2,1,0:T(8,128)(2,1)} %copy-done.2, f32[32,1024]{1,0:T(8,128)} %table.5, bf16[528,128]{1,0:T(8,128)(2,1)} %soften.2.rest_0_, ...), custom_call_target="tpu_custom_call" | custom-call | flops 8589934592 | bytes 4194304 | tf_op jit(solution)/shard_map/collect/pallas_call | solution.py:338
  106.7 1.0 reshape.24
  108.4 3.4 %collective-permute-start.24 = (f32[4,2048]{1,0:T(4,128)S(1)}, f32[4,2048]{1,0:T(4,128)S(1)}, u32[]{:S(2)}, u32[]{:S(2)}) collective-permute-start(f32[4,2048]{1,0:T(4,128)S(1)} %get-tuple-element.33), channel_id=1, source_target_pairs={{0,6},{1,7},{2,4},{3,5},{4,2},{5,3},{6,0},{7,1},{8,14},{9,15},{10,... | collective-permute-start | bytes 98312 | tf_op jit(solution)/shard_map/ppermute | solution.py:366
  111.8 2.3 %collective-permute-start.22 = (f32[4,2048]{1,0:T(4,128)S(1)}, f32[4,2048]{1,0:T(4,128)S(1)}, u32[]{:S(2)}, u32[]{:S(2)}) collective-permute-start(f32[4,2048]{1,0:T(4,128)S(1)} %get-tuple-element.35), channel_id=1, source_target_pairs={{0,4},{1,5},{2,6},{3,7},{4,0},{5,1},{6,2},{7,3},{8,12},{9,13},{10,... | collective-permute-start | bytes 98312 | tf_op jit(solution)/shard_map/ppermute | solution.py:366
  114.1 2.1 %collective-permute-start.20 = (f32[4,2048]{1,0:T(4,128)S(1)}, f32[4,2048]{1,0:T(4,128)S(1)}, u32[]{:S(2)}, u32[]{:S(2)}) collective-permute-start(f32[4,2048]{1,0:T(4,128)S(1)} %get-tuple-element.37), channel_id=1, source_target_pairs={{0,2},{1,3},{2,0},{3,1},{4,6},{5,7},{6,4},{7,5},{8,10},{9,11},{10,... | collective-permute-start | bytes 98312 | tf_op jit(solution)/shard_map/ppermute | solution.py:366
  116.2 0.9 collective-permute-done.23
  (84 shorter events, 11.4 us)
Async XLA Ops:
  0.6 20.1 %collective-permute-start.4 = (bf16[4,1024]{1,0:T(4,128)(2,1)}, bf16[4,1024]{1,0:T(4,128)(2,1)S(1)}, u32[]{:S(2)}, u32[]{:S(2)}) collective-permute-start(bf16[4,1024]{1,0:T(4,128)(2,1)} %param.10), channel_id=1, source_target_pairs={{0,5},{1,4},{2,7},{3,6},{4,1},{5,0},{6,3},{7,2},{8,13},{9,12},{10,... | collective-permute-start | bytes 24584 | tf_op jit(solution)/shard_map/ppermute | solution.py:366
  4.2 16.6 %collective-permute-start.3 = (bf16[4,1024]{1,0:T(4,128)(2,1)}, bf16[4,1024]{1,0:T(4,128)(2,1)S(1)}, u32[]{:S(2)}, u32[]{:S(2)}) collective-permute-start(bf16[4,1024]{1,0:T(4,128)(2,1)} %param.10), channel_id=1, source_target_pairs={{0,4},{1,5},{2,6},{3,7},{4,0},{5,1},{6,2},{7,3},{8,12},{9,13},{10,... | collective-permute-start | bytes 24584 | tf_op jit(solution)/shard_map/ppermute | solution.py:366
  4.8 15.9 %collective-permute-start.2 = (bf16[4,1024]{1,0:T(4,128)(2,1)}, bf16[4,1024]{1,0:T(4,128)(2,1)S(1)}, u32[]{:S(2)}, u32[]{:S(2)}) collective-permute-start(bf16[4,1024]{1,0:T(4,128)(2,1)} %param.10), channel_id=1, source_target_pairs={{0,3},{1,2},{2,1},{3,0},{4,7},{5,6},{6,5},{7,4},{8,11},{9,10},{10,... | collective-permute-start | bytes 24584 | tf_op jit(solution)/shard_map/ppermute | solution.py:366
  6.1 14.4 %collective-permute-start.1 = (bf16[4,1024]{1,0:T(4,128)(2,1)}, bf16[4,1024]{1,0:T(4,128)(2,1)S(1)}, u32[]{:S(2)}, u32[]{:S(2)}) collective-permute-start(bf16[4,1024]{1,0:T(4,128)(2,1)} %param.10), channel_id=1, source_target_pairs={{0,2},{1,3},{2,0},{3,1},{4,6},{5,7},{6,4},{7,5},{8,10},{9,11},{10,... | collective-permute-start | bytes 24584 | tf_op jit(solution)/shard_map/ppermute | solution.py:366
  6.5 10.3 %collective-permute-start = (bf16[4,1024]{1,0:T(4,128)(2,1)}, bf16[4,1024]{1,0:T(4,128)(2,1)S(1)}, u32[]{:S(2)}, u32[]{:S(2)}) collective-permute-start(bf16[4,1024]{1,0:T(4,128)(2,1)} %param.10), channel_id=1, source_target_pairs={{0,1},{1,0},{2,3},{3,2},{4,5},{5,4},{6,7},{7,6},{8,9},{9,8},{10,11... | collective-permute-start | bytes 24584 | tf_op jit(solution)/shard_map/ppermute | solution.py:366
  14.0 12.1 %copy-start.5 = (f32[32,1024]{1,0:T(8,128)S(1)}, f32[32,1024]{1,0:T(8,128)}, u32[]{:S(2)}) copy-start(f32[32,1024]{1,0:T(8,128)} %table.5) | copy-start | bytes 393220
  16.7 24.4 %copy-start.2 = (bf16[64,64,128]{2,1,0:T(8,128)(2,1)}, bf16[64,64,128]{2,1,0:T(8,128)(2,1)S(1)}, u32[]{:S(2)}) copy-start(bf16[64,64,128]{2,1,0:T(8,128)(2,1)S(1)} %pad_maximum_fusion.turns) | copy-start | bytes 3145732
  16.8 9.2 %collective-permute-start.6 = (bf16[4,1024]{1,0:T(4,128)(2,1)S(1)}, bf16[4,1024]{1,0:T(4,128)(2,1)S(1)}, u32[]{:S(2)}, u32[]{:S(2)}) collective-permute-start(bf16[4,1024]{1,0:T(4,128)(2,1)S(1)} %copy-done.8), channel_id=1, source_target_pairs={{0,7},{1,6},{2,5},{3,4},{4,3},{5,2},{6,1},{7,0},{8,15},{9,14},{10,... | collective-permute-start | bytes 24584 | tf_op jit(solution)/shard_map/ppermute | solution.py:366
  20.5 5.5 %collective-permute-start.5 = (bf16[4,1024]{1,0:T(4,128)(2,1)S(1)}, bf16[4,1024]{1,0:T(4,128)(2,1)S(1)}, u32[]{:S(2)}, u32[]{:S(2)}) collective-permute-start(bf16[4,1024]{1,0:T(4,128)(2,1)S(1)} %copy-done.8), channel_id=1, source_target_pairs={{0,6},{1,7},{2,4},{3,5},{4,2},{5,3},{6,0},{7,1},{8,14},{9,15},{10,... | collective-permute-start | bytes 24584 | tf_op jit(solution)/shard_map/ppermute | solution.py:366
  20.7 20.5 %copy-start.3 = (bf16[512,1024]{1,0:T(8,128)(2,1)S(1)}, bf16[512,1024]{1,0:T(8,128)(2,1)}, u32[]{:S(2)}) copy-start(bf16[512,1024]{1,0:T(8,128)(2,1)} %get-tuple-element.29.weighted) | copy-start | bytes 3145732
  41.2 8.9 %copy-start.7 = (f32[1,32]{1,0:T(1,128)}, f32[1,32]{1,0:T(1,128)S(1)}, u32[]{:S(2)}) copy-start(f32[1,32]{1,0:T(1,128)S(1)} %get-tuple-element.18.mean) | copy-start | bytes 388
  46.5 11.9 %collective-permute-start.15 = (f16[512,128]{1,0:T(8,128)(2,1)S(1)}, f16[512,128]{1,0:T(8,128)(2,1)S(1)}, u32[]{:S(2)}, u32[]{:S(2)}) collective-permute-start(f16[512,128]{1,0:T(8,128)(2,1)S(1)} %convert_element_type.47), channel_id=1, source_target_pairs={{0,24},{8,16},{16,8},{24,0},{1,25},{9,17},{17,9},{25,1},{2,26},{10... | collective-permute-start | bytes 393224 | tf_op jit(solution)/shard_map/ppermute | solution.py:366
  49.0 10.0 %collective-permute-start.14 = (f16[512,128]{1,0:T(8,128)(2,1)S(1)}, f16[512,128]{1,0:T(8,128)(2,1)S(1)}, u32[]{:S(2)}, u32[]{:S(2)}) collective-permute-start(f16[512,128]{1,0:T(8,128)(2,1)S(1)} %convert_element_type.45), channel_id=1, source_target_pairs={{0,16},{8,24},{16,0},{24,8},{1,17},{9,25},{17,1},{25,9},{2,18},{10... | collective-permute-start | bytes 393224 | tf_op jit(solution)/shard_map/ppermute | solution.py:366
  49.5 9.5 %collective-permute-start.13 = (f16[512,128]{1,0:T(8,128)(2,1)S(1)}, f16[512,128]{1,0:T(8,128)(2,1)S(1)}, u32[]{:S(2)}, u32[]{:S(2)}) collective-permute-start(f16[512,128]{1,0:T(8,128)(2,1)S(1)} %convert_element_type.43), channel_id=1, source_target_pairs={{0,8},{8,0},{16,24},{24,16},{1,9},{9,1},{17,25},{25,17},{2,10},{10... | collective-permute-start | bytes 393224 | tf_op jit(solution)/shard_map/ppermute | solution.py:366
  55.4 9.0 %collective-permute-start.9 = (f16[512,128]{1,0:T(8,128)(2,1)S(1)}, f16[512,128]{1,0:T(8,128)(2,1)S(1)}, u32[]{:S(2)}, u32[]{:S(2)}) collective-permute-start(f16[512,128]{1,0:T(8,128)(2,1)S(1)} %convert_element_type.41), channel_id=1, source_target_pairs={{0,24},{8,16},{16,8},{24,0},{1,25},{9,17},{17,9},{25,1},{2,26},{10... | collective-permute-start | bytes 393224 | tf_op jit(solution)/shard_map/ppermute | solution.py:366
  57.9 7.7 %collective-permute-start.8 = (f16[512,128]{1,0:T(8,128)(2,1)S(1)}, f16[512,128]{1,0:T(8,128)(2,1)S(1)}, u32[]{:S(2)}, u32[]{:S(2)}) collective-permute-start(f16[512,128]{1,0:T(8,128)(2,1)S(1)} %convert_element_type.39), channel_id=1, source_target_pairs={{0,16},{8,24},{16,0},{24,8},{1,17},{9,25},{17,1},{25,9},{2,18},{10... | collective-permute-start | bytes 393224 | tf_op jit(solution)/shard_map/ppermute | solution.py:366
  58.5 7.2 %collective-permute-start.7 = (f16[512,128]{1,0:T(8,128)(2,1)S(1)}, f16[512,128]{1,0:T(8,128)(2,1)S(1)}, u32[]{:S(2)}, u32[]{:S(2)}) collective-permute-start(f16[512,128]{1,0:T(8,128)(2,1)S(1)} %convert_element_type.37), channel_id=1, source_target_pairs={{0,8},{8,0},{16,24},{24,16},{1,9},{9,1},{17,25},{25,17},{2,10},{10... | collective-permute-start | bytes 393224 | tf_op jit(solution)/shard_map/ppermute | solution.py:366
  61.5 10.1 %collective-permute-start.18 = (bf16[528,128]{1,0:T(8,128)(2,1)}, bf16[528,128]{1,0:T(8,128)(2,1)S(1)}, u32[]{:S(2)}, u32[]{:S(2)}) collective-permute-start(bf16[528,128]{1,0:T(8,128)(2,1)} %soften.3.rest_4_), channel_id=1, source_target_pairs={{0,24},{8,16},{16,8},{24,0},{1,25},{9,17},{17,9},{25,1},{2,26},{10... | collective-permute-start | bytes 405512 | tf_op jit(solution)/shard_map/ppermute | solution.py:366
  64.0 8.6 %collective-permute-start.17 = (bf16[528,128]{1,0:T(8,128)(2,1)}, bf16[528,128]{1,0:T(8,128)(2,1)S(1)}, u32[]{:S(2)}, u32[]{:S(2)}) collective-permute-start(bf16[528,128]{1,0:T(8,128)(2,1)} %soften.3.rest_4_), channel_id=1, source_target_pairs={{0,16},{8,24},{16,0},{24,8},{1,17},{9,25},{17,1},{25,9},{2,18},{10... | collective-permute-start | bytes 405512 | tf_op jit(solution)/shard_map/ppermute | solution.py:366
  66.4 6.1 %collective-permute-start.16 = (bf16[528,128]{1,0:T(8,128)(2,1)}, bf16[528,128]{1,0:T(8,128)(2,1)S(1)}, u32[]{:S(2)}, u32[]{:S(2)}) collective-permute-start(bf16[528,128]{1,0:T(8,128)(2,1)} %soften.3.rest_4_), channel_id=1, source_target_pairs={{0,8},{8,0},{16,24},{24,16},{1,9},{9,1},{17,25},{25,17},{2,10},{10... | collective-permute-start | bytes 405512 | tf_op jit(solution)/shard_map/ppermute | solution.py:366
  68.2 6.2 %collective-permute-start.12 = (bf16[528,128]{1,0:T(8,128)(2,1)}, bf16[528,128]{1,0:T(8,128)(2,1)S(1)}, u32[]{:S(2)}, u32[]{:S(2)}) collective-permute-start(bf16[528,128]{1,0:T(8,128)(2,1)} %soften.2.rest_0_), channel_id=1, source_target_pairs={{0,24},{8,16},{16,8},{24,0},{1,25},{9,17},{17,9},{25,1},{2,26},{10... | collective-permute-start | bytes 405512 | tf_op jit(solution)/shard_map/ppermute | solution.py:366
  70.0 5.8 %collective-permute-start.11 = (bf16[528,128]{1,0:T(8,128)(2,1)}, bf16[528,128]{1,0:T(8,128)(2,1)S(1)}, u32[]{:S(2)}, u32[]{:S(2)}) collective-permute-start(bf16[528,128]{1,0:T(8,128)(2,1)} %soften.2.rest_0_), channel_id=1, source_target_pairs={{0,16},{8,24},{16,0},{24,8},{1,17},{9,25},{17,1},{25,9},{2,18},{10... | collective-permute-start | bytes 405512 | tf_op jit(solution)/shard_map/ppermute | solution.py:366
  71.7 5.2 %copy-start.9 = (bf16[528,128]{1,0:T(8,128)(2,1)}, bf16[528,128]{1,0:T(8,128)(2,1)S(1)}, u32[]{:S(2)}) copy-start(bf16[528,128]{1,0:T(8,128)(2,1)S(1)} %collective-permute-done.18.rest_7_) | copy-start | bytes 405508
  71.7 5.2 %collective-permute-start.10 = (bf16[528,128]{1,0:T(8,128)(2,1)}, bf16[528,128]{1,0:T(8,128)(2,1)S(1)}, u32[]{:S(2)}, u32[]{:S(2)}) collective-permute-start(bf16[528,128]{1,0:T(8,128)(2,1)} %soften.2.rest_0_), channel_id=1, source_target_pairs={{0,8},{8,0},{16,24},{24,16},{1,9},{9,1},{17,25},{25,17},{2,10},{10... | collective-permute-start | bytes 405512 | tf_op jit(solution)/shard_map/ppermute | solution.py:366
  72.5 4.4 %copy-start.10 = (bf16[528,128]{1,0:T(8,128)(2,1)}, bf16[528,128]{1,0:T(8,128)(2,1)S(1)}, u32[]{:S(2)}) copy-start(bf16[528,128]{1,0:T(8,128)(2,1)S(1)} %collective-permute-done.17.rest_6_) | copy-start | bytes 405508
  107.8 6.3 %collective-permute-start.19 = (f32[4,2048]{1,0:T(4,128)S(1)}, f32[4,2048]{1,0:T(4,128)S(1)}, u32[]{:S(2)}, u32[]{:S(2)}) collective-permute-start(f32[4,2048]{1,0:T(4,128)S(1)} %get-tuple-element.31), channel_id=1, source_target_pairs={{0,1},{1,0},{2,3},{3,2},{4,5},{5,4},{6,7},{7,6},{8,9},{9,8},{10,11... | collective-permute-start | bytes 98312 | tf_op jit(solution)/shard_map/ppermute | solution.py:366
  107.9 6.3 %collective-permute-start.25 = (f32[4,2048]{1,0:T(4,128)S(1)}, f32[4,2048]{1,0:T(4,128)S(1)}, u32[]{:S(2)}, u32[]{:S(2)}) collective-permute-start(f32[4,2048]{1,0:T(4,128)S(1)} %get-tuple-element.32), channel_id=1, source_target_pairs={{0,7},{1,6},{2,5},{3,4},{4,3},{5,2},{6,1},{7,0},{8,15},{9,14},{10,... | collective-permute-start | bytes 98312 | tf_op jit(solution)/shard_map/ppermute | solution.py:366
  108.4 7.8 %collective-permute-start.24 = (f32[4,2048]{1,0:T(4,128)S(1)}, f32[4,2048]{1,0:T(4,128)S(1)}, u32[]{:S(2)}, u32[]{:S(2)}) collective-permute-start(f32[4,2048]{1,0:T(4,128)S(1)} %get-tuple-element.33), channel_id=1, source_target_pairs={{0,6},{1,7},{2,4},{3,5},{4,2},{5,3},{6,0},{7,1},{8,14},{9,15},{10,... | collective-permute-start | bytes 98312 | tf_op jit(solution)/shard_map/ppermute | solution.py:366
  111.8 5.3 %collective-permute-start.23 = (f32[4,2048]{1,0:T(4,128)S(1)}, f32[4,2048]{1,0:T(4,128)S(1)}, u32[]{:S(2)}, u32[]{:S(2)}) collective-permute-start(f32[4,2048]{1,0:T(4,128)S(1)} %get-tuple-element.34), channel_id=1, source_target_pairs={{0,5},{1,4},{2,7},{3,6},{4,1},{5,0},{6,3},{7,2},{8,13},{9,12},{10,... | collective-permute-start | bytes 98312 | tf_op jit(solution)/shard_map/ppermute | solution.py:366
  111.8 6.0 %collective-permute-start.22 = (f32[4,2048]{1,0:T(4,128)S(1)}, f32[4,2048]{1,0:T(4,128)S(1)}, u32[]{:S(2)}, u32[]{:S(2)}) collective-permute-start(f32[4,2048]{1,0:T(4,128)S(1)} %get-tuple-element.35), channel_id=1, source_target_pairs={{0,4},{1,5},{2,6},{3,7},{4,0},{5,1},{6,2},{7,3},{8,12},{9,13},{10,... | collective-permute-start | bytes 98312 | tf_op jit(solution)/shard_map/ppermute | solution.py:366
  114.1 4.3 %collective-permute-start.21 = (f32[4,2048]{1,0:T(4,128)S(1)}, f32[4,2048]{1,0:T(4,128)S(1)}, u32[]{:S(2)}, u32[]{:S(2)}) collective-permute-start(f32[4,2048]{1,0:T(4,128)S(1)} %get-tuple-element.36), channel_id=1, source_target_pairs={{0,3},{1,2},{2,1},{3,0},{4,7},{5,6},{6,5},{7,4},{8,11},{9,10},{10,... | collective-permute-start | bytes 98312 | tf_op jit(solution)/shard_map/ppermute | solution.py:366
  114.1 5.0 %collective-permute-start.20 = (f32[4,2048]{1,0:T(4,128)S(1)}, f32[4,2048]{1,0:T(4,128)S(1)}, u32[]{:S(2)}, u32[]{:S(2)}) collective-permute-start(f32[4,2048]{1,0:T(4,128)S(1)} %get-tuple-element.37), channel_id=1, source_target_pairs={{0,2},{1,3},{2,0},{3,1},{4,6},{5,7},{6,4},{7,5},{8,10},{9,11},{10,... | collective-permute-start | bytes 98312 | tf_op jit(solution)/shard_map/ppermute | solution.py:366
  (9 other events, 15.4 us)

commit v2 on v1

v2 whole, which is shorter than its diff:
```python
import functools
import math

import jax
import jax.numpy as jnp
from jax import lax
from jax.experimental import pallas as pl
from jax.experimental.pallas import tpu as pltpu
from jax.sharding import PartitionSpec as P

f32, bf16 = jnp.float32, jnp.bfloat16
VMEM = pl.BlockSpec(memory_space=pltpu.VMEM)
SMEM = pl.BlockSpec(memory_space=pltpu.SMEM)
LANES, ROWS = 128, 8
NN = (((1,), (0,)), ((), ()))
NT = (((1,), (1,)), ((), ()))


def dot(a, b, dims):
    return lax.dot_general(a, b, dims, preferred_element_type=f32)


def split(x, parts):
    out = []
    for _ in range(parts):
        out.append(x.astype(bf16))
        x = x - out[-1].astype(f32)
    return out


def limits(mib, flops, moved, transcendentals=0):
    return dict(
        compiler_params=pltpu.CompilerParams(vmem_limit_bytes=mib << 20),
        cost_estimate=pl.CostEstimate(flops=flops, bytes_accessed=moved, transcendentals=transcendentals),
    )


def block_spec(steps, shape, dim):
    if steps == 1:
        return VMEM
    index = lambda i: tuple(i if d == dim else 0 for d in range(len(shape)))
    return pl.BlockSpec(shape, index)


def same_spec(steps, shape):
    return VMEM if steps == 1 else pl.BlockSpec(shape, lambda i: (0,) * len(shape))


def prepare_kernel(turns, table, matrix, response):
    turn_count, angles, _ = turns.shape
    kinds, pixels = table.shape
    per = LANES // angles
    pack = matrix.shape[1] // LANES
    tiles = pixels // LANES
    row = lax.broadcasted_iota(jnp.int32, (LANES, LANES), 0) // angles
    col = lax.broadcasted_iota(jnp.int32, (LANES, LANES), 1) // angles
    zero = jnp.zeros((), bf16)
    power = table[...] * table[...]
    hi, lo = split(power, 2)
    lhs = jnp.concatenate(
        [
            jnp.concatenate([part[:, t * LANES:(t + 1) * LANES] for part in (hi, lo)], axis=1)
            for t in range(tiles)
        ],
        axis=0,
    )
    for i in range(turn_count // pack):
        wide = []
        for j in range(pack):
            turn = turns[i * pack + j]
            turn = jnp.concatenate([jnp.concatenate([turn] * per, axis=1)] * per, axis=0)
            wide.append(jnp.where(row == col, turn, zero))
        wide = jnp.concatenate(wide, axis=1)
        matrix[i * LANES:(i + 1) * LANES, :] = wide
        value = dot(lhs, jnp.concatenate([wide, wide], axis=0), NN).astype(bf16)
        for j in range(pack):
            for t in range(tiles):
                response[i * kinds:(i + 1) * kinds, j * pixels + t * LANES:j * pixels + (t + 1) * LANES] = value[
                    t * kinds:(t + 1) * kinds, j * LANES:(j + 1) * LANES
                ]


def prepare(turns, table, pack):
    turn_count, angles, _ = turns.shape
    kinds, pixels = table.shape
    steps = turn_count // pack
    return pl.pallas_call(
        prepare_kernel,
        in_specs=[VMEM, VMEM],
        out_specs=[VMEM, VMEM],
        out_shape=[
            jax.ShapeDtypeStruct((steps * LANES, pack * LANES), bf16),
            jax.ShapeDtypeStruct((steps * kinds, pack * pixels), bf16),
        ],
        name="prepare",
        **limits(24, 4 * steps * kinds * pack * pixels * LANES, 2 * steps * kinds * pack * pixels),
    )(turns, table)


def weigh_kernel(pixels, kind, table, out):
    kinds, width = table.shape
    table3 = jnp.concatenate(split(table[...], 3), axis=0)
    ids = lax.broadcasted_iota(jnp.int32, (LANES, kind.shape[1]), 0)
    hit = jnp.where((ids % kinds == kind[...]) & (ids < 3 * kinds), 1.0, 0.0)
    hit = hit.T.astype(bf16)
    rows = dot(hit[:, :3 * kinds], table3, NN)
    out[:, :width] = (pixels[...].astype(f32) * rows).astype(bf16)
    out[:, width:] = hit


def weigh(particles, kind, table):
    count, pixels = particles.shape
    rows = math.gcd(count, 256)
    return pl.pallas_call(
        weigh_kernel,
        grid=(count // rows,),
        in_specs=[
            pl.BlockSpec((rows, pixels), lambda i: (i, 0)),
            pl.BlockSpec((1, rows), lambda i: (0, i)),
            pl.BlockSpec(table.shape, lambda i: (0, 0)),
        ],
        out_specs=pl.BlockSpec((rows, pixels + LANES), lambda i: (i, 0)),
        out_shape=jax.ShapeDtypeStruct((count, pixels + LANES), bf16),
        name="weigh",
        **limits(16, 2 * count * pixels * 96, 4 * count * pixels),
    )(particles, kind, table)


def rotate_kernel(groups, turn_count, refs, matrix, table, rotated, mean, center, energy):
    kinds, pixels = table.shape
    pack = matrix.shape[1] // LANES
    cpg = ROWS // pack
    tiles = pixels // LANES
    group_pairs = cpg * turn_count
    source = refs[...].astype(f32)
    inside = lax.broadcasted_iota(jnp.int32, (groups * ROWS, LANES), 0) % ROWS // cpg
    lhs = jnp.concatenate(
        [
            jnp.concatenate(
                [jnp.where(inside == j, source[:, t * LANES:(t + 1) * LANES], 0.0) for j in range(pack)], axis=1
            )
            for t in range(tiles)
        ],
        axis=0,
    ).astype(bf16)
    for s in range(turn_count // (2 * pack)):
        value = dot(lhs, matrix[s * 2 * LANES:(s + 1) * 2 * LANES, :], NT)
        for t in range(tiles):
            for g in range(groups):
                at = (t * groups + g) * ROWS
                pair = [value[at:at + ROWS, h * LANES:(h + 1) * LANES] for h in range(2)]
                to = g * group_pairs + s * 2 * ROWS
                rotated[to:to + 2 * ROWS, t * LANES:(t + 1) * LANES] = jnp.concatenate(pair, axis=0).astype(bf16)
    power = table[...] * table[...]
    power2 = jnp.concatenate(split(power, 2), axis=0)
    pairs = groups * group_pairs
    rows = math.gcd(pairs, 256)
    summed = jnp.zeros((kinds, 1), f32)
    for i in range(pairs // rows):
        at = slice(i * rows, (i + 1) * rows)
        value = rotated[at, :pixels].astype(f32)
        hi, lo = split(value * value, 2)
        total = dot(power2, hi, NT) + dot(power2, lo, NT)
        total = -0.5 * (total[:kinds] + total[kinds:])
        energy[:, at] = total
        summed = summed + jnp.sum(total, axis=1, keepdims=True)

    @pl.when(pl.program_id(0) == 0)
    def _():
        center[...] = summed * (1.0 / pairs)

    spread = lax.broadcasted_iota(jnp.int32, (kinds, LANES), 0) == lax.broadcasted_iota(jnp.int32, (kinds, LANES), 1)
    mean[...] = jnp.sum(jnp.where(spread, center[...], 0.0), axis=0, keepdims=True)
    blank = jnp.zeros((LANES - 3 * kinds, LANES), f32)
    for i in range(pairs // LANES):
        at = slice(i * LANES, (i + 1) * LANES)
        parts = [part.astype(f32) for part in split(energy[:, at] - center[...], 3)]
        rotated[at, pixels:] = jnp.concatenate(parts + [blank], axis=0).T.astype(bf16)


def rotate(refs, matrix, table, turn_count, groups):
    kinds, pixels = table.shape
    groups_all = refs.shape[0] // ROWS
    steps = groups_all // groups
    cpg = ROWS * LANES // matrix.shape[1]
    pairs = groups * cpg * turn_count
    return pl.pallas_call(
        functools.partial(rotate_kernel, groups, turn_count),
        grid=(steps,),
        in_specs=[
            block_spec(steps, (groups * ROWS, pixels), 0),
            same_spec(steps, matrix.shape),
            same_spec(steps, table.shape),
        ],
        out_specs=[block_spec(steps, (pairs, pixels + LANES), 0), same_spec(steps, (1, LANES))],
        out_shape=[
            jax.ShapeDtypeStruct((steps * pairs, pixels + LANES), bf16),
            jax.ShapeDtypeStruct((1, LANES), f32),
        ],
        scratch_shapes=[pltpu.VMEM((kinds, 1), f32), pltpu.VMEM((kinds, pairs), f32)],
        name="rotate",
        **limits(24, 8 * steps * pairs * pixels * 64, 2 * steps * pairs * pixels),
    )(refs, matrix, table)


def score_kernel(groups, scale, me, weighted, names, rotated, *rest):
    outs, acc = rest[:-1], rest[-1]
    step = pl.program_id(0)
    count = weighted.shape[0]
    pairs = rotated.shape[0] // groups
    span = math.gcd(count, 256)
    for n in range(count // span):
        cols = slice(n * span, (n + 1) * span)
        pix = weighted[cols, :]
        for g in range(groups):
            value = scale * dot(rotated[g * pairs:(g + 1) * pairs, :], pix, NT)
            group = step * groups + g
            for k in range(2):
                rows = slice(k * pairs, (k + 1) * pairs)
                hit = names[k:k + 1, cols] == group
                if g == 0:
                    hit = hit | (step == 0)
                acc[rows, cols] = jnp.where(hit, value, acc[rows, cols])

    @pl.when(step == pl.num_programs(0) - 1)
    def _():
        share = outs[0].shape[1]
        for k, out in enumerate(outs):
            start = pl.multiple_of((me[0] ^ k) * share, share)
            out[...] = acc[:, pl.ds(start, share)]


def score(weighted, names, rotated, me, peers, group_pairs, groups, scale):
    count, width = weighted.shape
    steps = rotated.shape[0] // (group_pairs * groups)
    share = count // peers
    rows = 2 * group_pairs
    return pl.pallas_call(
        functools.partial(score_kernel, groups, scale),
        grid=(steps,),
        in_specs=[
            SMEM,
            same_spec(steps, weighted.shape),
            same_spec(steps, names.shape),
            block_spec(steps, (groups * group_pairs, width), 0),
        ],
        out_specs=[same_spec(steps, (rows, share))] * peers,
        out_shape=[jax.ShapeDtypeStruct((rows, share), f32)] * peers,
        scratch_shapes=[pltpu.VMEM((rows, count), f32)],
        name="score",
        **limits(24, 2 * rotated.shape[0] * width * count, 2 * rotated.shape[0] * width),
    )(me, weighted, names, rotated)


def soften_kernel(scores, mean, out):
    value = scores[...]
    rows, share = value.shape
    top = jnp.max(value, axis=0, keepdims=True)
    grown = jnp.exp(value - top)
    total = jnp.sum(grown, axis=0, keepdims=True)
    out[:rows, :] = (grown * (1.0 / total)).astype(bf16)
    tail = jnp.zeros((2 * ROWS, share), f32)
    at = lax.broadcasted_iota(jnp.int32, tail.shape, 0)
    centers = mean[...]
    if share > LANES:
        centers = jnp.concatenate([centers, jnp.zeros((1, share - LANES), f32)], axis=1)
    for i, row in enumerate(split(top + jnp.log(total), 3) + split(centers, 3)):
        tail = jnp.where(at == i, row.astype(f32), tail)
    out[rows:, :] = tail.astype(bf16)


def soften(scores, mean):
    rows, share = scores.shape
    return pl.pallas_call(
        soften_kernel,
        in_specs=[VMEM, VMEM],
        out_specs=VMEM,
        out_shape=jax.ShapeDtypeStruct((rows + 2 * ROWS, share), bf16),
        name="soften",
        **limits(8, 4 * rows * share, 6 * rows * share, rows * share),
    )(scores, mean)


def collect_kernel(groups, turn_count, kinds, scale, peers, chunks, me, names, weighted, matrix, response, *rest):
    blocks = rest[:peers * chunks]
    sums, logs, weights, lhs, by_kind = rest[peers * chunks:]
    step = pl.program_id(0)
    count, pixels = weighted.shape[0], weighted.shape[1] - LANES
    share = blocks[0].shape[1]
    rows = weights.shape[0]
    pairs = rows // 2
    pack = matrix.shape[1] // LANES
    cpg = ROWS // pack
    tiles = pixels // LANES
    turns = turn_count // pack

    @pl.when(step == 0)
    def _():
        center = jnp.zeros((1, share), f32)
        for k in range(peers):
            for c in range(chunks):
                block = blocks[c * peers + k]
                start = pl.multiple_of((c * peers + (me[0] ^ k)) * share, share)
                weights[:, pl.ds(start, share)] = block[:rows, :]
                tail = block[rows:, :].astype(f32)
                logs[0:1, pl.ds(start, share)] = tail[0:1] + tail[1:2] + tail[2:3]
                if c == 0:
                    center = center + (tail[3:4] + tail[4:5] + tail[5:6])
        center3 = split(center[:, :LANES], 3)
        line = lax.broadcasted_iota(jnp.int32, (2 * ROWS, LANES), 0)
        first = lax.broadcasted_iota(jnp.int32, (2 * ROWS, LANES), 1) < kinds
        stack = jnp.zeros((2 * ROWS, LANES), f32)
        for i, part in enumerate(center3):
            stack = jnp.where((line == i) & first, part.astype(f32), stack)
        moved = dot(stack.astype(bf16), weighted[:, pixels:], NT)
        logs[...] = logs[...] + scale * jnp.sum(moved, axis=0, keepdims=True)

    zero = jnp.zeros((), bf16)
    for g in range(0, groups, 2):
        dense = []
        for q in range(2):
            group = step * groups + g + q
            dense.append(
                jnp.where(names[0:1, :] == group, weights[:pairs, :], zero)
                + jnp.where(names[1:2, :] == group, weights[pairs:, :], zero)
            )
        value = dot(jnp.concatenate(dense, axis=0), weighted[...], NN)
        for i in range(turns):
            for t in range(tiles):
                pair = [
                    value[q * pairs + i * ROWS:q * pairs + (i + 1) * ROWS, t * LANES:(t + 1) * LANES]
                    for q in range(2)
                ]
                at = (t * groups + g) * ROWS
                lhs[at:at + 2 * ROWS, i * LANES:(i + 1) * LANES] = jnp.concatenate(pair, axis=0).astype(bf16)
            for q in range(2):
                by_kind[(g + q) * ROWS:(g + q + 1) * ROWS, i * kinds:(i + 1) * kinds] = value[
                    q * pairs + i * ROWS:q * pairs + (i + 1) * ROWS, pixels:pixels + kinds
                ]
    total = dot(lhs[...], matrix[...], NN)
    heavy = dot(jnp.concatenate(split(by_kind[...], 2), axis=0), response[...], NN)
    heavy = heavy[:groups * ROWS] + heavy[groups * ROWS:]
    upper = lax.broadcasted_iota(jnp.int32, (ROWS, LANES), 0) < cpg

    def fold(parts):
        out = parts[0]
        for j in range(1, pack):
            out = out + pltpu.roll(parts[j], ROWS - j * cpg, 0)
        return out

    for g in range(groups):
        for t in range(tiles):
            at = slice((t * groups + g) * ROWS, (t * groups + g + 1) * ROWS)
            top = fold([total[at, j * LANES:(j + 1) * LANES] for j in range(pack)])
            at = slice(g * ROWS, (g + 1) * ROWS)
            low = fold(
                [heavy[at, j * pixels + t * LANES:j * pixels + (t + 1) * LANES] for j in range(pack)]
            )
            sums[at, t * LANES:(t + 1) * LANES] = jnp.where(upper, top, pltpu.roll(low, cpg, 0))


def collect(blocks, chunks, names, weighted, matrix, response, me, turn_count, kinds, group_pairs, groups, groups_all, scale):
    count, width = weighted.shape
    pixels = width - LANES
    peers = len(blocks) // chunks
    steps = groups_all // groups
    turns = matrix.shape[0] // LANES
    return pl.pallas_call(
        functools.partial(collect_kernel, groups, turn_count, kinds, scale, peers, chunks),
        grid=(steps,),
        in_specs=[SMEM]
        + [same_spec(steps, a.shape) for a in (names, weighted, matrix, response)]
        + [same_spec(steps, b.shape) for b in blocks],
        out_specs=[block_spec(steps, (groups * ROWS, pixels), 0), same_spec(steps, (1, count))],
        out_shape=[
            jax.ShapeDtypeStruct((groups_all * ROWS, pixels), f32),
            jax.ShapeDtypeStruct((1, count), f32),
        ],
        scratch_shapes=[
            pltpu.VMEM((2 * group_pairs, count), bf16),
            pltpu.VMEM((pixels // LANES * groups * ROWS, turns * LANES), bf16),
            pltpu.VMEM((groups * ROWS, turns * kinds), f32),
        ],
        name="collect",
        **limits(32, 2 * groups_all * group_pairs * width * count, 4 * count * pixels),
    )(me, names, weighted, matrix, response, *blocks)


def swap(x, axis, k):
    return lax.ppermute(x, axis, [(i, i ^ k) for i in range(lax.axis_size(axis))])


def paired(size):
    return size & (size - 1) == 0 and 2 <= size <= 8


def place(group, size):
    if not paired(size):
        return group
    apart = group ^ lax.axis_index("dom").astype(group.dtype)
    return (apart & 1) * (size // 2) + (apart >> 1)


def gather_dom(x, size):
    if not paired(size):
        return lax.all_gather(x, "dom", axis=0, tiled=True)
    half = jnp.concatenate([x] + [swap(x, "dom", 2 * k) for k in range(1, size // 2)], axis=0)
    return jnp.concatenate([half, swap(half, "dom", 1)], axis=0)


def scatter_dom(x, size):
    if not paired(size):
        return lax.psum_scatter(x, "dom", scatter_dimension=0, tiled=True)
    half = x.shape[0] // 2
    rows = x.shape[0] // size
    x = x[:half] + swap(x[half:], "dom", 1)
    total = x[:rows]
    for k in range(1, size // 2):
        total = total + swap(x[k * rows:(k + 1) * rows], "dom", 2 * k)
    return total


def local(particles, candidates, defocus, ctf_table, references, rotations):
    count, pixels = particles.shape
    peers = lax.axis_size("cls")
    owners = lax.axis_size("dom")
    turn_count = rotations.shape[0]
    cpg = references.shape[0]
    pack = ROWS // cpg
    group_pairs = cpg * turn_count
    groups = math.gcd(owners, 8)
    kinds = ctf_table.shape[0]
    scale = 4.0 / math.sqrt(pixels * peers)
    me = lax.axis_index("cls").astype(jnp.int32).reshape(1)
    kind = defocus.reshape(1, count)
    names = place(candidates.T, owners)
    refs = gather_dom(jnp.concatenate([references] * pack, axis=0), owners)
    matrix, response = prepare(rotations, ctf_table, pack)
    weighted = weigh(particles, kind, ctf_table)
    rotated, mean = rotate(refs, matrix, ctf_table, turn_count, groups)
    chunks = 2
    size = count // chunks
    blocks = []
    for c in range(chunks):
        at = slice(c * size, (c + 1) * size)
        cut = score(weighted[at], names[:, at], rotated, me, peers, group_pairs, groups, scale)
        total = cut[0]
        for k in range(1, peers):
            total = total + swap(cut[k].astype(jnp.float16), "cls", k).astype(f32)
        own = soften(total, mean)
        blocks.extend([own] + [swap(own, "cls", k) for k in range(1, peers)])
    sums, logs = collect(
        blocks, chunks, names, weighted, matrix, response, me, turn_count, kinds, group_pairs, groups, owners, scale
    )
    total = scatter_dom(sums, owners)
    return total[:cpg].astype(bf16), total[cpg:], logs.reshape(count)


def solution(mesh):
    in_specs = (P("dom", "cls"), P("dom", None), P("dom"), P(None, "cls"), P("dom", "cls"), P())
    out_specs = (P("dom", "cls"), P("dom", "cls"), P("dom"))
    return jax.shard_map(local, mesh=mesh, in_specs=in_specs, out_specs=out_specs, check_vma=False)
```

time: 121 us -> 93.5 us (0.77)
  Pallas kernels: 59.6 us -> 22.4 us
  local copies, waits for them, and re-layouts: 9.46 us -> 26.7 us
  starting transfers between devices: 31.9 us -> 25.5 us
  other arithmetic: 4 us -> 1.67 us
    pallas_call x4 -> x5, Pallas kernels: 54.8 us -> 20.7 us  [the longest x1 8.31 us: collect(): pl.pallas_call(functools.partial(collect_kernel, groups, turn_count, kind...]
    concatenate x0 -> x2, local copies, waits for them, and re-layouts: none -> 12.1 us  [the longest x1 6.8 us: gather_dom(): return jnp.concatenate([half, swap(half, 'dom', 1)], axis=0)]
    unnamed x30 -> x28, local copies, waits for them, and re-layouts: 4.25 us -> 12.2 us
    ppermute x26 -> x20, starting transfers between devices: 31.9 us -> 25.5 us  [swap(): lax.ppermute(x, axis, [(i, i ^ k) for i in range(lax.axis_size(axis))])]
    pallas_call x2, Pallas kernels: 3.49 us -> 0.27 us  [soften(): pl.pallas_call(soften_kernel, in_specs=[VMEM, VMEM], out_specs=VMEM, out_...]
    add x2, other arithmetic: 1.56 us -> 0.11 us  [local(): total = total + swap(cut[k].astype(jnp.float16), 'cls', k).astype(f32)]
    ppermute x26 -> x20, waiting for transfers between devices: 14.6 us -> 15.1 us  [swap(): lax.ppermute(x, axis, [(i, i ^ k) for i in range(lax.axis_size(axis))])]
  transfers between devices with their start and end apart: 26 -> 20, of which waited for: 10 -> 7; matrix products, arithmetic and copies ran while one was open for 6% -> 2% of each run, Pallas kernels for 8% -> 7%
where the time goes in v2:
time: 93.5 us; the launch traced here: 92.3 us
  local copies, waits for them, and re-layouts  26.7 us (29%)
  starting transfers between devices  25.5 us (27%)
  Pallas kernels  22.4 us (24%)
  waiting for transfers between devices  15.1 us (16%)
  other arithmetic  1.67 us (2%)
    ppermute x20, starting transfers between devices, swap(): lax.ppermute(x, axis, [(i, i ^ k) for i in range(lax.axis_size(axis))])  25.5 us
    ppermute x20, waiting for transfers between devices, swap(): lax.ppermute(x, axis, [(i, i ^ k) for i in range(lax.axis_size(axis))])  15.1 us
    unnamed x28, local copies, waits for them, and re-layouts  12.2 us
    pallas_call x1, Pallas kernels, collect(): pl.pallas_call(functools.partial(collect_kernel, groups, turn_count, kind...  8.31 us
    concatenate x1, local copies, waits for them, and re-layouts, gather_dom(): return jnp.concatenate([half, swap(half, 'dom', 1)], axis=0)  6.8 us
    pallas_call x2, Pallas kernels, score(): pl.pallas_call(functools.partial(score_kernel, groups, scale), grid=(step...  6.34 us
    concatenate x1, local copies, waits for them, and re-layouts, gather_dom(): jnp.concatenate([x] + [swap(x, 'dom', 2 * k) for k in range(1, size // 2)...  5.34 us
    pallas_call x1, Pallas kernels, rotate(): pl.pallas_call(functools.partial(rotate_kernel, groups, turn_count), grid...  4.48 us
  transfers between devices with their start and end apart: 20, of which 7 were waited for; matrix products, arithmetic and copies ran while one was open for 2% of the time, Pallas kernels for 7%

profile of v2, /device:TPU:0, one launch (start us, length us, event | category | flops | bytes accessed | tf_op | source)
XLA Modules:
  0.0 92.3 jit_solution(10165125854198055701)
XLA Ops:
  0.6 1.4 %pad_maximum_fusion = bf16[8,1024]{1,0:T(8,128)(2,1)} fusion(bf16[4,1024]{1,0:T(4,128)(2,1)} %param.10), kind=kLoop, calls=%fused_computation.7 | loop fusion | flops 32768 | bytes 24576 | tf_op jit(solution)/shard_map/concatenate | solution.py:437
  2.0 5.0 %collective-permute-start.2 = (bf16[8,1024]{1,0:T(8,128)(2,1)}, bf16[8,1024]{1,0:T(8,128)(2,1)}, u32[]{:S(2)}, u32[]{:S(2)}) collective-permute-start(bf16[8,1024]{1,0:T(8,128)(2,1)} %pad_maximum_fusion), channel_id=1, source_target_pairs={{0,6},{1,7},{2,4},{3,5},{4,2},{5,3},{6,0},{7,1},{8,14},{9,15},{10,... | collective-permute-start | bytes 49160 | tf_op jit(solution)/shard_map/ppermute | solution.py:390
  7.6 1.6 %copy-done = bf16[1024,1024]{1,0:T(8,128)(2,1)S(1)} copy-done((bf16[1024,1024]{1,0:T(8,128)(2,1)S(1)}, bf16[1024,1024]{1,0:T(8,128)(2,1)}, u32[]{:S(2)}) %copy-start) | copy-done | bytes 2097176
  10.8 1.4 %weigh.1.weighted = bf16[1024,1152]{1,0:T(8,128)(2,1)S(1)} custom-call(bf16[1024,1024]{1,0:T(8,128)(2,1)S(1)} %copy-done, s32[1,1024]{1,0:T(1,128)S(1)} %bitcast.5, f32[32,1024]{1,0:T(8,128)S(1)} %copy-done.3), custom_call_target="tpu_custom_call" | custom-call | flops 201326592 | bytes 4194304 | tf_op jit(solution)/shard_map/weigh/pallas_call | solution.py:114
  12.2 1.2 %fusion.2 = (bf16[512,1152]{1,0:T(8,128)(2,1)}, bf16[512,1152]{1,0:T(8,128)(2,1)S(1)}) fusion(bf16[1024,1152]{1,0:T(8,128)(2,1)S(1)} %weigh.1.weighted), kind=kLoop, calls=%fused_computation.9 | loop fusion | bytes 4718592 | tf_op jit(solution)/shard_map/slice | solution.py:446
  13.5 5.3 %concatenate.12 = bf16[32,1024]{1,0:T(8,128)(2,1)} concatenate(bf16[4,1024]{1,0:T(4,128)(2,1)} %param.10, bf16[4,1024]{1,0:T(4,128)(2,1)} %param.10, bf16[8,1024]{1,0:T(8,128)(2,1)} %collective-permute-done, bf16[8,1024]{1,0:T(8,128)(2,1)} %collective-permute-done.1, bf16[8,1024]{1,0:T(8,128)(2,1)} %collective-permute-done.2), dimensions={0} | concatenate | bytes 131072 | tf_op jit(solution)/shard_map/concatenate | solution.py:407
  18.8 0.9 copy-done.4
  19.8 1.2 %copy-done.7 = bf16[64,64,64]{2,1,0:T(8,128)(2,1)S(1)} copy-done((bf16[64,64,64]{2,1,0:T(8,128)(2,1)S(1)}, bf16[64,64,64]{2,1,0:T(8,128)(2,1)}, u32[]{:S(2)}) %copy-start.7) | copy-done | bytes 524312
  21.0 1.6 %prepare.1 = (bf16[4096,256]{1,0:T(8,128)(2,1)S(1)}, bf16[1024,2048]{1,0:T(8,128)(2,1)S(1)}) custom-call(bf16[64,64,64]{2,1,0:T(8,128)(2,1)S(1)} %copy-done.7, f32[32,1024]{1,0:T(8,128)S(1)} %copy-done.4), custom_call_target="tpu_custom_call" | custom-call | flops 1073741824 | bytes 4194304 | tf_op jit(solution)/shard_map/prepare/pallas_call | solution.py:87
  22.6 1.4 %copy-done.8 = bf16[4096,256]{1,0:T(8,128)(2,1)} copy-done((bf16[4096,256]{1,0:T(8,128)(2,1)}, bf16[4096,256]{1,0:T(8,128)(2,1)S(1)}, u32[]{:S(2)}) %copy-start.8) | copy-done | bytes 2097176
  24.0 2.0 %copy-done.11 = bf16[1024,2048]{1,0:T(8,128)(2,1)} copy-done((bf16[1024,2048]{1,0:T(8,128)(2,1)}, bf16[1024,2048]{1,0:T(8,128)(2,1)S(1)}, u32[]{:S(2)}) %copy-start.11) | copy-done | bytes 4194328
  25.9 6.8 %concatenate.13.refs = bf16[64,1024]{1,0:T(8,128)(2,1)} concatenate(bf16[4,1024]{1,0:T(4,128)(2,1)} %param.10, bf16[4,1024]{1,0:T(4,128)(2,1)} %param.10, bf16[8,1024]{1,0:T(8,128)(2,1)} %collective-permute-done, bf16[8,1024]{1,0:T(8,128)(2,1)} %collective-permute-done.1, bf16[8,1024]{1,0:T(8,128)(2,1)} %collective-permute-done.2, bf16[32,1024]{1,0:T(8,128)(2,1)} %collective-permute-done.3), dimensions={0} | concatenate | bytes 262144 | tf_op jit(solution)/shard_map/concatenate | solution.py:408
  32.7 1.0 %copy-done.2 = bf16[64,1024]{1,0:T(8,128)(2,1)S(1)} copy-done((bf16[64,1024]{1,0:T(8,128)(2,1)S(1)}, bf16[64,1024]{1,0:T(8,128)(2,1)}, u32[]{:S(2)}) %copy-start.2) | copy-done | bytes 131096
  34.7 1.6 %copy-done.9 = bf16[4096,256]{1,0:T(8,128)(2,1)S(1)} copy-done((bf16[4096,256]{1,0:T(8,128)(2,1)S(1)}, bf16[4096,256]{1,0:T(8,128)(2,1)}, u32[]{:S(2)}) %copy-start.9) | copy-done | bytes 2097176
  36.2 4.5 %rotate.1 = (bf16[2048,1152]{1,0:T(8,128)(2,1)S(1)}, f32[1,128]{1,0:T(1,128)S(1)}) custom-call(bf16[64,1024]{1,0:T(8,128)(2,1)S(1)} %copy-done.2, bf16[4096,256]{1,0:T(8,128)(2,1)S(1)} %copy-done.9, f32[32,1024]{1,0:T(8,128)S(1)} %copy-done.5), custom_call_target="tpu_custom_call" | custom-call | flops 1073741824 | bytes 4194304 | tf_op jit(solution)/shard_map/rotate/pallas_call | solution.py:187
  40.7 3.1 %score.3 = (f32[512,128]{1,0:T(8,128)S(1)}, f32[512,128]{1,0:T(8,128)S(1)}, f32[512,128]{1,0:T(8,128)S(1)}, f32[512,128]{1,0:T(8,128)S(1)}) custom-call(s32[1]{0:T(128)} %bitcast.me, bf16[512,1152]{1,0:T(8,128)(2,1)S(1)} %copy-done.1, s32[2,512]{1,0:T(2,128)S(1)} %get-tuple-element.36.names, bf16[2048,1152]{1,0:T(8,128)(2,1)S(1)} %get-tuple-element.19.rotated), custom_call_target="tpu_custom_call" | custom-call | flops 2415919104 | bytes 4718592 | tf_op jit(solution)/shard_map/score/pallas_call | solution.py:238
  44.0 2.7 %collective-permute-start.12 = (f16[512,128]{1,0:T(8,128)(2,1)S(1)}, f16[512,128]{1,0:T(8,128)(2,1)S(1)}, u32[]{:S(2)}, u32[]{:S(2)}) collective-permute-start(f16[512,128]{1,0:T(8,128)(2,1)S(1)} %convert_element_type.47), channel_id=1, source_target_pairs={{0,24},{8,16},{16,8},{24,0},{1,25},{9,17},{17,9},{25,1},{2,26},{10... | collective-permute-start | bytes 393224 | tf_op jit(solution)/shard_map/ppermute | solution.py:390
  47.5 3.2 %score.2 = (f32[512,128]{1,0:T(8,128)S(1)}, f32[512,128]{1,0:T(8,128)S(1)}, f32[512,128]{1,0:T(8,128)S(1)}, f32[512,128]{1,0:T(8,128)S(1)}) custom-call(s32[1]{0:T(128)} %bitcast.me, bf16[512,1152]{1,0:T(8,128)(2,1)S(1)} %get-tuple-element.32.weighted, s32[2,512]{1,0:T(2,128)S(1)} %get-tuple-element.37.names, bf16[2048,1152]{1,0:T(8,128)(2,1)S(1)} %get-tuple-element.19.rotated), custom_call_target="tpu_custom_call" | custom-call | flops 2415919104 | bytes 4718592 | tf_op jit(solution)/shard_map/score/pallas_call | solution.py:238
  50.8 2.7 %collective-permute-start.6 = (f16[512,128]{1,0:T(8,128)(2,1)S(1)}, f16[512,128]{1,0:T(8,128)(2,1)S(1)}, u32[]{:S(2)}, u32[]{:S(2)}) collective-permute-start(f16[512,128]{1,0:T(8,128)(2,1)S(1)} %convert_element_type.41), channel_id=1, source_target_pairs={{0,24},{8,16},{16,8},{24,0},{1,25},{9,17},{17,9},{25,1},{2,26},{10... | collective-permute-start | bytes 393224 | tf_op jit(solution)/shard_map/ppermute | solution.py:390
  54.6 2.7 %collective-permute-start.15 = (bf16[528,128]{1,0:T(8,128)(2,1)S(1)}, bf16[528,128]{1,0:T(8,128)(2,1)S(1)}, u32[]{:S(2)}, u32[]{:S(2)}) collective-permute-start(bf16[528,128]{1,0:T(8,128)(2,1)S(1)} %soften.3.rest_4_), channel_id=1, source_target_pairs={{0,24},{8,16},{16,8},{24,0},{1,25},{9,17},{17,9},{25,1},{2,26},{10... | collective-permute-start | bytes 405512 | tf_op jit(solution)/shard_map/ppermute | solution.py:390
  57.8 5.0 %collective-permute-done.5 = f16[512,128]{1,0:T(8,128)(2,1)S(1)} collective-permute-done((f16[512,128]{1,0:T(8,128)(2,1)S(1)}, f16[512,128]{1,0:T(8,128)(2,1)S(1)}, u32[]{:S(2)}, u32[]{:S(2)}) %collective-permute-start.5) | collective-permute-done | bytes 131104 | tf_op jit(solution)/shard_map/ppermute | solution.py:390
  62.9 1.7 %collective-permute-start.13 = (bf16[528,128]{1,0:T(8,128)(2,1)S(1)}, bf16[528,128]{1,0:T(8,128)(2,1)S(1)}, u32[]{:S(2)}, u32[]{:S(2)}) collective-permute-start(bf16[528,128]{1,0:T(8,128)(2,1)S(1)} %soften.3.rest_4_), channel_id=1, source_target_pairs={{0,8},{8,0},{16,24},{24,16},{1,9},{9,1},{17,25},{25,17},{2,10},{10... | collective-permute-start | bytes 405512 | tf_op jit(solution)/shard_map/ppermute | solution.py:390
  64.7 1.5 %collective-permute-start.9 = (bf16[528,128]{1,0:T(8,128)(2,1)S(1)}, bf16[528,128]{1,0:T(8,128)(2,1)S(1)}, u32[]{:S(2)}, u32[]{:S(2)}) collective-permute-start(bf16[528,128]{1,0:T(8,128)(2,1)S(1)} %soften.2.rest_0_), channel_id=1, source_target_pairs={{0,24},{8,16},{16,8},{24,0},{1,25},{9,17},{17,9},{25,1},{2,26},{10... | collective-permute-start | bytes 405512 | tf_op jit(solution)/shard_map/ppermute | solution.py:390
  66.7 1.6 %collective-permute-start.7 = (bf16[528,128]{1,0:T(8,128)(2,1)S(1)}, bf16[528,128]{1,0:T(8,128)(2,1)S(1)}, u32[]{:S(2)}, u32[]{:S(2)}) collective-permute-start(bf16[528,128]{1,0:T(8,128)(2,1)S(1)} %soften.2.rest_0_), channel_id=1, source_target_pairs={{0,8},{8,0},{16,24},{24,16},{1,9},{9,1},{17,25},{25,17},{2,10},{10... | collective-permute-start | bytes 405512 | tf_op jit(solution)/shard_map/ppermute | solution.py:390
  68.3 1.2 %collective-permute-done.13.rest_5_ = bf16[528,128]{1,0:T(8,128)(2,1)S(1)} collective-permute-done((bf16[528,128]{1,0:T(8,128)(2,1)S(1)}, bf16[528,128]{1,0:T(8,128)(2,1)S(1)}, u32[]{:S(2)}, u32[]{:S(2)}) %collective-permute-start.13) | collective-permute-done | bytes 135200 | tf_op jit(solution)/shard_map/ppermute | solution.py:390
  69.5 2.5 %collective-permute-done.9.rest_3_ = bf16[528,128]{1,0:T(8,128)(2,1)S(1)} collective-permute-done((bf16[528,128]{1,0:T(8,128)(2,1)S(1)}, bf16[528,128]{1,0:T(8,128)(2,1)S(1)}, u32[]{:S(2)}, u32[]{:S(2)}) %collective-permute-start.9) | collective-permute-done | bytes 135200 | tf_op jit(solution)/shard_map/ppermute | solution.py:390
  72.8 8.3 %collect.1 = (f32[64,1024]{1,0:T(8,128)S(1)}, f32[1,1024]{1,0:T(1,128)}) custom-call(s32[1]{0:T(128)} %bitcast.me, s32[2,1024]{1,0:T(2,128)S(1)} %add_bitcast_fusion.names, bf16[1024,1152]{1,0:T(8,128)(2,1)S(1)} %weigh.1.weighted, bf16[4096,256]{1,0:T(8,128)(2,1)S(1)} %copy-done.10, bf16[1024,2048]{1,0:T(8,128)(2,1)S(1)} %copy-done.12, ...), custom_call_target="tpu_custom_call" | custom-call | flops 4831838208 | bytes 4194304 | tf_op jit(solution)/shard_map/collect/pallas_call | solution.py:368
  81.2 1.3 %collective-permute-done.16 = f32[32,1024]{1,0:T(8,128)S(1)} collective-permute-done((f32[32,1024]{1,0:T(8,128)S(1)}, f32[32,1024]{1,0:T(8,128)S(1)}, u32[]{:S(2)}, u32[]{:S(2)}) %collective-permute-start.16) | collective-permute-done | bytes 131104 | tf_op jit(solution)/shard_map/ppermute | solution.py:390
  82.5 1.3 %collective-permute-start.17 = (f32[8,1024]{1,0:T(8,128)S(1)}, f32[8,1024]{1,0:T(8,128)S(1)}, u32[]{:S(2)}, u32[]{:S(2)}) collective-permute-start(f32[8,1024]{1,0:T(8,128)S(1)} %get-tuple-element.33), channel_id=1, source_target_pairs={{0,2},{1,3},{2,0},{3,1},{4,6},{5,7},{6,4},{7,5},{8,10},{9,11},{10,... | collective-permute-start | bytes 98312 | tf_op jit(solution)/shard_map/ppermute | solution.py:390
  83.9 2.4 %collective-permute-start.19 = (f32[8,1024]{1,0:T(8,128)S(1)}, f32[8,1024]{1,0:T(8,128)S(1)}, u32[]{:S(2)}, u32[]{:S(2)}) collective-permute-start(f32[8,1024]{1,0:T(8,128)S(1)} %get-tuple-element.34), channel_id=1, source_target_pairs={{0,6},{1,7},{2,4},{3,5},{4,2},{5,3},{6,0},{7,1},{8,14},{9,15},{10,... | collective-permute-start | bytes 98312 | tf_op jit(solution)/shard_map/ppermute | solution.py:390
  86.8 2.8 %collective-permute-done.19 = f32[8,1024]{1,0:T(8,128)S(1)} collective-permute-done((f32[8,1024]{1,0:T(8,128)S(1)}, f32[8,1024]{1,0:T(8,128)S(1)}, u32[]{:S(2)}, u32[]{:S(2)}) %collective-permute-start.19) | collective-permute-done | bytes 32800 | tf_op jit(solution)/shard_map/ppermute | solution.py:390
  89.6 1.5 %collective-permute-done.18 = f32[8,1024]{1,0:T(8,128)S(1)} collective-permute-done((f32[8,1024]{1,0:T(8,128)S(1)}, f32[8,1024]{1,0:T(8,128)S(1)}, u32[]{:S(2)}, u32[]{:S(2)}) %collective-permute-start.18) | collective-permute-done | bytes 32800 | tf_op jit(solution)/shard_map/ppermute | solution.py:390
  (64 shorter events, 8.7 us)
Async XLA Ops:
  2.0 11.4 %collective-permute-start.2 = (bf16[8,1024]{1,0:T(8,128)(2,1)}, bf16[8,1024]{1,0:T(8,128)(2,1)}, u32[]{:S(2)}, u32[]{:S(2)}) collective-permute-start(bf16[8,1024]{1,0:T(8,128)(2,1)} %pad_maximum_fusion), channel_id=1, source_target_pairs={{0,6},{1,7},{2,4},{3,5},{4,2},{5,3},{6,0},{7,1},{8,14},{9,15},{10,... | collective-permute-start | bytes 49160 | tf_op jit(solution)/shard_map/ppermute | solution.py:390
  7.1 6.4 %collective-permute-start.1 = (bf16[8,1024]{1,0:T(8,128)(2,1)}, bf16[8,1024]{1,0:T(8,128)(2,1)}, u32[]{:S(2)}, u32[]{:S(2)}) collective-permute-start(bf16[8,1024]{1,0:T(8,128)(2,1)} %pad_maximum_fusion), channel_id=1, source_target_pairs={{0,4},{1,5},{2,6},{3,7},{4,0},{5,1},{6,2},{7,3},{8,12},{9,13},{10,... | collective-permute-start | bytes 49160 | tf_op jit(solution)/shard_map/ppermute | solution.py:390
  7.1 6.4 %collective-permute-start = (bf16[8,1024]{1,0:T(8,128)(2,1)}, bf16[8,1024]{1,0:T(8,128)(2,1)}, u32[]{:S(2)}, u32[]{:S(2)}) collective-permute-start(bf16[8,1024]{1,0:T(8,128)(2,1)} %pad_maximum_fusion), channel_id=1, source_target_pairs={{0,2},{1,3},{2,0},{3,1},{4,6},{5,7},{6,4},{7,5},{8,10},{9,11},{10,... | collective-permute-start | bytes 49160 | tf_op jit(solution)/shard_map/ppermute | solution.py:390
  7.6 1.6 %copy-start = (bf16[1024,1024]{1,0:T(8,128)(2,1)S(1)}, bf16[1024,1024]{1,0:T(8,128)(2,1)}, u32[]{:S(2)}) copy-start(bf16[1024,1024]{1,0:T(8,128)(2,1)} %pixels.1) | copy-start | bytes 6291460
  9.2 0.9 copy-start.3
  12.2 1.2 %copy-start.13 = (s32[1024,2]{0,1:T(2,128)S(1)}, s32[1024,2]{0,1:T(2,128)}, u32[]{:S(2)}) copy-start(s32[1024,2]{0,1:T(2,128)} %param.7) | copy-start | bytes 24580
  18.8 7.1 %collective-permute-start.3 = (bf16[32,1024]{1,0:T(8,128)(2,1)}, bf16[32,1024]{1,0:T(8,128)(2,1)}, u32[]{:S(2)}, u32[]{:S(2)}) collective-permute-start(bf16[32,1024]{1,0:T(8,128)(2,1)} %concatenate.12), channel_id=1, source_target_pairs={{0,1},{1,0},{2,3},{3,2},{4,5},{5,4},{6,7},{7,6},{8,9},{9,8},{10,11... | collective-permute-start | bytes 196616 | tf_op jit(solution)/shard_map/ppermute | solution.py:390
  18.8 0.9 copy-start.4
  19.8 1.2 %copy-start.7 = (bf16[64,64,64]{2,1,0:T(8,128)(2,1)S(1)}, bf16[64,64,64]{2,1,0:T(8,128)(2,1)}, u32[]{:S(2)}) copy-start(bf16[64,64,64]{2,1,0:T(8,128)(2,1)} %turns.1) | copy-start | bytes 1572868
  22.6 1.4 %copy-start.8 = (bf16[4096,256]{1,0:T(8,128)(2,1)}, bf16[4096,256]{1,0:T(8,128)(2,1)S(1)}, u32[]{:S(2)}) copy-start(bf16[4096,256]{1,0:T(8,128)(2,1)S(1)} %get-tuple-element.17.matrix) | copy-start | bytes 6291460
  24.0 2.0 %copy-start.11 = (bf16[1024,2048]{1,0:T(8,128)(2,1)}, bf16[1024,2048]{1,0:T(8,128)(2,1)S(1)}, u32[]{:S(2)}) copy-start(bf16[1024,2048]{1,0:T(8,128)(2,1)S(1)} %get-tuple-element.18.response) | copy-start | bytes 12582916
  32.7 8.0 %copy-start.1 = (bf16[512,1152]{1,0:T(8,128)(2,1)S(1)}, bf16[512,1152]{1,0:T(8,128)(2,1)}, u32[]{:S(2)}) copy-start(bf16[512,1152]{1,0:T(8,128)(2,1)} %get-tuple-element.31.weighted) | copy-start | bytes 3538948
  32.7 1.0 %copy-start.2 = (bf16[64,1024]{1,0:T(8,128)(2,1)S(1)}, bf16[64,1024]{1,0:T(8,128)(2,1)}, u32[]{:S(2)}) copy-start(bf16[64,1024]{1,0:T(8,128)(2,1)} %concatenate.13.refs) | copy-start | bytes 393220
  34.6 1.6 %copy-start.9 = (bf16[4096,256]{1,0:T(8,128)(2,1)S(1)}, bf16[4096,256]{1,0:T(8,128)(2,1)}, u32[]{:S(2)}) copy-start(bf16[4096,256]{1,0:T(8,128)(2,1)} %copy-done.8) | copy-start | bytes 6291460
  44.0 10.1 %collective-permute-start.12 = (f16[512,128]{1,0:T(8,128)(2,1)S(1)}, f16[512,128]{1,0:T(8,128)(2,1)S(1)}, u32[]{:S(2)}, u32[]{:S(2)}) collective-permute-start(f16[512,128]{1,0:T(8,128)(2,1)S(1)} %convert_element_type.47), channel_id=1, source_target_pairs={{0,24},{8,16},{16,8},{24,0},{1,25},{9,17},{17,9},{25,1},{2,26},{10... | collective-permute-start | bytes 393224 | tf_op jit(solution)/shard_map/ppermute | solution.py:390
  46.7 7.7 %collective-permute-start.11 = (f16[512,128]{1,0:T(8,128)(2,1)S(1)}, f16[512,128]{1,0:T(8,128)(2,1)S(1)}, u32[]{:S(2)}, u32[]{:S(2)}) collective-permute-start(f16[512,128]{1,0:T(8,128)(2,1)S(1)} %convert_element_type.45), channel_id=1, source_target_pairs={{0,16},{8,24},{16,0},{24,8},{1,17},{9,25},{17,1},{25,9},{2,18},{10... | collective-permute-start | bytes 393224 | tf_op jit(solution)/shard_map/ppermute | solution.py:390
  47.2 7.2 %collective-permute-start.10 = (f16[512,128]{1,0:T(8,128)(2,1)S(1)}, f16[512,128]{1,0:T(8,128)(2,1)S(1)}, u32[]{:S(2)}, u32[]{:S(2)}) collective-permute-start(f16[512,128]{1,0:T(8,128)(2,1)S(1)} %convert_element_type.43), channel_id=1, source_target_pairs={{0,8},{8,0},{16,24},{24,16},{1,9},{9,1},{17,25},{25,17},{2,10},{10... | collective-permute-start | bytes 393224 | tf_op jit(solution)/shard_map/ppermute | solution.py:390
  47.5 25.2 %copy-start.12 = (bf16[1024,2048]{1,0:T(8,128)(2,1)S(1)}, bf16[1024,2048]{1,0:T(8,128)(2,1)}, u32[]{:S(2)}) copy-start(bf16[1024,2048]{1,0:T(8,128)(2,1)} %copy-done.11) | copy-start | bytes 12582916
  50.7 22.0 %copy-start.10 = (bf16[4096,256]{1,0:T(8,128)(2,1)S(1)}, bf16[4096,256]{1,0:T(8,128)(2,1)}, u32[]{:S(2)}) copy-start(bf16[4096,256]{1,0:T(8,128)(2,1)} %copy-done.8) | copy-start | bytes 6291460
  50.8 7.0 %collective-permute-start.6 = (f16[512,128]{1,0:T(8,128)(2,1)S(1)}, f16[512,128]{1,0:T(8,128)(2,1)S(1)}, u32[]{:S(2)}, u32[]{:S(2)}) collective-permute-start(f16[512,128]{1,0:T(8,128)(2,1)S(1)} %convert_element_type.41), channel_id=1, source_target_pairs={{0,24},{8,16},{16,8},{24,0},{1,25},{9,17},{17,9},{25,1},{2,26},{10... | collective-permute-start | bytes 393224 | tf_op jit(solution)/shard_map/ppermute | solution.py:390
  53.6 9.3 %collective-permute-start.5 = (f16[512,128]{1,0:T(8,128)(2,1)S(1)}, f16[512,128]{1,0:T(8,128)(2,1)S(1)}, u32[]{:S(2)}, u32[]{:S(2)}) collective-permute-start(f16[512,128]{1,0:T(8,128)(2,1)S(1)} %convert_element_type.39), channel_id=1, source_target_pairs={{0,16},{8,24},{16,0},{24,8},{1,17},{9,25},{17,1},{25,9},{2,18},{10... | collective-permute-start | bytes 393224 | tf_op jit(solution)/shard_map/ppermute | solution.py:390
  54.1 8.8 %collective-permute-start.4 = (f16[512,128]{1,0:T(8,128)(2,1)S(1)}, f16[512,128]{1,0:T(8,128)(2,1)S(1)}, u32[]{:S(2)}, u32[]{:S(2)}) collective-permute-start(f16[512,128]{1,0:T(8,128)(2,1)S(1)} %convert_element_type.37), channel_id=1, source_target_pairs={{0,8},{8,0},{16,24},{24,16},{1,9},{9,1},{17,25},{25,17},{2,10},{10... | collective-permute-start | bytes 393224 | tf_op jit(solution)/shard_map/ppermute | solution.py:390
  54.6 12.1 %collective-permute-start.15 = (bf16[528,128]{1,0:T(8,128)(2,1)S(1)}, bf16[528,128]{1,0:T(8,128)(2,1)S(1)}, u32[]{:S(2)}, u32[]{:S(2)}) collective-permute-start(bf16[528,128]{1,0:T(8,128)(2,1)S(1)} %soften.3.rest_4_), channel_id=1, source_target_pairs={{0,24},{8,16},{16,8},{24,0},{1,25},{9,17},{17,9},{25,1},{2,26},{10... | collective-permute-start | bytes 405512 | tf_op jit(solution)/shard_map/ppermute | solution.py:390
  57.3 11.0 %collective-permute-start.14 = (bf16[528,128]{1,0:T(8,128)(2,1)S(1)}, bf16[528,128]{1,0:T(8,128)(2,1)S(1)}, u32[]{:S(2)}, u32[]{:S(2)}) collective-permute-start(bf16[528,128]{1,0:T(8,128)(2,1)S(1)} %soften.3.rest_4_), channel_id=1, source_target_pairs={{0,16},{8,24},{16,0},{24,8},{1,17},{9,25},{17,1},{25,9},{2,18},{10... | collective-permute-start | bytes 405512 | tf_op jit(solution)/shard_map/ppermute | solution.py:390
  62.9 6.6 %collective-permute-start.13 = (bf16[528,128]{1,0:T(8,128)(2,1)S(1)}, bf16[528,128]{1,0:T(8,128)(2,1)S(1)}, u32[]{:S(2)}, u32[]{:S(2)}) collective-permute-start(bf16[528,128]{1,0:T(8,128)(2,1)S(1)} %soften.3.rest_4_), channel_id=1, source_target_pairs={{0,8},{8,0},{16,24},{24,16},{1,9},{9,1},{17,25},{25,17},{2,10},{10... | collective-permute-start | bytes 405512 | tf_op jit(solution)/shard_map/ppermute | solution.py:390
  64.7 7.3 %collective-permute-start.9 = (bf16[528,128]{1,0:T(8,128)(2,1)S(1)}, bf16[528,128]{1,0:T(8,128)(2,1)S(1)}, u32[]{:S(2)}, u32[]{:S(2)}) collective-permute-start(bf16[528,128]{1,0:T(8,128)(2,1)S(1)} %soften.2.rest_0_), channel_id=1, source_target_pairs={{0,24},{8,16},{16,8},{24,0},{1,25},{9,17},{17,9},{25,1},{2,26},{10... | collective-permute-start | bytes 405512 | tf_op jit(solution)/shard_map/ppermute | solution.py:390
  66.3 6.5 %collective-permute-start.8 = (bf16[528,128]{1,0:T(8,128)(2,1)S(1)}, bf16[528,128]{1,0:T(8,128)(2,1)S(1)}, u32[]{:S(2)}, u32[]{:S(2)}) collective-permute-start(bf16[528,128]{1,0:T(8,128)(2,1)S(1)} %soften.2.rest_0_), channel_id=1, source_target_pairs={{0,16},{8,24},{16,0},{24,8},{1,17},{9,25},{17,1},{25,9},{2,18},{10... | collective-permute-start | bytes 405512 | tf_op jit(solution)/shard_map/ppermute | solution.py:390
  66.7 6.1 %collective-permute-start.7 = (bf16[528,128]{1,0:T(8,128)(2,1)S(1)}, bf16[528,128]{1,0:T(8,128)(2,1)S(1)}, u32[]{:S(2)}, u32[]{:S(2)}) collective-permute-start(bf16[528,128]{1,0:T(8,128)(2,1)S(1)} %soften.2.rest_0_), channel_id=1, source_target_pairs={{0,8},{8,0},{16,24},{24,16},{1,9},{9,1},{17,25},{25,17},{2,10},{10... | collective-permute-start | bytes 405512 | tf_op jit(solution)/shard_map/ppermute | solution.py:390
  81.1 1.4 %collective-permute-start.16 = (f32[32,1024]{1,0:T(8,128)S(1)}, f32[32,1024]{1,0:T(8,128)S(1)}, u32[]{:S(2)}, u32[]{:S(2)}) collective-permute-start(f32[32,1024]{1,0:T(8,128)S(1)} %slice.42), channel_id=1, source_target_pairs={{0,1},{1,0},{2,3},{3,2},{4,5},{5,4},{6,7},{7,6},{8,9},{9,8},{10,11... | collective-permute-start | bytes 393224 | tf_op jit(solution)/shard_map/ppermute | solution.py:390
  82.5 4.2 %collective-permute-start.17 = (f32[8,1024]{1,0:T(8,128)S(1)}, f32[8,1024]{1,0:T(8,128)S(1)}, u32[]{:S(2)}, u32[]{:S(2)}) collective-permute-start(f32[8,1024]{1,0:T(8,128)S(1)} %get-tuple-element.33), channel_id=1, source_target_pairs={{0,2},{1,3},{2,0},{3,1},{4,6},{5,7},{6,4},{7,5},{8,10},{9,11},{10,... | collective-permute-start | bytes 98312 | tf_op jit(solution)/shard_map/ppermute | solution.py:390
  83.9 5.7 %collective-permute-start.19 = (f32[8,1024]{1,0:T(8,128)S(1)}, f32[8,1024]{1,0:T(8,128)S(1)}, u32[]{:S(2)}, u32[]{:S(2)}) collective-permute-start(f32[8,1024]{1,0:T(8,128)S(1)} %get-tuple-element.34), channel_id=1, source_target_pairs={{0,6},{1,7},{2,4},{3,5},{4,2},{5,3},{6,0},{7,1},{8,14},{9,15},{10,... | collective-permute-start | bytes 98312 | tf_op jit(solution)/shard_map/ppermute | solution.py:390
  86.3 4.8 %collective-permute-start.18 = (f32[8,1024]{1,0:T(8,128)S(1)}, f32[8,1024]{1,0:T(8,128)S(1)}, u32[]{:S(2)}, u32[]{:S(2)}) collective-permute-start(f32[8,1024]{1,0:T(8,128)S(1)} %get-tuple-element.35), channel_id=1, source_target_pairs={{0,4},{1,5},{2,6},{3,7},{4,0},{5,1},{6,2},{7,3},{8,12},{9,13},{10,... | collective-permute-start | bytes 98312 | tf_op jit(solution)/shard_map/ppermute | solution.py:390
  (2 other events, 1.6 us)

commit v3 on v2

v3 whole, which is shorter than its diff:
```python
import functools
import math

import jax
import jax.numpy as jnp
from jax import lax
from jax.experimental import pallas as pl
from jax.experimental.pallas import tpu as pltpu
from jax.sharding import PartitionSpec as P

f32, bf16 = jnp.float32, jnp.bfloat16
VMEM = pl.BlockSpec(memory_space=pltpu.VMEM)
SMEM = pl.BlockSpec(memory_space=pltpu.SMEM)
HBM = pl.BlockSpec(memory_space=pltpu.HBM)
LANES, ROWS = 128, 8
NN = (((1,), (0,)), ((), ()))
NT = (((1,), (1,)), ((), ()))


def dot(a, b, dims):
    return lax.dot_general(a, b, dims, preferred_element_type=f32)


def split(x, parts):
    out = []
    for _ in range(parts):
        out.append(x.astype(bf16))
        x = x - out[-1].astype(f32)
    return out


def limits(mib, flops, moved, transcendentals=0):
    return dict(
        compiler_params=pltpu.CompilerParams(vmem_limit_bytes=mib << 20),
        cost_estimate=pl.CostEstimate(flops=flops, bytes_accessed=moved, transcendentals=transcendentals),
    )


def block_spec(steps, shape, dim):
    if steps == 1:
        return VMEM
    index = lambda i: tuple(i if d == dim else 0 for d in range(len(shape)))
    return pl.BlockSpec(shape, index)


def same_spec(steps, shape):
    return VMEM if steps == 1 else pl.BlockSpec(shape, lambda i: (0,) * len(shape))


def start_kernel(pack, pixels_in, turns_in, table_in, kind_in, names_in, *rest):
    matrix, response, weighted, power_out, names = rest[:5]
    pixels, turns, table, kind, done = rest[5:]
    moves = [
        pltpu.make_async_copy(source, target, done.at[i])
        for i, (source, target) in enumerate(
            [(turns_in, turns), (table_in, table), (kind_in, kind), (names_in, names), (pixels_in, pixels)]
        )
    ]
    for move in moves:
        move.start()
    turn_count, angles, _ = turns.shape
    kinds, width = table.shape
    per = LANES // angles
    tiles = width // LANES
    row = lax.broadcasted_iota(jnp.int32, (LANES, LANES), 0) // angles
    col = lax.broadcasted_iota(jnp.int32, (LANES, LANES), 1) // angles
    zero = jnp.zeros((), bf16)
    moves[0].wait()
    moves[1].wait()
    power = split(table[...] * table[...], 2)
    power_out[...] = jnp.concatenate(power, axis=0)
    lhs = jnp.concatenate(
        [
            jnp.concatenate([part[:, t * LANES:(t + 1) * LANES] for part in power], axis=1)
            for t in range(tiles)
        ],
        axis=0,
    )
    for i in range(turn_count // pack):
        wide = []
        for j in range(pack):
            turn = turns[i * pack + j]
            turn = jnp.concatenate([jnp.concatenate([turn] * per, axis=1)] * per, axis=0)
            wide.append(jnp.where(row == col, turn, zero))
        wide = jnp.concatenate(wide, axis=1)
        matrix[i * LANES:(i + 1) * LANES, :] = wide
        value = dot(lhs, jnp.concatenate([wide, wide], axis=0), NN).astype(bf16)
        for j in range(pack):
            for t in range(tiles):
                response[i * kinds:(i + 1) * kinds, j * width + t * LANES:j * width + (t + 1) * LANES] = value[
                    t * kinds:(t + 1) * kinds, j * LANES:(j + 1) * LANES
                ]
    for move in moves[2:]:
        move.wait()
    table3 = jnp.concatenate(split(table[...], 3), axis=0)
    count = pixels.shape[0]
    rows = math.gcd(count, 256)
    ids = lax.broadcasted_iota(jnp.int32, (LANES, rows), 0)
    for i in range(count // rows):
        at = slice(i * rows, (i + 1) * rows)
        hit = jnp.where((ids % kinds == kind[:, at]) & (ids < 3 * kinds), 1.0, 0.0).T.astype(bf16)
        factor = dot(hit[:, :3 * kinds], table3, NN)
        weighted[at, :width] = (pixels[at, :].astype(f32) * factor).astype(bf16)
        weighted[at, width:] = hit


def start(particles, turns, table, kind, names, pack):
    count, pixels = particles.shape
    turn_count, angles, _ = turns.shape
    kinds = table.shape[0]
    steps = turn_count // pack
    return pl.pallas_call(
        functools.partial(start_kernel, pack),
        in_specs=[HBM] * 5,
        out_specs=[VMEM] * 5,
        out_shape=[
            jax.ShapeDtypeStruct((steps * LANES, pack * LANES), bf16),
            jax.ShapeDtypeStruct((steps * kinds, pack * pixels), bf16),
            jax.ShapeDtypeStruct((count, pixels + LANES), bf16),
            jax.ShapeDtypeStruct((2 * kinds, pixels), bf16),
            jax.ShapeDtypeStruct(names.shape, jnp.int32),
        ],
        scratch_shapes=[
            pltpu.VMEM(particles.shape, bf16),
            pltpu.VMEM(turns.shape, bf16),
            pltpu.VMEM(table.shape, f32),
            pltpu.VMEM(kind.shape, jnp.int32),
            pltpu.SemaphoreType.DMA((5,)),
        ],
        name="start",
        **limits(12, 8 * steps * kinds * pack * pixels * LANES, 4 * count * pixels),
    )(particles, turns, table, kind, names)


def pack_kernel(own, other, out):
    rows = own.shape[0]
    out[:rows, :] = own[...]
    out[rows:, :] = other[...]


def pack_pair(own, other):
    return pl.pallas_call(
        pack_kernel,
        in_specs=[VMEM, VMEM],
        out_specs=VMEM,
        out_shape=jax.ShapeDtypeStruct((2 * own.shape[0], own.shape[1]), own.dtype),
        name="pack_pair",
        **limits(4, 0, 4 * own.size),
    )(own, other)


def rotate_kernel(groups, turn_count, power2, matrix, *rest):
    refs = rest[:-4]
    rotated, mean, center, energy = rest[-4:]
    kinds, pixels = power2.shape[0] // 2, power2.shape[1]
    pack = matrix.shape[1] // LANES
    cpg = ROWS // pack
    tiles = pixels // LANES
    group_pairs = cpg * turn_count
    if len(refs) > 1:
        source = jnp.concatenate([block[...].astype(f32) for block in refs], axis=0)
    else:
        source = refs[0][...].astype(f32)
    line = lax.broadcasted_iota(jnp.int32, (ROWS, pixels), 0) // cpg
    copies = []
    for i in range(groups // pack):
        tile = source[i * ROWS:(i + 1) * ROWS, :]
        for k in range(pack):
            out = tile
            for j in range(pack):
                if j != k:
                    out = jnp.where(line == j, pltpu.roll(tile, (j - k) % pack * cpg, 0), out)
            copies.append(out)
    source = jnp.concatenate(copies, axis=0)
    inside = lax.broadcasted_iota(jnp.int32, (groups * ROWS, LANES), 0) % ROWS // cpg
    lhs = jnp.concatenate(
        [
            jnp.concatenate(
                [jnp.where(inside == j, source[:, t * LANES:(t + 1) * LANES], 0.0) for j in range(pack)], axis=1
            )
            for t in range(tiles)
        ],
        axis=0,
    ).astype(bf16)
    for s in range(turn_count // (2 * pack)):
        value = dot(lhs, matrix[s * 2 * LANES:(s + 1) * 2 * LANES, :], NT)
        for t in range(tiles):
            for g in range(groups):
                at = (t * groups + g) * ROWS
                pair = [value[at:at + ROWS, h * LANES:(h + 1) * LANES] for h in range(2)]
                to = g * group_pairs + s * 2 * ROWS
                rotated[to:to + 2 * ROWS, t * LANES:(t + 1) * LANES] = jnp.concatenate(pair, axis=0).astype(bf16)
    power = power2[...]
    pairs = groups * group_pairs
    rows = math.gcd(pairs, 256)
    summed = jnp.zeros((kinds, 1), f32)
    for i in range(pairs // rows):
        at = slice(i * rows, (i + 1) * rows)
        value = rotated[at, :pixels].astype(f32)
        hi, lo = split(value * value, 2)
        total = dot(power, hi, NT) + dot(power, lo, NT)
        total = -0.5 * (total[:kinds] + total[kinds:])
        energy[:, at] = total
        summed = summed + jnp.sum(total, axis=1, keepdims=True)

    @pl.when(pl.program_id(0) == 0)
    def _():
        center[...] = summed * (1.0 / pairs)

    spread = lax.broadcasted_iota(jnp.int32, (kinds, LANES), 0) == lax.broadcasted_iota(jnp.int32, (kinds, LANES), 1)
    mean[...] = jnp.sum(jnp.where(spread, center[...], 0.0), axis=0, keepdims=True)
    blank = jnp.zeros((LANES - 3 * kinds, LANES), f32)
    for i in range(pairs // LANES):
        at = slice(i * LANES, (i + 1) * LANES)
        parts = [part.astype(f32) for part in split(energy[:, at] - center[...], 3)]
        rotated[at, pixels:] = jnp.concatenate(parts + [blank], axis=0).T.astype(bf16)


def rotate(refs, matrix, power2, turn_count, groups):
    kinds, pixels = power2.shape[0] // 2, power2.shape[1]
    cpg = ROWS * LANES // matrix.shape[1]
    groups_all = sum(block.shape[0] for block in refs) // cpg
    steps = groups_all // groups
    pairs = groups * cpg * turn_count
    return pl.pallas_call(
        functools.partial(rotate_kernel, groups, turn_count),
        grid=(steps,),
        in_specs=[same_spec(steps, power2.shape), same_spec(steps, matrix.shape)]
        + [block_spec(steps, (block.shape[0] // steps, pixels), 0) for block in refs],
        out_specs=[block_spec(steps, (pairs, pixels + LANES), 0), same_spec(steps, (1, LANES))],
        out_shape=[
            jax.ShapeDtypeStruct((steps * pairs, pixels + LANES), bf16),
            jax.ShapeDtypeStruct((1, LANES), f32),
        ],
        scratch_shapes=[pltpu.VMEM((kinds, 1), f32), pltpu.VMEM((kinds, pairs), f32)],
        name="rotate",
        **limits(12 if steps == 1 else 32, 8 * steps * pairs * pixels * 64, 2 * steps * pairs * pixels),
    )(power2, matrix, *refs)


def score_kernel(groups, scale, begin, me, here, weighted, names, rotated, *rest):
    outs, acc = rest[:-1], rest[-1]
    step = pl.program_id(0)
    count = acc.shape[1]
    pairs = rotated.shape[0] // groups
    span = math.gcd(count, 256)
    for n in range(count // span):
        cols = slice(n * span, (n + 1) * span)
        at = slice(begin + n * span, begin + (n + 1) * span)
        pix = weighted[at, :]
        for g in range(groups):
            value = scale * dot(rotated[g * pairs:(g + 1) * pairs, :], pix, NT)
            group = (step * groups + g) ^ here[0]
            for k in range(2):
                rows = slice(k * pairs, (k + 1) * pairs)
                hit = names[k:k + 1, at] == group
                if g == 0:
                    hit = hit | (step == 0)
                acc[rows, cols] = jnp.where(hit, value, acc[rows, cols])

    @pl.when(step == pl.num_programs(0) - 1)
    def _():
        share = outs[0].shape[1]
        for k, out in enumerate(outs):
            start = pl.multiple_of((me[0] ^ k) * share, share)
            out[...] = acc[:, pl.ds(start, share)]


def score(begin, count, weighted, names, rotated, me, here, peers, group_pairs, groups, scale):
    width = weighted.shape[1]
    steps = rotated.shape[0] // (group_pairs * groups)
    share = count // peers
    rows = 2 * group_pairs
    return pl.pallas_call(
        functools.partial(score_kernel, groups, scale, begin),
        grid=(steps,),
        in_specs=[
            SMEM,
            SMEM,
            same_spec(steps, weighted.shape),
            same_spec(steps, names.shape),
            block_spec(steps, (groups * group_pairs, width), 0),
        ],
        out_specs=[same_spec(steps, (rows, share))] * peers,
        out_shape=[jax.ShapeDtypeStruct((rows, share), f32)] * peers,
        scratch_shapes=[pltpu.VMEM((rows, count), f32)],
        name="score",
        **limits(12 if steps == 1 else 32, 2 * rotated.shape[0] * width * count, 2 * rotated.shape[0] * width),
    )(me, here, weighted, names, rotated)


def soften_kernel(scores, mean, out):
    value = scores[...]
    rows, share = value.shape
    top = jnp.max(value, axis=0, keepdims=True)
    grown = jnp.exp(value - top)
    total = jnp.sum(grown, axis=0, keepdims=True)
    out[:rows, :] = (grown * (1.0 / total)).astype(bf16)
    tail = jnp.zeros((2 * ROWS, share), f32)
    at = lax.broadcasted_iota(jnp.int32, tail.shape, 0)
    centers = mean[...]
    if share > LANES:
        centers = jnp.concatenate([centers, jnp.zeros((1, share - LANES), f32)], axis=1)
    for i, row in enumerate(split(top + jnp.log(total), 3) + split(centers, 3)):
        tail = jnp.where(at == i, row.astype(f32), tail)
    out[rows:, :] = tail.astype(bf16)


def soften(scores, mean):
    rows, share = scores.shape
    return pl.pallas_call(
        soften_kernel,
        in_specs=[VMEM, VMEM],
        out_specs=VMEM,
        out_shape=jax.ShapeDtypeStruct((rows + 2 * ROWS, share), bf16),
        name="soften",
        **limits(8, 4 * rows * share, 6 * rows * share, rows * share),
    )(scores, mean)


def collect_kernel(groups, parts, turn_count, kinds, scale, begin, peers, more, me, here, names, weighted, *rest):
    matrix, response = rest[:2]
    blocks = rest[2:2 + peers]
    before = rest[2 + peers:2 + peers + (parts + 1) * more]
    sums = rest[2 + peers + (parts + 1) * more:][:parts]
    logs, weights, lhs, by_kind = rest[-4:]
    step = pl.program_id(0)
    pixels = weighted.shape[1] - LANES
    share = blocks[0].shape[1]
    count = share * peers
    rows = weights.shape[0]
    pairs = rows // 2
    pack = matrix.shape[1] // LANES
    cpg = ROWS // pack
    tiles = pixels // LANES
    turns = turn_count // pack
    own = slice(begin, begin + count)

    @pl.when(step == 0)
    def _():
        center = jnp.zeros((1, share), f32)
        for k, block in enumerate(blocks):
            start = pl.multiple_of((me[0] ^ k) * share, share)
            weights[:, pl.ds(start, share)] = block[:rows, :]
            tail = block[rows:, :].astype(f32)
            logs[0:1, pl.ds(begin + start, share)] = tail[0:1] + tail[1:2] + tail[2:3]
            center = center + (tail[3:4] + tail[4:5] + tail[5:6])
        line = lax.broadcasted_iota(jnp.int32, (2 * ROWS, LANES), 0)
        first = lax.broadcasted_iota(jnp.int32, (2 * ROWS, LANES), 1) < kinds
        stack = jnp.zeros((2 * ROWS, LANES), f32)
        for i, part in enumerate(split(center[:, :LANES], 3)):
            stack = jnp.where((line == i) & first, part.astype(f32), stack)
        moved = dot(stack.astype(bf16), weighted[own, pixels:], NT)
        logs[:, own] = logs[:, own] + scale * jnp.sum(moved, axis=0, keepdims=True)
        if more:
            logs[:, :begin] = before[-1][:, :begin]

    zero = jnp.zeros((), bf16)
    for g in range(0, groups, 2):
        dense = []
        for q in range(2):
            group = (step * groups + g + q) ^ here[0]
            dense.append(
                jnp.where(names[0:1, own] == group, weights[:pairs, :], zero)
                + jnp.where(names[1:2, own] == group, weights[pairs:, :], zero)
            )
        value = dot(jnp.concatenate(dense, axis=0), weighted[own, :], NN)
        for i in range(turns):
            for t in range(tiles):
                pair = [
                    value[q * pairs + i * ROWS:q * pairs + (i + 1) * ROWS, t * LANES:(t + 1) * LANES]
                    for q in range(2)
                ]
                at = (t * groups + g) * ROWS
                lhs[at:at + 2 * ROWS, i * LANES:(i + 1) * LANES] = jnp.concatenate(pair, axis=0).astype(bf16)
            for q in range(2):
                by_kind[(g + q) * ROWS:(g + q + 1) * ROWS, i * kinds:(i + 1) * kinds] = value[
                    q * pairs + i * ROWS:q * pairs + (i + 1) * ROWS, pixels:pixels + kinds
                ]
    total = dot(lhs[...], matrix[...], NN)
    heavy = dot(jnp.concatenate(split(by_kind[...], 2), axis=0), response[...], NN)
    heavy = heavy[:groups * ROWS] + heavy[groups * ROWS:]
    upper = lax.broadcasted_iota(jnp.int32, (ROWS, LANES), 0) < cpg

    def fold(terms):
        out = terms[0]
        for j in range(1, pack):
            out = out + pltpu.roll(terms[j], ROWS - j * cpg, 0)
        return out

    for g in range(groups):
        to = slice(g // parts * ROWS, (g // parts + 1) * ROWS)
        for t in range(tiles):
            lanes = slice(t * LANES, (t + 1) * LANES)
            at = slice((t * groups + g) * ROWS, (t * groups + g + 1) * ROWS)
            top = fold([total[at, j * LANES:(j + 1) * LANES] for j in range(pack)])
            at = slice(g * ROWS, (g + 1) * ROWS)
            low = fold(
                [heavy[at, j * pixels + t * LANES:j * pixels + (t + 1) * LANES] for j in range(pack)]
            )
            value = jnp.where(upper, top, pltpu.roll(low, cpg, 0))
            if more:
                value = value + before[g % parts][to, lanes]
            sums[g % parts][to, lanes] = value


def collect(
    begin, blocks, before, names, weighted, matrix, response, me, here, parts, turn_count, kinds, group_pairs, groups,
    groups_all, scale
):
    count, width = weighted.shape
    pixels = width - LANES
    peers = len(blocks)
    steps = groups_all // groups
    turns = matrix.shape[0] // LANES
    rows = groups * ROWS // parts
    sums_spec = [block_spec(steps, (rows, pixels), 0)] * parts
    return pl.pallas_call(
        functools.partial(
            collect_kernel, groups, parts, turn_count, kinds, scale, begin, peers, 1 if before else 0
        ),
        grid=(steps,),
        in_specs=[SMEM, SMEM]
        + [same_spec(steps, a.shape) for a in (names, weighted, matrix, response)]
        + [same_spec(steps, b.shape) for b in blocks]
        + (sums_spec + [same_spec(steps, (1, count))] if before else []),
        out_specs=sums_spec + [same_spec(steps, (1, count))],
        out_shape=[jax.ShapeDtypeStruct((steps * rows, pixels), f32)] * parts
        + [jax.ShapeDtypeStruct((1, count), f32)],
        scratch_shapes=[
            pltpu.VMEM((2 * group_pairs, peers * blocks[0].shape[1]), bf16),
            pltpu.VMEM((pixels // LANES * groups * ROWS, turns * LANES), bf16),
            pltpu.VMEM((groups * ROWS, turns * kinds), f32),
        ],
        name="collect",
        **limits(
            20 if steps == 1 else 40, 2 * groups_all * group_pairs * width * peers * blocks[0].shape[1],
            4 * count * pixels
        ),
    )(me, here, names, weighted, matrix, response, *blocks, *before)


def add_kernel(left, right, *outs):
    rows = outs[0].shape[0]
    for i, out in enumerate(outs):
        at = slice(i * rows, (i + 1) * rows)
        out[...] = left[at, :] + right[at, :]


def add_cut(left, right, pieces):
    shape = (left.shape[0] // pieces, left.shape[1])
    return pl.pallas_call(
        add_kernel,
        in_specs=[VMEM, VMEM],
        out_specs=[VMEM] * pieces,
        out_shape=[jax.ShapeDtypeStruct(shape, f32)] * pieces,
        name="add_cut",
        **limits(4, left.size, 12 * left.size),
    )(left, right)


def finish_kernel(*refs):
    sums, weights = refs[-2:]
    total = refs[0][...]
    for ref in refs[1:-2]:
        total = total + ref[...]
    sums[...] = total[:sums.shape[0], :].astype(bf16)
    weights[...] = total[sums.shape[0]:, :]


def finish(pieces, cpg):
    shape = (cpg, pieces[0].shape[1])
    return pl.pallas_call(
        finish_kernel,
        in_specs=[VMEM] * len(pieces),
        out_specs=[VMEM] * 2,
        out_shape=[jax.ShapeDtypeStruct(shape, bf16), jax.ShapeDtypeStruct(shape, f32)],
        name="finish",
        **limits(4, pieces[0].size, 12 * pieces[0].size),
    )(*pieces)


def swap(x, axis, k):
    return lax.ppermute(x, axis, [(i, i ^ k) for i in range(lax.axis_size(axis))])


def local(particles, candidates, defocus, ctf_table, references, rotations):
    count, pixels = particles.shape
    peers = lax.axis_size("cls")
    owners = lax.axis_size("dom")
    paired = owners & (owners - 1) == 0 and 4 <= owners <= 8
    turn_count = rotations.shape[0]
    cpg = references.shape[0]
    pack = ROWS // cpg
    group_pairs = cpg * turn_count
    groups = math.gcd(owners, 8)
    kinds = ctf_table.shape[0]
    scale = 4.0 / math.sqrt(pixels * peers)
    me = lax.axis_index("cls").astype(jnp.int32).reshape(1)
    here = lax.axis_index("dom").astype(jnp.int32).reshape(1)
    if paired:
        pair = pack_pair(references, swap(references, "dom", 1))
        refs = [pair] + [swap(pair, "dom", 2 * k) for k in range(1, owners // 2)]
    else:
        here = jnp.zeros_like(here)
        refs = [lax.all_gather(references, "dom", axis=0, tiled=True)]
    matrix, response, weighted, power2, names = start(
        particles, rotations, ctf_table, defocus.reshape(1, count), candidates.T, pack
    )
    rotated, mean = rotate(refs, matrix, power2, turn_count, groups)
    chunks = 2
    size = count // chunks
    blocks = []
    for c in range(chunks):
        cut = score(c * size, size, weighted, names, rotated, me, here, peers, group_pairs, groups, scale)
        total = cut[0]
        for k in range(1, peers):
            total = total + swap(cut[k].astype(jnp.float16), "cls", k).astype(f32)
        own = soften(total, mean)
        blocks.append([own] + [swap(own, "cls", k) for k in range(1, peers)])
    parts = 2 if paired else 1
    out = []
    for c in range(chunks):
        out = collect(
            c * size, blocks[c], out, names, weighted, matrix, response, me, here, parts, turn_count, kinds,
            group_pairs, groups, owners, scale
        )
    if paired:
        pieces = add_cut(out[0], swap(out[1], "dom", 1), owners // 2)
        pieces = [pieces[0]] + [swap(pieces[k], "dom", 2 * k) for k in range(1, owners // 2)]
    else:
        pieces = [lax.psum_scatter(out[0], "dom", scatter_dimension=0, tiled=True)]
    class_sums, class_weights = finish(pieces, cpg)
    return class_sums, class_weights, out[-1].reshape(count)


def solution(mesh):
    in_specs = (P("dom", "cls"), P("dom", None), P("dom"), P(None, "cls"), P("dom", "cls"), P())
    out_specs = (P("dom", "cls"), P("dom", "cls"), P("dom"))
    return jax.shard_map(local, mesh=mesh, in_specs=in_specs, out_specs=out_specs, check_vma=False)
```

time: 93.5 us -> 76.6 us (0.82)
  local copies, waits for them, and re-layouts: 26.7 us -> 10.7 us
  Pallas kernels: 22.4 us -> 25.9 us
  waiting for transfers between devices: 15.1 us -> 12 us
  other arithmetic: 1.67 us -> 0.27 us
  starting transfers between devices: 25.5 us -> 26.5 us
    concatenate x2 -> x0, local copies, waits for them, and re-layouts: 12.1 us -> none  [the longest x1 6.8 us: gather_dom(): return jnp.concatenate([half, swap(half, 'dom', 1)], axis=0)]
    pallas_call x5 -> x8, Pallas kernels: 17.6 us -> 21.2 us  [the longest x2 11.6 us: collect(): pl.pallas_call(functools.partial(collect_kernel, groups, parts, turn_coun...]
    ppermute x20, waiting for transfers between devices: 15.1 us -> 12 us  [swap(): lax.ppermute(x, axis, [(i, i ^ k) for i in range(lax.axis_size(axis))])]
    slice x6 -> x0, local copies, waits for them, and re-layouts: 2.44 us -> none  [the longest x2 1.21 us: local(): return (total[:cpg].astype(bf16), total[cpg:], logs.reshape(count))]
    unnamed x28 -> x22, local copies, waits for them, and re-layouts: 12.2 us -> 10.7 us
    concatenate x1 -> x0, other arithmetic: 1.39 us -> none  [local(): refs = gather_dom(jnp.concatenate([references] * pack, axis=0), owners)]
    ppermute x20, starting transfers between devices: 25.5 us -> 26.5 us  [swap(): lax.ppermute(x, axis, [(i, i ^ k) for i in range(lax.axis_size(axis))])]
  transfers between devices with their start and end apart: 20 -> 20, of which waited for: 7 -> 6; matrix products, arithmetic and copies ran while one was open for 2% -> 0% of each run, Pallas kernels for 7% -> 15%
where the time goes in v3:
time: 76.6 us; the launch traced here: 76.2 us
  starting transfers between devices  26.5 us (35%)
  Pallas kernels  25.9 us (34%)
  waiting for transfers between devices  12 us (16%)
  local copies, waits for them, and re-layouts  10.7 us (14%)
  between operations  0.81 us (1%)
    ppermute x20, starting transfers between devices, swap(): lax.ppermute(x, axis, [(i, i ^ k) for i in range(lax.axis_size(axis))])  26.5 us
    ppermute x20, waiting for transfers between devices, swap(): lax.ppermute(x, axis, [(i, i ^ k) for i in range(lax.axis_size(axis))])  12 us
    pallas_call x2, Pallas kernels, collect(): pl.pallas_call(functools.partial(collect_kernel, groups, parts, turn_coun...  11.6 us
    unnamed x22, local copies, waits for them, and re-layouts  10.7 us
    pallas_call x2, Pallas kernels, score(): pl.pallas_call(functools.partial(score_kernel, groups, scale, begin), gri...  6.08 us
    pallas_call x1, Pallas kernels, rotate(): pl.pallas_call(functools.partial(rotate_kernel, groups, turn_count), grid...  4.46 us
    pallas_call x1, Pallas kernels, start(): pl.pallas_call(functools.partial(start_kernel, pack), in_specs=[HBM] * 5,...  2.8 us
  transfers between devices with their start and end apart: 20, of which 6 were waited for; matrix products, arithmetic and copies ran while one was open for 0% of the time, Pallas kernels for 15%

profile of v3, /device:TPU:0, one launch (start us, length us, event | category | flops | bytes accessed | tf_op | source)
XLA Modules:
  0.0 76.2 jit_solution(12436400222114028545)
XLA Ops:
  1.1 1.0 %collective-permute-done.other = bf16[4,1024]{1,0:T(4,128)(2,1)S(1)} collective-permute-done((bf16[4,1024]{1,0:T(4,128)(2,1)}, bf16[4,1024]{1,0:T(4,128)(2,1)S(1)}, u32[]{:S(2)}, u32[]{:S(2)}) %collective-permute-start) | collective-permute-done | bytes 8224 | tf_op jit(solution)/shard_map/ppermute | solution.py:484
  2.9 2.9 %collective-permute-start.1 = (bf16[8,1024]{1,0:T(8,128)(2,1)S(1)}, bf16[8,1024]{1,0:T(8,128)(2,1)S(1)}, u32[]{:S(2)}, u32[]{:S(2)}) collective-permute-start(bf16[8,1024]{1,0:T(8,128)(2,1)S(1)} %pack_pair.1.rest_0_), channel_id=1, source_target_pairs={{0,2},{1,3},{2,0},{3,1},{4,6},{5,7},{6,4},{7,5},{8,10},{9,11},{10,... | collective-permute-start | bytes 49160 | tf_op jit(solution)/shard_map/ppermute | solution.py:484
  5.8 2.6 %collective-permute-start.2 = (bf16[8,1024]{1,0:T(8,128)(2,1)S(1)}, bf16[8,1024]{1,0:T(8,128)(2,1)S(1)}, u32[]{:S(2)}, u32[]{:S(2)}) collective-permute-start(bf16[8,1024]{1,0:T(8,128)(2,1)S(1)} %pack_pair.1.rest_0_), channel_id=1, source_target_pairs={{0,4},{1,5},{2,6},{3,7},{4,0},{5,1},{6,2},{7,3},{8,12},{9,13},{10,... | collective-permute-start | bytes 49160 | tf_op jit(solution)/shard_map/ppermute | solution.py:484
  8.4 1.6 %copy-done.6 = bf16[1024,1024]{1,0:T(8,128)(2,1)S(1)} copy-done((bf16[1024,1024]{1,0:T(8,128)(2,1)S(1)}, bf16[1024,1024]{1,0:T(8,128)(2,1)}, u32[]{:S(2)}) %copy-start.6) | copy-done | bytes 2097176
  10.0 1.2 %copy-done.7 = bf16[64,64,64]{2,1,0:T(8,128)(2,1)S(1)} copy-done((bf16[64,64,64]{2,1,0:T(8,128)(2,1)S(1)}, bf16[64,64,64]{2,1,0:T(8,128)(2,1)}, u32[]{:S(2)}) %copy-start.7) | copy-done | bytes 524312
  11.2 0.9 %copy-done.8 = f32[32,1024]{1,0:T(8,128)S(1)} copy-done((f32[32,1024]{1,0:T(8,128)S(1)}, f32[32,1024]{1,0:T(8,128)}, u32[]{:S(2)}) %copy-start.8) | copy-done | bytes 131096
  13.5 2.8 %start.1 = (bf16[4096,256]{1,0:T(8,128)(2,1)S(1)}, bf16[1024,2048]{1,0:T(8,128)(2,1)S(1)}, bf16[1024,1152]{1,0:T(8,128)(2,1)S(1)}, bf16[64,1024]{1,0:T(8,128)(2,1)S(1)}, s32[2,1024]{1,0:T(2,128)S(1)}) custom-call(bf16[1024,1024]{1,0:T(8,128)(2,1)S(1)} %copy-done.6, bf16[64,64,64]{2,1,0:T(8,128)(2,1)S(1)} %copy-done.7, f32[32,1024]{1,0:T(8,128)S(1)} %copy-done.8, ...), custom_call_target="tpu_custom_call" | custom-call | flops 2147483648 | bytes 4194304 | tf_op jit(solution)/shard_map/start/pallas_call | solution.py:112
  16.3 2.0 %copy-done = bf16[1024,2048]{1,0:T(8,128)(2,1)} copy-done((bf16[1024,2048]{1,0:T(8,128)(2,1)}, bf16[1024,2048]{1,0:T(8,128)(2,1)S(1)}, u32[]{:S(2)}) %copy-start) | copy-done | bytes 4194328
  18.3 1.4 %copy-done.2 = bf16[4096,256]{1,0:T(8,128)(2,1)} copy-done((bf16[4096,256]{1,0:T(8,128)(2,1)}, bf16[4096,256]{1,0:T(8,128)(2,1)S(1)}, u32[]{:S(2)}) %copy-start.2) | copy-done | bytes 2097176
  19.7 1.6 %copy-done.3 = bf16[4096,256]{1,0:T(8,128)(2,1)S(1)} copy-done((bf16[4096,256]{1,0:T(8,128)(2,1)S(1)}, bf16[4096,256]{1,0:T(8,128)(2,1)}, u32[]{:S(2)}) %copy-start.3) | copy-done | bytes 2097176
  21.3 4.5 %rotate.1 = (bf16[2048,1152]{1,0:T(8,128)(2,1)S(1)}, f32[1,128]{1,0:T(1,128)S(1)}) custom-call(bf16[64,1024]{1,0:T(8,128)(2,1)S(1)} %get-tuple-element.34.power2, bf16[4096,256]{1,0:T(8,128)(2,1)S(1)} %copy-done.3, bf16[8,1024]{1,0:T(8,128)(2,1)S(1)} %pack_pair.1.rest_0_, bf16[8,1024]{1,0:T(8,128)(2,1)S(1)} %collective-permute-done.1.rest_1_, ...), custom_call_target="tpu_custom_call" | custom-call | flops 1073741824 | bytes 4194304 | tf_op jit(solution)/shard_map/rotate/pallas_call | solution.py:225
  25.7 3.0 %score.3 = (f32[512,128]{1,0:T(8,128)S(1)}, f32[512,128]{1,0:T(8,128)S(1)}, f32[512,128]{1,0:T(8,128)S(1)}, f32[512,128]{1,0:T(8,128)S(1)}) custom-call(s32[1]{0:T(128)} %bitcast.me, s32[1]{0:T(128)} %bitcast.1.here, bf16[1024,1152]{1,0:T(8,128)(2,1)S(1)} %get-tuple-element.31.weighted, s32[2,1024]{1,0:T(2,128)S(1)} %get-tuple-element.30.names, ...), custom_call_target="tpu_custom_call" | custom-call | flops 2415919104 | bytes 4718592 | tf_op jit(solution)/shard_map/score/pallas_call | solution.py:274
  28.8 1.8 %collective-permute-start.10 = (f16[512,128]{1,0:T(8,128)(2,1)S(1)}, f16[512,128]{1,0:T(8,128)(2,1)S(1)}, u32[]{:S(2)}, u32[]{:S(2)}) collective-permute-start(f16[512,128]{1,0:T(8,128)(2,1)S(1)} %convert_element_type.42), channel_id=1, source_target_pairs={{0,8},{8,0},{16,24},{24,16},{1,9},{9,1},{17,25},{25,17},{2,10},{10... | collective-permute-start | bytes 393224 | tf_op jit(solution)/shard_map/ppermute | solution.py:484
  30.6 1.6 %collective-permute-start.11 = (f16[512,128]{1,0:T(8,128)(2,1)S(1)}, f16[512,128]{1,0:T(8,128)(2,1)S(1)}, u32[]{:S(2)}, u32[]{:S(2)}) collective-permute-start(f16[512,128]{1,0:T(8,128)(2,1)S(1)} %convert_element_type.44), channel_id=1, source_target_pairs={{0,16},{8,24},{16,0},{24,8},{1,17},{9,25},{17,1},{25,9},{2,18},{10... | collective-permute-start | bytes 393224 | tf_op jit(solution)/shard_map/ppermute | solution.py:484
  32.5 3.0 %score.2 = (f32[512,128]{1,0:T(8,128)S(1)}, f32[512,128]{1,0:T(8,128)S(1)}, f32[512,128]{1,0:T(8,128)S(1)}, f32[512,128]{1,0:T(8,128)S(1)}) custom-call(s32[1]{0:T(128)} %bitcast.me, s32[1]{0:T(128)} %bitcast.1.here, bf16[1024,1152]{1,0:T(8,128)(2,1)S(1)} %get-tuple-element.31.weighted, s32[2,1024]{1,0:T(2,128)S(1)} %get-tuple-element.30.names, ...), custom_call_target="tpu_custom_call" | custom-call | flops 2415919104 | bytes 4718592 | tf_op jit(solution)/shard_map/score/pallas_call | solution.py:274
  35.6 1.8 %collective-permute-start.4 = (f16[512,128]{1,0:T(8,128)(2,1)S(1)}, f16[512,128]{1,0:T(8,128)(2,1)S(1)}, u32[]{:S(2)}, u32[]{:S(2)}) collective-permute-start(f16[512,128]{1,0:T(8,128)(2,1)S(1)} %convert_element_type.36), channel_id=1, source_target_pairs={{0,8},{8,0},{16,24},{24,16},{1,9},{9,1},{17,25},{25,17},{2,10},{10... | collective-permute-start | bytes 393224 | tf_op jit(solution)/shard_map/ppermute | solution.py:484
  37.4 1.6 %collective-permute-start.5 = (f16[512,128]{1,0:T(8,128)(2,1)S(1)}, f16[512,128]{1,0:T(8,128)(2,1)S(1)}, u32[]{:S(2)}, u32[]{:S(2)}) collective-permute-start(f16[512,128]{1,0:T(8,128)(2,1)S(1)} %convert_element_type.38), channel_id=1, source_target_pairs={{0,16},{8,24},{16,0},{24,8},{1,17},{9,25},{17,1},{25,9},{2,18},{10... | collective-permute-start | bytes 393224 | tf_op jit(solution)/shard_map/ppermute | solution.py:484
  39.6 1.8 %collective-permute-start.13 = (bf16[528,128]{1,0:T(8,128)(2,1)S(1)}, bf16[528,128]{1,0:T(8,128)(2,1)S(1)}, u32[]{:S(2)}, u32[]{:S(2)}) collective-permute-start(bf16[528,128]{1,0:T(8,128)(2,1)S(1)} %soften.3.rest_2_), channel_id=1, source_target_pairs={{0,8},{8,0},{16,24},{24,16},{1,9},{9,1},{17,25},{25,17},{2,10},{10... | collective-permute-start | bytes 405512 | tf_op jit(solution)/shard_map/ppermute | solution.py:484
  41.4 1.5 %collective-permute-start.14 = (bf16[528,128]{1,0:T(8,128)(2,1)S(1)}, bf16[528,128]{1,0:T(8,128)(2,1)S(1)}, u32[]{:S(2)}, u32[]{:S(2)}) collective-permute-start(bf16[528,128]{1,0:T(8,128)(2,1)S(1)} %soften.3.rest_2_), channel_id=1, source_target_pairs={{0,16},{8,24},{16,0},{24,8},{1,17},{9,25},{17,1},{25,9},{2,18},{10... | collective-permute-start | bytes 405512 | tf_op jit(solution)/shard_map/ppermute | solution.py:484
  42.9 1.8 %collective-permute-start.15 = (bf16[528,128]{1,0:T(8,128)(2,1)S(1)}, bf16[528,128]{1,0:T(8,128)(2,1)S(1)}, u32[]{:S(2)}, u32[]{:S(2)}) collective-permute-start(bf16[528,128]{1,0:T(8,128)(2,1)S(1)} %soften.3.rest_2_), channel_id=1, source_target_pairs={{0,24},{8,16},{16,8},{24,0},{1,25},{9,17},{17,9},{25,1},{2,26},{10... | collective-permute-start | bytes 405512 | tf_op jit(solution)/shard_map/ppermute | solution.py:484
  44.7 2.1 %collective-permute-done.5 = f16[512,128]{1,0:T(8,128)(2,1)S(1)} collective-permute-done((f16[512,128]{1,0:T(8,128)(2,1)S(1)}, f16[512,128]{1,0:T(8,128)(2,1)S(1)}, u32[]{:S(2)}, u32[]{:S(2)}) %collective-permute-start.5) | collective-permute-done | bytes 131104 | tf_op jit(solution)/shard_map/ppermute | solution.py:484
  47.1 0.8 %collective-permute-start.7 = (bf16[528,128]{1,0:T(8,128)(2,1)S(1)}, bf16[528,128]{1,0:T(8,128)(2,1)S(1)}, u32[]{:S(2)}, u32[]{:S(2)}) collective-permute-start(bf16[528,128]{1,0:T(8,128)(2,1)S(1)} %soften.2.rest_2_), channel_id=1, source_target_pairs={{0,8},{8,0},{16,24},{24,16},{1,9},{9,1},{17,25},{25,17},{2,10},{10... | collective-permute-start | bytes 405512 | tf_op jit(solution)/shard_map/ppermute | solution.py:484
  47.9 1.1 %collective-permute-start.8 = (bf16[528,128]{1,0:T(8,128)(2,1)S(1)}, bf16[528,128]{1,0:T(8,128)(2,1)S(1)}, u32[]{:S(2)}, u32[]{:S(2)}) collective-permute-start(bf16[528,128]{1,0:T(8,128)(2,1)S(1)} %soften.2.rest_2_), channel_id=1, source_target_pairs={{0,16},{8,24},{16,0},{24,8},{1,17},{9,25},{17,1},{25,9},{2,18},{10... | collective-permute-start | bytes 405512 | tf_op jit(solution)/shard_map/ppermute | solution.py:484
  49.0 1.6 %collective-permute-start.9 = (bf16[528,128]{1,0:T(8,128)(2,1)S(1)}, bf16[528,128]{1,0:T(8,128)(2,1)S(1)}, u32[]{:S(2)}, u32[]{:S(2)}) collective-permute-start(bf16[528,128]{1,0:T(8,128)(2,1)S(1)} %soften.2.rest_2_), channel_id=1, source_target_pairs={{0,24},{8,16},{16,8},{24,0},{1,25},{9,17},{17,9},{25,1},{2,26},{10... | collective-permute-start | bytes 405512 | tf_op jit(solution)/shard_map/ppermute | solution.py:484
  50.6 2.0 %collective-permute-done.14.rest_4_ = bf16[528,128]{1,0:T(8,128)(2,1)S(1)} collective-permute-done((bf16[528,128]{1,0:T(8,128)(2,1)S(1)}, bf16[528,128]{1,0:T(8,128)(2,1)S(1)}, u32[]{:S(2)}, u32[]{:S(2)}) %collective-permute-start.14) | collective-permute-done | bytes 135200 | tf_op jit(solution)/shard_map/ppermute | solution.py:484
  52.6 5.7 %collect.2 = (f32[32,1024]{1,0:T(8,128)S(1)}, f32[32,1024]{1,0:T(8,128)S(1)}, f32[1,1024]{1,0:T(1,128)S(1)}) custom-call(s32[1]{0:T(128)} %bitcast.me, s32[1]{0:T(128)} %bitcast.1.here, s32[2,1024]{1,0:T(2,128)S(1)} %get-tuple-element.30.names, bf16[1024,1152]{1,0:T(8,128)(2,1)S(1)} %get-tuple-element.31.weighted, bf16[4096,256]{1,0:T(8,128)(2,1)S(1)} %copy-done.4, ...), custom_call_target="tpu_custom_call" | custom-call | flops 2415919104 | bytes 4194304 | tf_op jit(solution)/shard_map/collect/pallas_call | solution.py:418
  58.3 6.0 %collect.3 = (f32[32,1024]{1,0:T(8,128)S(1)}, f32[32,1024]{1,0:T(8,128)S(1)}, f32[1,1024]{1,0:T(1,128)}) custom-call(s32[1]{0:T(128)} %bitcast.me, s32[1]{0:T(128)} %bitcast.1.here, s32[2,1024]{1,0:T(2,128)S(1)} %get-tuple-element.30.names, bf16[1024,1152]{1,0:T(8,128)(2,1)S(1)} %get-tuple-element.31.weighted, bf16[4096,256]{1,0:T(8,128)(2,1)S(1)} %copy-done.4, ...), custom_call_target="tpu_custom_call" | custom-call | flops 2415919104 | bytes 4194304 | tf_op jit(solution)/shard_map/collect/pallas_call | solution.py:418
  64.3 1.3 %collective-permute-done.16.right = f32[32,1024]{1,0:T(8,128)S(1)} collective-permute-done((f32[32,1024]{1,0:T(8,128)S(1)}, f32[32,1024]{1,0:T(8,128)S(1)}, u32[]{:S(2)}, u32[]{:S(2)}) %collective-permute-start.16) | collective-permute-done | bytes 131104 | tf_op jit(solution)/shard_map/ppermute | solution.py:484
  65.7 0.7 collective-permute-start.17
  66.4 3.5 %collective-permute-start.18 = (f32[8,1024]{1,0:T(8,128)S(1)}, f32[8,1024]{1,0:T(8,128)S(1)}, u32[]{:S(2)}, u32[]{:S(2)}) collective-permute-start(f32[8,1024]{1,0:T(8,128)S(1)} %get-tuple-element.52), channel_id=1, source_target_pairs={{0,4},{1,5},{2,6},{3,7},{4,0},{5,1},{6,2},{7,3},{8,12},{9,13},{10,... | collective-permute-start | bytes 98312 | tf_op jit(solution)/shard_map/ppermute | solution.py:484
  70.1 2.1 %collective-permute-done.18.refs_2_ = f32[8,1024]{1,0:T(8,128)S(1)} collective-permute-done((f32[8,1024]{1,0:T(8,128)S(1)}, f32[8,1024]{1,0:T(8,128)S(1)}, u32[]{:S(2)}, u32[]{:S(2)}) %collective-permute-start.18) | collective-permute-done | bytes 32800 | tf_op jit(solution)/shard_map/ppermute | solution.py:484
  72.2 3.4 %collective-permute-done.19.refs_3_ = f32[8,1024]{1,0:T(8,128)S(1)} collective-permute-done((f32[8,1024]{1,0:T(8,128)S(1)}, f32[8,1024]{1,0:T(8,128)S(1)}, u32[]{:S(2)}, u32[]{:S(2)}) %collective-permute-start.19) | collective-permute-done | bytes 32800 | tf_op jit(solution)/shard_map/ppermute | solution.py:484
  (49 shorter events, 4.7 us)
Async XLA Ops:
  0.6 1.6 %collective-permute-start = (bf16[4,1024]{1,0:T(4,128)(2,1)}, bf16[4,1024]{1,0:T(4,128)(2,1)S(1)}, u32[]{:S(2)}, u32[]{:S(2)}) collective-permute-start(bf16[4,1024]{1,0:T(4,128)(2,1)} %own.1), channel_id=1, source_target_pairs={{0,1},{1,0},{2,3},{3,2},{4,5},{5,4},{6,7},{7,6},{8,9},{9,8},{10,11... | collective-permute-start | bytes 24584 | tf_op jit(solution)/shard_map/ppermute | solution.py:484
  2.2 0.7 copy-start.5
  2.9 16.8 %collective-permute-start.1 = (bf16[8,1024]{1,0:T(8,128)(2,1)S(1)}, bf16[8,1024]{1,0:T(8,128)(2,1)S(1)}, u32[]{:S(2)}, u32[]{:S(2)}) collective-permute-start(bf16[8,1024]{1,0:T(8,128)(2,1)S(1)} %pack_pair.1.rest_0_), channel_id=1, source_target_pairs={{0,2},{1,3},{2,0},{3,1},{4,6},{5,7},{6,4},{7,5},{8,10},{9,11},{10,... | collective-permute-start | bytes 49160 | tf_op jit(solution)/shard_map/ppermute | solution.py:484
  5.8 13.9 %collective-permute-start.2 = (bf16[8,1024]{1,0:T(8,128)(2,1)S(1)}, bf16[8,1024]{1,0:T(8,128)(2,1)S(1)}, u32[]{:S(2)}, u32[]{:S(2)}) collective-permute-start(bf16[8,1024]{1,0:T(8,128)(2,1)S(1)} %pack_pair.1.rest_0_), channel_id=1, source_target_pairs={{0,4},{1,5},{2,6},{3,7},{4,0},{5,1},{6,2},{7,3},{8,12},{9,13},{10,... | collective-permute-start | bytes 49160 | tf_op jit(solution)/shard_map/ppermute | solution.py:484
  8.4 11.3 %collective-permute-start.3 = (bf16[8,1024]{1,0:T(8,128)(2,1)S(1)}, bf16[8,1024]{1,0:T(8,128)(2,1)S(1)}, u32[]{:S(2)}, u32[]{:S(2)}) collective-permute-start(bf16[8,1024]{1,0:T(8,128)(2,1)S(1)} %pack_pair.1.rest_0_), channel_id=1, source_target_pairs={{0,6},{1,7},{2,4},{3,5},{4,2},{5,3},{6,0},{7,1},{8,14},{9,15},{10,... | collective-permute-start | bytes 49160 | tf_op jit(solution)/shard_map/ppermute | solution.py:484
  8.4 1.6 %copy-start.6 = (bf16[1024,1024]{1,0:T(8,128)(2,1)S(1)}, bf16[1024,1024]{1,0:T(8,128)(2,1)}, u32[]{:S(2)}) copy-start(bf16[1024,1024]{1,0:T(8,128)(2,1)} %pixels_in.1) | copy-start | bytes 6291460
  10.0 1.2 %copy-start.7 = (bf16[64,64,64]{2,1,0:T(8,128)(2,1)S(1)}, bf16[64,64,64]{2,1,0:T(8,128)(2,1)}, u32[]{:S(2)}) copy-start(bf16[64,64,64]{2,1,0:T(8,128)(2,1)} %turns_in.1) | copy-start | bytes 1572868
  11.2 0.9 %copy-start.8 = (f32[32,1024]{1,0:T(8,128)S(1)}, f32[32,1024]{1,0:T(8,128)}, u32[]{:S(2)}) copy-start(f32[32,1024]{1,0:T(8,128)} %table_in.1) | copy-start | bytes 393220
  12.1 0.7 copy-start.9
  12.8 0.7 copy-start.10
  16.3 2.0 %copy-start = (bf16[1024,2048]{1,0:T(8,128)(2,1)}, bf16[1024,2048]{1,0:T(8,128)(2,1)S(1)}, u32[]{:S(2)}) copy-start(bf16[1024,2048]{1,0:T(8,128)(2,1)S(1)} %get-tuple-element.33.rest_1_) | copy-start | bytes 12582916
  18.3 1.4 %copy-start.2 = (bf16[4096,256]{1,0:T(8,128)(2,1)}, bf16[4096,256]{1,0:T(8,128)(2,1)S(1)}, u32[]{:S(2)}) copy-start(bf16[4096,256]{1,0:T(8,128)(2,1)S(1)} %get-tuple-element.32.matrix.rest_0_) | copy-start | bytes 6291460
  19.7 1.6 %copy-start.3 = (bf16[4096,256]{1,0:T(8,128)(2,1)S(1)}, bf16[4096,256]{1,0:T(8,128)(2,1)}, u32[]{:S(2)}) copy-start(bf16[4096,256]{1,0:T(8,128)(2,1)} %copy-done.2) | copy-start | bytes 6291460
  28.8 10.2 %collective-permute-start.10 = (f16[512,128]{1,0:T(8,128)(2,1)S(1)}, f16[512,128]{1,0:T(8,128)(2,1)S(1)}, u32[]{:S(2)}, u32[]{:S(2)}) collective-permute-start(f16[512,128]{1,0:T(8,128)(2,1)S(1)} %convert_element_type.42), channel_id=1, source_target_pairs={{0,8},{8,0},{16,24},{24,16},{1,9},{9,1},{17,25},{25,17},{2,10},{10... | collective-permute-start | bytes 393224 | tf_op jit(solution)/shard_map/ppermute | solution.py:484
  30.6 8.8 %collective-permute-start.11 = (f16[512,128]{1,0:T(8,128)(2,1)S(1)}, f16[512,128]{1,0:T(8,128)(2,1)S(1)}, u32[]{:S(2)}, u32[]{:S(2)}) collective-permute-start(f16[512,128]{1,0:T(8,128)(2,1)S(1)} %convert_element_type.44), channel_id=1, source_target_pairs={{0,16},{8,24},{16,0},{24,8},{1,17},{9,25},{17,1},{25,9},{2,18},{10... | collective-permute-start | bytes 393224 | tf_op jit(solution)/shard_map/ppermute | solution.py:484
  32.2 7.2 %collective-permute-start.12 = (f16[512,128]{1,0:T(8,128)(2,1)S(1)}, f16[512,128]{1,0:T(8,128)(2,1)S(1)}, u32[]{:S(2)}, u32[]{:S(2)}) collective-permute-start(f16[512,128]{1,0:T(8,128)(2,1)S(1)} %convert_element_type.46), channel_id=1, source_target_pairs={{0,24},{8,16},{16,8},{24,0},{1,25},{9,17},{17,9},{25,1},{2,26},{10... | collective-permute-start | bytes 393224 | tf_op jit(solution)/shard_map/ppermute | solution.py:484
  32.5 20.1 %copy-start.1 = (bf16[1024,2048]{1,0:T(8,128)(2,1)S(1)}, bf16[1024,2048]{1,0:T(8,128)(2,1)}, u32[]{:S(2)}) copy-start(bf16[1024,2048]{1,0:T(8,128)(2,1)} %copy-done) | copy-start | bytes 12582916
  35.6 17.0 %copy-start.4 = (bf16[4096,256]{1,0:T(8,128)(2,1)S(1)}, bf16[4096,256]{1,0:T(8,128)(2,1)}, u32[]{:S(2)}) copy-start(bf16[4096,256]{1,0:T(8,128)(2,1)} %copy-done.2) | copy-start | bytes 6291460
  35.6 7.3 %collective-permute-start.4 = (f16[512,128]{1,0:T(8,128)(2,1)S(1)}, f16[512,128]{1,0:T(8,128)(2,1)S(1)}, u32[]{:S(2)}, u32[]{:S(2)}) collective-permute-start(f16[512,128]{1,0:T(8,128)(2,1)S(1)} %convert_element_type.36), channel_id=1, source_target_pairs={{0,8},{8,0},{16,24},{24,16},{1,9},{9,1},{17,25},{25,17},{2,10},{10... | collective-permute-start | bytes 393224 | tf_op jit(solution)/shard_map/ppermute | solution.py:484
  37.4 9.4 %collective-permute-start.5 = (f16[512,128]{1,0:T(8,128)(2,1)S(1)}, f16[512,128]{1,0:T(8,128)(2,1)S(1)}, u32[]{:S(2)}, u32[]{:S(2)}) collective-permute-start(f16[512,128]{1,0:T(8,128)(2,1)S(1)} %convert_element_type.38), channel_id=1, source_target_pairs={{0,16},{8,24},{16,0},{24,8},{1,17},{9,25},{17,1},{25,9},{2,18},{10... | collective-permute-start | bytes 393224 | tf_op jit(solution)/shard_map/ppermute | solution.py:484
  39.1 7.8 %collective-permute-start.6 = (f16[512,128]{1,0:T(8,128)(2,1)S(1)}, f16[512,128]{1,0:T(8,128)(2,1)S(1)}, u32[]{:S(2)}, u32[]{:S(2)}) collective-permute-start(f16[512,128]{1,0:T(8,128)(2,1)S(1)} %convert_element_type.40), channel_id=1, source_target_pairs={{0,24},{8,16},{16,8},{24,0},{1,25},{9,17},{17,9},{25,1},{2,26},{10... | collective-permute-start | bytes 393224 | tf_op jit(solution)/shard_map/ppermute | solution.py:484
  39.6 9.4 %collective-permute-start.13 = (bf16[528,128]{1,0:T(8,128)(2,1)S(1)}, bf16[528,128]{1,0:T(8,128)(2,1)S(1)}, u32[]{:S(2)}, u32[]{:S(2)}) collective-permute-start(bf16[528,128]{1,0:T(8,128)(2,1)S(1)} %soften.3.rest_2_), channel_id=1, source_target_pairs={{0,8},{8,0},{16,24},{24,16},{1,9},{9,1},{17,25},{25,17},{2,10},{10... | collective-permute-start | bytes 405512 | tf_op jit(solution)/shard_map/ppermute | solution.py:484
  41.4 11.2 %collective-permute-start.14 = (bf16[528,128]{1,0:T(8,128)(2,1)S(1)}, bf16[528,128]{1,0:T(8,128)(2,1)S(1)}, u32[]{:S(2)}, u32[]{:S(2)}) collective-permute-start(bf16[528,128]{1,0:T(8,128)(2,1)S(1)} %soften.3.rest_2_), channel_id=1, source_target_pairs={{0,16},{8,24},{16,0},{24,8},{1,17},{9,25},{17,1},{25,9},{2,18},{10... | collective-permute-start | bytes 405512 | tf_op jit(solution)/shard_map/ppermute | solution.py:484
  42.9 9.7 %collective-permute-start.15 = (bf16[528,128]{1,0:T(8,128)(2,1)S(1)}, bf16[528,128]{1,0:T(8,128)(2,1)S(1)}, u32[]{:S(2)}, u32[]{:S(2)}) collective-permute-start(bf16[528,128]{1,0:T(8,128)(2,1)S(1)} %soften.3.rest_2_), channel_id=1, source_target_pairs={{0,24},{8,16},{16,8},{24,0},{1,25},{9,17},{17,9},{25,1},{2,26},{10... | collective-permute-start | bytes 405512 | tf_op jit(solution)/shard_map/ppermute | solution.py:484
  47.1 11.2 %collective-permute-start.7 = (bf16[528,128]{1,0:T(8,128)(2,1)S(1)}, bf16[528,128]{1,0:T(8,128)(2,1)S(1)}, u32[]{:S(2)}, u32[]{:S(2)}) collective-permute-start(bf16[528,128]{1,0:T(8,128)(2,1)S(1)} %soften.2.rest_2_), channel_id=1, source_target_pairs={{0,8},{8,0},{16,24},{24,16},{1,9},{9,1},{17,25},{25,17},{2,10},{10... | collective-permute-start | bytes 405512 | tf_op jit(solution)/shard_map/ppermute | solution.py:484
  47.9 10.4 %collective-permute-start.8 = (bf16[528,128]{1,0:T(8,128)(2,1)S(1)}, bf16[528,128]{1,0:T(8,128)(2,1)S(1)}, u32[]{:S(2)}, u32[]{:S(2)}) collective-permute-start(bf16[528,128]{1,0:T(8,128)(2,1)S(1)} %soften.2.rest_2_), channel_id=1, source_target_pairs={{0,16},{8,24},{16,0},{24,8},{1,17},{9,25},{17,1},{25,9},{2,18},{10... | collective-permute-start | bytes 405512 | tf_op jit(solution)/shard_map/ppermute | solution.py:484
  49.0 9.3 %collective-permute-start.9 = (bf16[528,128]{1,0:T(8,128)(2,1)S(1)}, bf16[528,128]{1,0:T(8,128)(2,1)S(1)}, u32[]{:S(2)}, u32[]{:S(2)}) collective-permute-start(bf16[528,128]{1,0:T(8,128)(2,1)S(1)} %soften.2.rest_2_), channel_id=1, source_target_pairs={{0,24},{8,16},{16,8},{24,0},{1,25},{9,17},{17,9},{25,1},{2,26},{10... | collective-permute-start | bytes 405512 | tf_op jit(solution)/shard_map/ppermute | solution.py:484
  64.3 1.3 %collective-permute-start.16 = (f32[32,1024]{1,0:T(8,128)S(1)}, f32[32,1024]{1,0:T(8,128)S(1)}, u32[]{:S(2)}, u32[]{:S(2)}) collective-permute-start(f32[32,1024]{1,0:T(8,128)S(1)} %get-tuple-element.49), channel_id=1, source_target_pairs={{0,1},{1,0},{2,3},{3,2},{4,5},{5,4},{6,7},{7,6},{8,9},{9,8},{10,11... | collective-permute-start | bytes 393224 | tf_op jit(solution)/shard_map/ppermute | solution.py:484
  65.7 4.5 %collective-permute-start.17 = (f32[8,1024]{1,0:T(8,128)S(1)}, f32[8,1024]{1,0:T(8,128)S(1)}, u32[]{:S(2)}, u32[]{:S(2)}) collective-permute-start(f32[8,1024]{1,0:T(8,128)S(1)} %get-tuple-element.51), channel_id=1, source_target_pairs={{0,2},{1,3},{2,0},{3,1},{4,6},{5,7},{6,4},{7,5},{8,10},{9,11},{10,... | collective-permute-start | bytes 98312 | tf_op jit(solution)/shard_map/ppermute | solution.py:484
  66.4 5.8 %collective-permute-start.18 = (f32[8,1024]{1,0:T(8,128)S(1)}, f32[8,1024]{1,0:T(8,128)S(1)}, u32[]{:S(2)}, u32[]{:S(2)}) collective-permute-start(f32[8,1024]{1,0:T(8,128)S(1)} %get-tuple-element.52), channel_id=1, source_target_pairs={{0,4},{1,5},{2,6},{3,7},{4,0},{5,1},{6,2},{7,3},{8,12},{9,13},{10,... | collective-permute-start | bytes 98312 | tf_op jit(solution)/shard_map/ppermute | solution.py:484
  69.9 5.7 %collective-permute-start.19 = (f32[8,1024]{1,0:T(8,128)S(1)}, f32[8,1024]{1,0:T(8,128)S(1)}, u32[]{:S(2)}, u32[]{:S(2)}) collective-permute-start(f32[8,1024]{1,0:T(8,128)S(1)} %get-tuple-element.53), channel_id=1, source_target_pairs={{0,6},{1,7},{2,4},{3,5},{4,2},{5,3},{6,0},{7,1},{8,14},{9,15},{10,... | collective-permute-start | bytes 98312 | tf_op jit(solution)/shard_map/ppermute | solution.py:484

commit v4 on v3

--- a/solution.py
+++ b/solution.py
@@ -13,6 +13,7 @@
 SMEM = pl.BlockSpec(memory_space=pltpu.SMEM)
 HBM = pl.BlockSpec(memory_space=pltpu.HBM)
 LANES, ROWS = 128, 8
+START_MIB = 16
 NN = (((1,), (0,)), ((), ()))
 NT = (((1,), (1,)), ((), ()))
 
@@ -36,6 +37,10 @@
     )
 
 
+def group_at(place, here):
+    return place ^ here[0]
+
+
 def block_spec(steps, shape, dim):
     if steps == 1:
         return VMEM
@@ -48,8 +53,8 @@
 
 
 def start_kernel(pack, pixels_in, turns_in, table_in, kind_in, names_in, *rest):
-    matrix, response, weighted, power_out, names = rest[:5]
-    pixels, turns, table, kind, done = rest[5:]
+    matrix, response_out, weighted, power_out, names = rest[:5]
+    pixels, turns, table, kind, response, done, sent = rest[5:]
     moves = [
         pltpu.make_async_copy(source, target, done.at[i])
         for i, (source, target) in enumerate(
@@ -76,7 +81,10 @@
         ],
         axis=0,
     )
-    for i in range(turn_count // pack):
+    steps = turn_count // pack
+    bands = math.gcd(steps, 4)
+    sends = []
+    for i in range(steps):
         wide = []
         for j in range(pack):
             turn = turns[i * pack + j]
@@ -90,6 +98,12 @@
                 response[i * kinds:(i + 1) * kinds, j * width + t * LANES:j * width + (t + 1) * LANES] = value[
                     t * kinds:(t + 1) * kinds, j * LANES:(j + 1) * LANES
                 ]
+        if (i + 1) % (steps // bands) == 0:
+            band = len(sends)
+            at = pl.ds(band * (steps // bands) * kinds, steps // bands * kinds)
+            send = pltpu.make_async_copy(response.at[at, :], response_out.at[at, :], sent.at[band])
+            send.start()
+            sends.append(send)
     for move in moves[2:]:
         move.wait()
     table3 = jnp.concatenate(split(table[...], 3), axis=0)
@@ -102,6 +116,8 @@
         factor = dot(hit[:, :3 * kinds], table3, NN)
         weighted[at, :width] = (pixels[at, :].astype(f32) * factor).astype(bf16)
         weighted[at, width:] = hit
+    for send in sends:
+        send.wait()
 
 
 def start(particles, turns, table, kind, names, pack):
@@ -112,7 +128,7 @@
     return pl.pallas_call(
         functools.partial(start_kernel, pack),
         in_specs=[HBM] * 5,
-        out_specs=[VMEM] * 5,
+        out_specs=[VMEM, HBM, VMEM, VMEM, VMEM],
         out_shape=[
             jax.ShapeDtypeStruct((steps * LANES, pack * LANES), bf16),
             jax.ShapeDtypeStruct((steps * kinds, pack * pixels), bf16),
@@ -125,28 +141,32 @@
             pltpu.VMEM(turns.shape, bf16),
             pltpu.VMEM(table.shape, f32),
             pltpu.VMEM(kind.shape, jnp.int32),
+            pltpu.VMEM((steps * kinds, pack * pixels), bf16),
             pltpu.SemaphoreType.DMA((5,)),
+            pltpu.SemaphoreType.DMA((4,)),
         ],
         name="start",
-        **limits(12, 8 * steps * kinds * pack * pixels * LANES, 4 * count * pixels),
+        **limits(START_MIB, 1000000, 0),
     )(particles, turns, table, kind, names)
 
 
-def pack_kernel(own, other, out):
-    rows = own.shape[0]
-    out[:rows, :] = own[...]
-    out[rows:, :] = other[...]
-
-
-def pack_pair(own, other):
-    return pl.pallas_call(
-        pack_kernel,
-        in_specs=[VMEM, VMEM],
+def stack_kernel(*refs):
+    out = refs[-1]
+    rows = refs[0].shape[0]
+    for i, ref in enumerate(refs[:-1]):
+        out[i * rows:(i + 1) * rows, :] = ref[...]
+
+
+def stack(blocks):
+    rows, columns = blocks[0].shape
+    return pl.pallas_call(
+        stack_kernel,
+        in_specs=[VMEM] * len(blocks),
         out_specs=VMEM,
-        out_shape=jax.ShapeDtypeStruct((2 * own.shape[0], own.shape[1]), own.dtype),
-        name="pack_pair",
-        **limits(4, 0, 4 * own.size),
-    )(own, other)
+        out_shape=jax.ShapeDtypeStruct((len(blocks) * rows, columns), blocks[0].dtype),
+        name="stack",
+        **limits(4, 20_000_000_000, 1 << 25),
+    )(*blocks)
 
 
 def rotate_kernel(groups, turn_count, power2, matrix, *rest):
@@ -157,10 +177,10 @@
     cpg = ROWS // pack
     tiles = pixels // LANES
     group_pairs = cpg * turn_count
+    source = [block[...].astype(f32) for block in refs]
     if len(refs) > 1:
-        source = jnp.concatenate([block[...].astype(f32) for block in refs], axis=0)
-    else:
-        source = refs[0][...].astype(f32)
+        source = [part[i * cpg:(i + 1) * cpg, :] for i in range(groups // len(refs)) for part in source]
+    source = jnp.concatenate(source, axis=0)
     line = lax.broadcasted_iota(jnp.int32, (ROWS, pixels), 0) // cpg
     copies = []
     for i in range(groups // pack):
@@ -250,7 +270,7 @@
         pix = weighted[at, :]
         for g in range(groups):
             value = scale * dot(rotated[g * pairs:(g + 1) * pairs, :], pix, NT)
-            group = (step * groups + g) ^ here[0]
+            group = group_at(step * groups + g, here)
             for k in range(2):
                 rows = slice(k * pairs, (k + 1) * pairs)
                 hit = names[k:k + 1, at] == group
@@ -318,22 +338,24 @@
     )(scores, mean)
 
 
-def collect_kernel(groups, parts, turn_count, kinds, scale, begin, peers, more, me, here, names, weighted, *rest):
-    matrix, response = rest[:2]
-    blocks = rest[2:2 + peers]
-    before = rest[2 + peers:2 + peers + (parts + 1) * more]
-    sums = rest[2 + peers + (parts + 1) * more:][:parts]
-    logs, weights, lhs, by_kind = rest[-4:]
+def collect_kernel(groups, parts, turn_count, kinds, scale, begin, peers, first, last, me, here, names, weighted, *rest):
+    rest = list(rest)
+    take = lambda n: [rest.pop(0) for _ in range(n)]
+    matrix, response = take(2) if last else (None, None)
+    blocks = take(peers)
+    before = None if first else take(3)
+    sums = take(parts) if last else None
+    logs, weights, lhs, by_kind = rest if last else [rest[i] for i in (2, 3, 0, 1)]
     step = pl.program_id(0)
     pixels = weighted.shape[1] - LANES
     share = blocks[0].shape[1]
     count = share * peers
     rows = weights.shape[0]
     pairs = rows // 2
-    pack = matrix.shape[1] // LANES
+    turns = lhs.shape[1] // LANES
+    pack = turn_count // turns
     cpg = ROWS // pack
     tiles = pixels // LANES
-    turns = turn_count // pack
     own = slice(begin, begin + count)
 
     @pl.when(step == 0)
@@ -346,39 +368,48 @@
             logs[0:1, pl.ds(begin + start, share)] = tail[0:1] + tail[1:2] + tail[2:3]
             center = center + (tail[3:4] + tail[4:5] + tail[5:6])
         line = lax.broadcasted_iota(jnp.int32, (2 * ROWS, LANES), 0)
-        first = lax.broadcasted_iota(jnp.int32, (2 * ROWS, LANES), 1) < kinds
-        stack = jnp.zeros((2 * ROWS, LANES), f32)
+        inside = lax.broadcasted_iota(jnp.int32, (2 * ROWS, LANES), 1) < kinds
+        stacked = jnp.zeros((2 * ROWS, LANES), f32)
         for i, part in enumerate(split(center[:, :LANES], 3)):
-            stack = jnp.where((line == i) & first, part.astype(f32), stack)
-        moved = dot(stack.astype(bf16), weighted[own, pixels:], NT)
+            stacked = jnp.where((line == i) & inside, part.astype(f32), stacked)
+        moved = dot(stacked.astype(bf16), weighted[own, pixels:], NT)
         logs[:, own] = logs[:, own] + scale * jnp.sum(moved, axis=0, keepdims=True)
-        if more:
-            logs[:, :begin] = before[-1][:, :begin]
+        if not first:
+            logs[:, :begin] = before[2][:, :begin]
 
     zero = jnp.zeros((), bf16)
     for g in range(0, groups, 2):
         dense = []
         for q in range(2):
-            group = (step * groups + g + q) ^ here[0]
+            group = group_at(step * groups + g + q, here)
             dense.append(
                 jnp.where(names[0:1, own] == group, weights[:pairs, :], zero)
                 + jnp.where(names[1:2, own] == group, weights[pairs:, :], zero)
             )
         value = dot(jnp.concatenate(dense, axis=0), weighted[own, :], NN)
         for i in range(turns):
+            lanes = slice(i * LANES, (i + 1) * LANES)
             for t in range(tiles):
                 pair = [
                     value[q * pairs + i * ROWS:q * pairs + (i + 1) * ROWS, t * LANES:(t + 1) * LANES]
                     for q in range(2)
                 ]
-                at = (t * groups + g) * ROWS
-                lhs[at:at + 2 * ROWS, i * LANES:(i + 1) * LANES] = jnp.concatenate(pair, axis=0).astype(bf16)
+                pair = jnp.concatenate(pair, axis=0)
+                at = slice((t * groups + g) * ROWS, (t * groups + g + 2) * ROWS)
+                if not first:
+                    pair = pair + before[0][at, lanes]
+                lhs[at, lanes] = pair.astype(lhs.dtype)
             for q in range(2):
                 by_kind[(g + q) * ROWS:(g + q + 1) * ROWS, i * kinds:(i + 1) * kinds] = value[
                     q * pairs + i * ROWS:q * pairs + (i + 1) * ROWS, pixels:pixels + kinds
                 ]
+    if not last:
+        if not first:
+            by_kind[...] = by_kind[...] + before[1][...]
+        return
     total = dot(lhs[...], matrix[...], NN)
-    heavy = dot(jnp.concatenate(split(by_kind[...], 2), axis=0), response[...], NN)
+    light = by_kind[...] if first else by_kind[...] + before[1][...]
+    heavy = dot(jnp.concatenate(split(light, 2), axis=0), response[...], NN)
     heavy = heavy[:groups * ROWS] + heavy[groups * ROWS:]
     upper = lax.broadcasted_iota(jnp.int32, (ROWS, LANES), 0) < cpg
 
@@ -389,7 +420,7 @@
         return out
 
     for g in range(groups):
-        to = slice(g // parts * ROWS, (g // parts + 1) * ROWS)
+        part, to = g % parts, slice(g // parts * ROWS, (g // parts + 1) * ROWS)
         for t in range(tiles):
             lanes = slice(t * LANES, (t + 1) * LANES)
             at = slice((t * groups + g) * ROWS, (t * groups + g + 1) * ROWS)
@@ -398,15 +429,12 @@
             low = fold(
                 [heavy[at, j * pixels + t * LANES:j * pixels + (t + 1) * LANES] for j in range(pack)]
             )
-            value = jnp.where(upper, top, pltpu.roll(low, cpg, 0))
-            if more:
-                value = value + before[g % parts][to, lanes]
-            sums[g % parts][to, lanes] = value
+            sums[part][to, lanes] = jnp.where(upper, top, pltpu.roll(low, cpg, 0))
 
 
 def collect(
-    begin, blocks, before, names, weighted, matrix, response, me, here, parts, turn_count, kinds, group_pairs, groups,
-    groups_all, scale
+    begin, blocks, before, last, names, weighted, matrix, response, me, here, parts, turn_count, kinds, group_pairs,
+    groups, groups_all, scale
 ):
     count, width = weighted.shape
     pixels = width - LANES
@@ -414,30 +442,39 @@
     steps = groups_all // groups
     turns = matrix.shape[0] // LANES
     rows = groups * ROWS // parts
-    sums_spec = [block_spec(steps, (rows, pixels), 0)] * parts
+    first = not before
+    left = (pixels // LANES * groups * ROWS, turns * LANES)
+    light = (groups * ROWS, turns * kinds)
+    logs_spec = same_spec(steps, (1, count))
+    logs_shape = jax.ShapeDtypeStruct((1, count), f32)
+    sides = [block_spec(steps, left, 0), block_spec(steps, light, 0)]
+    weights_scratch = pltpu.VMEM((2 * group_pairs, peers * blocks[0].shape[1]), bf16)
+    if last:
+        out_specs = [block_spec(steps, (rows, pixels), 0)] * parts + [logs_spec]
+        out_shape = [jax.ShapeDtypeStruct((steps * rows, pixels), f32)] * parts + [logs_shape]
+        scratch = [weights_scratch, pltpu.VMEM(left, bf16), pltpu.VMEM(light, f32)]
+    else:
+        out_specs = sides + [logs_spec]
+        out_shape = [jax.ShapeDtypeStruct((steps * shape[0], shape[1]), f32) for shape in (left, light)] + [logs_shape]
+        scratch = [weights_scratch]
+    both = [names, weighted] + ([matrix, response] if last else []) + blocks
     return pl.pallas_call(
         functools.partial(
-            collect_kernel, groups, parts, turn_count, kinds, scale, begin, peers, 1 if before else 0
+            collect_kernel, groups, parts, turn_count, kinds, scale, begin, peers, first, last
         ),
         grid=(steps,),
         in_specs=[SMEM, SMEM]
-        + [same_spec(steps, a.shape) for a in (names, weighted, matrix, response)]
-        + [same_spec(steps, b.shape) for b in blocks]
-        + (sums_spec + [same_spec(steps, (1, count))] if before else []),
-        out_specs=sums_spec + [same_spec(steps, (1, count))],
-        out_shape=[jax.ShapeDtypeStruct((steps * rows, pixels), f32)] * parts
-        + [jax.ShapeDtypeStruct((1, count), f32)],
-        scratch_shapes=[
-            pltpu.VMEM((2 * group_pairs, peers * blocks[0].shape[1]), bf16),
-            pltpu.VMEM((pixels // LANES * groups * ROWS, turns * LANES), bf16),
-            pltpu.VMEM((groups * ROWS, turns * kinds), f32),
-        ],
+        + [same_spec(steps, a.shape) for a in both]
+        + ([] if first else sides + [logs_spec]),
+        out_specs=out_specs,
+        out_shape=out_shape,
+        scratch_shapes=scratch,
         name="collect",
         **limits(
-            20 if steps == 1 else 40, 2 * groups_all * group_pairs * width * peers * blocks[0].shape[1],
+            20 if steps == 1 else 56, 2 * groups_all * group_pairs * width * peers * blocks[0].shape[1],
             4 * count * pixels
         ),
-    )(me, here, names, weighted, matrix, response, *blocks, *before)
+    )(me, here, *both, *before)
 
 
 def add_kernel(left, right, *outs):
@@ -497,12 +534,11 @@
     kinds = ctf_table.shape[0]
     scale = 4.0 / math.sqrt(pixels * peers)
     me = lax.axis_index("cls").astype(jnp.int32).reshape(1)
-    here = lax.axis_index("dom").astype(jnp.int32).reshape(1)
+    here = (lax.axis_index("dom") if paired else jnp.int32(0)).astype(jnp.int32).reshape(1)
     if paired:
-        pair = pack_pair(references, swap(references, "dom", 1))
-        refs = [pair] + [swap(pair, "dom", 2 * k) for k in range(1, owners // 2)]
+        half = stack([references] + [swap(references, "dom", 2 * k) for k in range(1, owners // 2)])
+        refs = [half, swap(half, "dom", 1)]
     else:
-        here = jnp.zeros_like(here)
         refs = [lax.all_gather(references, "dom", axis=0, tiled=True)]
     matrix, response, weighted, power2, names = start(
         particles, rotations, ctf_table, defocus.reshape(1, count), candidates.T, pack
@@ -522,8 +558,8 @@
     out = []
     for c in range(chunks):
         out = collect(
-            c * size, blocks[c], out, names, weighted, matrix, response, me, here, parts, turn_count, kinds,
-            group_pairs, groups, owners, scale
+            c * size, blocks[c], out, c == chunks - 1, names, weighted, matrix, response, me, here, parts, turn_count,
+            kinds, group_pairs, groups, owners, scale
         )
     if paired:
         pieces = add_cut(out[0], swap(out[1], "dom", 1), owners // 2)

time: 76.6 us -> 67 us (0.87)
  local copies, waits for them, and re-layouts: 10.7 us -> 0.72 us
  waiting for transfers between devices: 12 us -> 13.7 us
    unnamed x22 -> x12, local copies, waits for them, and re-layouts: 10.7 us -> 0.72 us
    pallas_call x2, Pallas kernels: 11.6 us -> 9.45 us  [collect(): pl.pallas_call(functools.partial(collect_kernel, groups, parts, turn_coun...]
    ppermute x20, waiting for transfers between devices: 12 us -> 13.7 us  [swap(): lax.ppermute(x, axis, [(i, i ^ k) for i in range(lax.axis_size(axis))])]
    pallas_call x1, Pallas kernels: 2.8 us -> 4.04 us  [start(): pl.pallas_call(functools.partial(start_kernel, pack), in_specs=[HBM] * 5,...]
  transfers between devices with their start and end apart: 20 -> 20, of which waited for: 6 -> 8; matrix products, arithmetic and copies ran while one was open for 0% -> 0% of each run, Pallas kernels for 15% -> 16%
where the time goes in v4:
time: 67 us; the launch traced here: 66.8 us
  starting transfers between devices  26.1 us (39%)
  Pallas kernels  25.2 us (38%)
  waiting for transfers between devices  13.7 us (20%)
  between operations  0.88 us (1%)
  local copies, waits for them, and re-layouts  0.72 us (1%)
    ppermute x20, starting transfers between devices, swap(): lax.ppermute(x, axis, [(i, i ^ k) for i in range(lax.axis_size(axis))])  26.1 us
    ppermute x20, waiting for transfers between devices, swap(): lax.ppermute(x, axis, [(i, i ^ k) for i in range(lax.axis_size(axis))])  13.7 us
    pallas_call x2, Pallas kernels, collect(): pl.pallas_call(functools.partial(collect_kernel, groups, parts, turn_coun...  9.45 us
    pallas_call x2, Pallas kernels, score(): pl.pallas_call(functools.partial(score_kernel, groups, scale, begin), gri...  6.25 us
    pallas_call x1, Pallas kernels, rotate(): pl.pallas_call(functools.partial(rotate_kernel, groups, turn_count), grid...  4.51 us
    pallas_call x1, Pallas kernels, start(): pl.pallas_call(functools.partial(start_kernel, pack), in_specs=[HBM] * 5,...  4.04 us
  transfers between devices with their start and end apart: 20, of which 8 were waited for; matrix products, arithmetic and copies ran while one was open for 0% of the time, Pallas kernels for 16%

profile of v4, /device:TPU:0, one launch (start us, length us, event | category | flops | bytes accessed | tf_op | source)
XLA Modules:
  0.0 66.8 jit_solution(18148650551908240466)
XLA Ops:
  0.7 4.1 %collective-permute-start.1 = (bf16[4,1024]{1,0:T(4,128)(2,1)}, bf16[4,1024]{1,0:T(4,128)(2,1)S(1)}, u32[]{:S(2)}, u32[]{:S(2)}) collective-permute-start(bf16[4,1024]{1,0:T(4,128)(2,1)} %refs_0_.1), channel_id=1, source_target_pairs={{0,4},{1,5},{2,6},{3,7},{4,0},{5,1},{6,2},{7,3},{8,12},{9,13},{10,... | collective-permute-start | bytes 24584 | tf_op jit(solution)/shard_map/ppermute | solution.py:521
  4.8 1.6 %collective-permute-start = (bf16[4,1024]{1,0:T(4,128)(2,1)}, bf16[4,1024]{1,0:T(4,128)(2,1)S(1)}, u32[]{:S(2)}, u32[]{:S(2)}) collective-permute-start(bf16[4,1024]{1,0:T(4,128)(2,1)} %refs_0_.1), channel_id=1, source_target_pairs={{0,2},{1,3},{2,0},{3,1},{4,6},{5,7},{6,4},{7,5},{8,10},{9,11},{10,... | collective-permute-start | bytes 24584 | tf_op jit(solution)/shard_map/ppermute | solution.py:521
  6.4 0.3 collective-permute-done.1.refs_2_
  6.6 2.0 %collective-permute-done.refs_1_ = bf16[4,1024]{1,0:T(4,128)(2,1)S(1)} collective-permute-done((bf16[4,1024]{1,0:T(4,128)(2,1)}, bf16[4,1024]{1,0:T(4,128)(2,1)S(1)}, u32[]{:S(2)}, u32[]{:S(2)}) %collective-permute-start) | collective-permute-done | bytes 8224 | tf_op jit(solution)/shard_map/ppermute | solution.py:521
  8.6 3.4 %collective-permute-done.2.refs_3_ = bf16[4,1024]{1,0:T(4,128)(2,1)S(1)} collective-permute-done((bf16[4,1024]{1,0:T(4,128)(2,1)}, bf16[4,1024]{1,0:T(4,128)(2,1)S(1)}, u32[]{:S(2)}, u32[]{:S(2)}) %collective-permute-start.2) | collective-permute-done | bytes 8224 | tf_op jit(solution)/shard_map/ppermute | solution.py:521
  12.0 0.7 %copy-done.5 = bf16[4,1024]{1,0:T(4,128)(2,1)S(1)} copy-done((bf16[4,1024]{1,0:T(4,128)(2,1)S(1)}, bf16[4,1024]{1,0:T(4,128)(2,1)}, u32[]{:S(2)}) %copy-start.5) | copy-done | bytes 8216
  12.9 4.0 %start.1 = (bf16[4096,256]{1,0:T(8,128)(2,1)S(1)}, bf16[1024,2048]{1,0:T(8,128)(2,1)S(1)}, bf16[1024,1152]{1,0:T(8,128)(2,1)S(1)}, bf16[64,1024]{1,0:T(8,128)(2,1)S(1)}, s32[2,1024]{1,0:T(2,128)S(1)}) custom-call(bf16[1024,1024]{1,0:T(8,128)(2,1)S(1)} %copy-done, bf16[64,64,64]{2,1,0:T(8,128)(2,1)S(1)} %copy-done.1, f32[32,1024]{1,0:T(8,128)S(1)} %copy-done.2, ...), custom_call_target="tpu_custom_call" | custom-call | flops 1000000 | tf_op jit(solution)/shard_map/start/pallas_call | solution.py:128
  16.9 4.5 %rotate.1 = (bf16[2048,1152]{1,0:T(8,128)(2,1)S(1)}, f32[1,128]{1,0:T(1,128)S(1)}) custom-call(bf16[64,1024]{1,0:T(8,128)(2,1)S(1)} %get-tuple-element.34.power2, bf16[4096,256]{1,0:T(8,128)(2,1)S(1)} %get-tuple-element.32.matrix.rest_0_, bf16[16,1024]{1,0:T(8,128)(2,1)S(1)} %stack.1.rest_0_, bf16[16,1024]{1,0:T(8,128)(2,1)S(1)} %collective-permute-done.3.rest_1_), custom_call_target="tpu_custom_call" | custom-call | flops 1073741824 | bytes 4194304 | tf_op jit(solution)/shard_map/rotate/pallas_call | solution.py:245
  21.4 3.1 %score.3 = (f32[512,128]{1,0:T(8,128)S(1)}, f32[512,128]{1,0:T(8,128)S(1)}, f32[512,128]{1,0:T(8,128)S(1)}, f32[512,128]{1,0:T(8,128)S(1)}) custom-call(s32[1]{0:T(128)} %bitcast.me, s32[1]{0:T(128)} %bitcast.1.here, bf16[1024,1152]{1,0:T(8,128)(2,1)S(1)} %get-tuple-element.31.weighted, s32[2,1024]{1,0:T(2,128)S(1)} %get-tuple-element.30.names, ...), custom_call_target="tpu_custom_call" | custom-call | flops 2415919104 | bytes 4718592 | tf_op jit(solution)/shard_map/score/pallas_call | solution.py:294
  24.7 2.5 %collective-permute-start.12 = (f16[512,128]{1,0:T(8,128)(2,1)S(1)}, f16[512,128]{1,0:T(8,128)(2,1)S(1)}, u32[]{:S(2)}, u32[]{:S(2)}) collective-permute-start(f16[512,128]{1,0:T(8,128)(2,1)S(1)} %convert_element_type.46), channel_id=1, source_target_pairs={{0,24},{8,16},{16,8},{24,0},{1,25},{9,17},{17,9},{25,1},{2,26},{10... | collective-permute-start | bytes 393224 | tf_op jit(solution)/shard_map/ppermute | solution.py:521
  27.2 0.5 collective-permute-start.11
  27.7 0.5 collective-permute-start.10
  28.2 3.1 %score.2 = (f32[512,128]{1,0:T(8,128)S(1)}, f32[512,128]{1,0:T(8,128)S(1)}, f32[512,128]{1,0:T(8,128)S(1)}, f32[512,128]{1,0:T(8,128)S(1)}) custom-call(s32[1]{0:T(128)} %bitcast.me, s32[1]{0:T(128)} %bitcast.1.here, bf16[1024,1152]{1,0:T(8,128)(2,1)S(1)} %get-tuple-element.31.weighted, s32[2,1024]{1,0:T(2,128)S(1)} %get-tuple-element.30.names, ...), custom_call_target="tpu_custom_call" | custom-call | flops 2415919104 | bytes 4718592 | tf_op jit(solution)/shard_map/score/pallas_call | solution.py:294
  31.4 2.5 %collective-permute-start.6 = (f16[512,128]{1,0:T(8,128)(2,1)S(1)}, f16[512,128]{1,0:T(8,128)(2,1)S(1)}, u32[]{:S(2)}, u32[]{:S(2)}) collective-permute-start(f16[512,128]{1,0:T(8,128)(2,1)S(1)} %convert_element_type.40), channel_id=1, source_target_pairs={{0,24},{8,16},{16,8},{24,0},{1,25},{9,17},{17,9},{25,1},{2,26},{10... | collective-permute-start | bytes 393224 | tf_op jit(solution)/shard_map/ppermute | solution.py:521
  33.9 0.5 collective-permute-start.5
  34.5 0.5 collective-permute-start.4
  35.2 2.5 %collective-permute-start.15 = (bf16[528,128]{1,0:T(8,128)(2,1)S(1)}, bf16[528,128]{1,0:T(8,128)(2,1)S(1)}, u32[]{:S(2)}, u32[]{:S(2)}) collective-permute-start(bf16[528,128]{1,0:T(8,128)(2,1)S(1)} %soften.3.rest_0_), channel_id=1, source_target_pairs={{0,24},{8,16},{16,8},{24,0},{1,25},{9,17},{17,9},{25,1},{2,26},{10... | collective-permute-start | bytes 405512 | tf_op jit(solution)/shard_map/ppermute | solution.py:521
  37.7 0.5 collective-permute-start.14
  38.2 2.0 %collective-permute-start.13 = (bf16[528,128]{1,0:T(8,128)(2,1)S(1)}, bf16[528,128]{1,0:T(8,128)(2,1)S(1)}, u32[]{:S(2)}, u32[]{:S(2)}) collective-permute-start(bf16[528,128]{1,0:T(8,128)(2,1)S(1)} %soften.3.rest_0_), channel_id=1, source_target_pairs={{0,8},{8,0},{16,24},{24,16},{1,9},{9,1},{17,25},{25,17},{2,10},{10... | collective-permute-start | bytes 405512 | tf_op jit(solution)/shard_map/ppermute | solution.py:521
  40.2 1.7 %collective-permute-done.5 = f16[512,128]{1,0:T(8,128)(2,1)S(1)} collective-permute-done((f16[512,128]{1,0:T(8,128)(2,1)S(1)}, f16[512,128]{1,0:T(8,128)(2,1)S(1)}, u32[]{:S(2)}, u32[]{:S(2)}) %collective-permute-start.5) | collective-permute-done | bytes 131104 | tf_op jit(solution)/shard_map/ppermute | solution.py:521
  42.1 2.6 %collective-permute-start.9 = (bf16[528,128]{1,0:T(8,128)(2,1)S(1)}, bf16[528,128]{1,0:T(8,128)(2,1)S(1)}, u32[]{:S(2)}, u32[]{:S(2)}) collective-permute-start(bf16[528,128]{1,0:T(8,128)(2,1)S(1)} %soften.2.rest_2_), channel_id=1, source_target_pairs={{0,24},{8,16},{16,8},{24,0},{1,25},{9,17},{17,9},{25,1},{2,26},{10... | collective-permute-start | bytes 405512 | tf_op jit(solution)/shard_map/ppermute | solution.py:521
  44.8 0.7 %collective-permute-start.8 = (bf16[528,128]{1,0:T(8,128)(2,1)S(1)}, bf16[528,128]{1,0:T(8,128)(2,1)S(1)}, u32[]{:S(2)}, u32[]{:S(2)}) collective-permute-start(bf16[528,128]{1,0:T(8,128)(2,1)S(1)} %soften.2.rest_2_), channel_id=1, source_target_pairs={{0,16},{8,24},{16,0},{24,8},{1,17},{9,25},{17,1},{25,9},{2,18},{10... | collective-permute-start | bytes 405512 | tf_op jit(solution)/shard_map/ppermute | solution.py:521
  45.5 0.5 collective-permute-start.7
  45.9 2.7 %collective-permute-done.14.rest_2_ = bf16[528,128]{1,0:T(8,128)(2,1)S(1)} collective-permute-done((bf16[528,128]{1,0:T(8,128)(2,1)S(1)}, bf16[528,128]{1,0:T(8,128)(2,1)S(1)}, u32[]{:S(2)}, u32[]{:S(2)}) %collective-permute-start.14) | collective-permute-done | bytes 135200 | tf_op jit(solution)/shard_map/ppermute | solution.py:521
  48.6 3.3 %collect.2 = (f32[512,4096]{1,0:T(8,128)S(1)}, f32[64,1024]{1,0:T(8,128)S(1)}, f32[1,1024]{1,0:T(1,128)S(1)}) custom-call(s32[1]{0:T(128)} %bitcast.me, s32[1]{0:T(128)} %bitcast.1.here, s32[2,1024]{1,0:T(2,128)S(1)} %get-tuple-element.30.names, bf16[1024,1152]{1,0:T(8,128)(2,1)S(1)} %get-tuple-element.31.weighted, bf16[528,128]{1,0:T(8,128)(2,1)S(1)} %soften.3.rest_0_, ...), custom_call_target="tpu_custom_call" | custom-call | flops 2415919104 | bytes 4194304 | tf_op jit(solution)/shard_map/collect/pallas_call | solution.py:461
  52.0 6.1 %collect.3 = (f32[32,1024]{1,0:T(8,128)S(1)}, f32[32,1024]{1,0:T(8,128)S(1)}, f32[1,1024]{1,0:T(1,128)}) custom-call(s32[1]{0:T(128)} %bitcast.me, s32[1]{0:T(128)} %bitcast.1.here, s32[2,1024]{1,0:T(2,128)S(1)} %get-tuple-element.30.names, bf16[1024,1152]{1,0:T(8,128)(2,1)S(1)} %get-tuple-element.31.weighted, ...), custom_call_target="tpu_custom_call" | custom-call | flops 2415919104 | bytes 4194304 | tf_op jit(solution)/shard_map/collect/pallas_call | solution.py:461
  58.1 1.3 %collective-permute-done.16.right = f32[32,1024]{1,0:T(8,128)S(1)} collective-permute-done((f32[32,1024]{1,0:T(8,128)S(1)}, f32[32,1024]{1,0:T(8,128)S(1)}, u32[]{:S(2)}, u32[]{:S(2)}) %collective-permute-start.16) | collective-permute-done | bytes 131104 | tf_op jit(solution)/shard_map/ppermute | solution.py:521
  59.6 0.7 %collective-permute-start.18 = (f32[8,1024]{1,0:T(8,128)S(1)}, f32[8,1024]{1,0:T(8,128)S(1)}, u32[]{:S(2)}, u32[]{:S(2)}) collective-permute-start(f32[8,1024]{1,0:T(8,128)S(1)} %get-tuple-element.52), channel_id=1, source_target_pairs={{0,4},{1,5},{2,6},{3,7},{4,0},{5,1},{6,2},{7,3},{8,12},{9,13},{10,... | collective-permute-start | bytes 98312 | tf_op jit(solution)/shard_map/ppermute | solution.py:521
  60.3 3.7 %collective-permute-start.19 = (f32[8,1024]{1,0:T(8,128)S(1)}, f32[8,1024]{1,0:T(8,128)S(1)}, u32[]{:S(2)}, u32[]{:S(2)}) collective-permute-start(f32[8,1024]{1,0:T(8,128)S(1)} %get-tuple-element.53), channel_id=1, source_target_pairs={{0,6},{1,7},{2,4},{3,5},{4,2},{5,3},{6,0},{7,1},{8,14},{9,15},{10,... | collective-permute-start | bytes 98312 | tf_op jit(solution)/shard_map/ppermute | solution.py:521
  63.9 0.5 collective-permute-done.18.refs_2_
  64.5 1.7 %collective-permute-done.19.refs_3_ = f32[8,1024]{1,0:T(8,128)S(1)} collective-permute-done((f32[8,1024]{1,0:T(8,128)S(1)}, f32[8,1024]{1,0:T(8,128)S(1)}, u32[]{:S(2)}, u32[]{:S(2)}) %collective-permute-start.19) | collective-permute-done | bytes 32800 | tf_op jit(solution)/shard_map/ppermute | solution.py:521
  66.2 0.6 finish.1
  (39 shorter events, 0.8 us)
Async XLA Ops:
  0.6 12.2 %copy-start.1 = (bf16[64,64,64]{2,1,0:T(8,128)(2,1)S(1)}, bf16[64,64,64]{2,1,0:T(8,128)(2,1)}, u32[]{:S(2)}) copy-start(bf16[64,64,64]{2,1,0:T(8,128)(2,1)} %turns_in.1) | copy-start | bytes 1572868
  0.6 12.2 %copy-start.2 = (f32[32,1024]{1,0:T(8,128)S(1)}, f32[32,1024]{1,0:T(8,128)}, u32[]{:S(2)}) copy-start(f32[32,1024]{1,0:T(8,128)} %table_in.1) | copy-start | bytes 393220
  0.7 12.2 %copy-start.4 = (s32[1024]{0:T(1024)S(1)}, s32[1024]{0:T(1024)}, u32[]{:S(2)}) copy-start(s32[1024]{0:T(1024)} %param.8) | copy-start | bytes 12292
  0.7 12.2 %copy-start.3 = (s32[1024,2]{0,1:T(2,128)S(1)}, s32[1024,2]{0,1:T(2,128)}, u32[]{:S(2)}) copy-start(s32[1024,2]{0,1:T(2,128)} %param.7) | copy-start | bytes 24580
  0.7 12.2 %copy-start = (bf16[1024,1024]{1,0:T(8,128)(2,1)S(1)}, bf16[1024,1024]{1,0:T(8,128)(2,1)}, u32[]{:S(2)}) copy-start(bf16[1024,1024]{1,0:T(8,128)(2,1)} %pixels_in.1) | copy-start | bytes 6291460
  0.7 5.9 %collective-permute-start.1 = (bf16[4,1024]{1,0:T(4,128)(2,1)}, bf16[4,1024]{1,0:T(4,128)(2,1)S(1)}, u32[]{:S(2)}, u32[]{:S(2)}) collective-permute-start(bf16[4,1024]{1,0:T(4,128)(2,1)} %refs_0_.1), channel_id=1, source_target_pairs={{0,4},{1,5},{2,6},{3,7},{4,0},{5,1},{6,2},{7,3},{8,12},{9,13},{10,... | collective-permute-start | bytes 24584 | tf_op jit(solution)/shard_map/ppermute | solution.py:521
  4.8 3.9 %collective-permute-start = (bf16[4,1024]{1,0:T(4,128)(2,1)}, bf16[4,1024]{1,0:T(4,128)(2,1)S(1)}, u32[]{:S(2)}, u32[]{:S(2)}) collective-permute-start(bf16[4,1024]{1,0:T(4,128)(2,1)} %refs_0_.1), channel_id=1, source_target_pairs={{0,2},{1,3},{2,0},{3,1},{4,6},{5,7},{6,4},{7,5},{8,10},{9,11},{10,... | collective-permute-start | bytes 24584 | tf_op jit(solution)/shard_map/ppermute | solution.py:521
  6.4 5.7 %collective-permute-start.2 = (bf16[4,1024]{1,0:T(4,128)(2,1)}, bf16[4,1024]{1,0:T(4,128)(2,1)S(1)}, u32[]{:S(2)}, u32[]{:S(2)}) collective-permute-start(bf16[4,1024]{1,0:T(4,128)(2,1)} %refs_0_.1), channel_id=1, source_target_pairs={{0,6},{1,7},{2,4},{3,5},{4,2},{5,3},{6,0},{7,1},{8,14},{9,15},{10,... | collective-permute-start | bytes 24584 | tf_op jit(solution)/shard_map/ppermute | solution.py:521
  12.0 0.7 %copy-start.5 = (bf16[4,1024]{1,0:T(4,128)(2,1)S(1)}, bf16[4,1024]{1,0:T(4,128)(2,1)}, u32[]{:S(2)}) copy-start(bf16[4,1024]{1,0:T(4,128)(2,1)} %refs_0_.1) | copy-start | bytes 24580
  12.7 4.2 %collective-permute-start.3 = (bf16[16,1024]{1,0:T(8,128)(2,1)S(1)}, bf16[16,1024]{1,0:T(8,128)(2,1)S(1)}, u32[]{:S(2)}, u32[]{:S(2)}) collective-permute-start(bf16[16,1024]{1,0:T(8,128)(2,1)S(1)} %stack.1.rest_0_), channel_id=1, source_target_pairs={{0,1},{1,0},{2,3},{3,2},{4,5},{5,4},{6,7},{7,6},{8,9},{9,8},{10,11... | collective-permute-start | bytes 98312 | tf_op jit(solution)/shard_map/ppermute | solution.py:521
  24.7 9.8 %collective-permute-start.12 = (f16[512,128]{1,0:T(8,128)(2,1)S(1)}, f16[512,128]{1,0:T(8,128)(2,1)S(1)}, u32[]{:S(2)}, u32[]{:S(2)}) collective-permute-start(f16[512,128]{1,0:T(8,128)(2,1)S(1)} %convert_element_type.46), channel_id=1, source_target_pairs={{0,24},{8,16},{16,8},{24,0},{1,25},{9,17},{17,9},{25,1},{2,26},{10... | collective-permute-start | bytes 393224 | tf_op jit(solution)/shard_map/ppermute | solution.py:521
  27.2 7.8 %collective-permute-start.11 = (f16[512,128]{1,0:T(8,128)(2,1)S(1)}, f16[512,128]{1,0:T(8,128)(2,1)S(1)}, u32[]{:S(2)}, u32[]{:S(2)}) collective-permute-start(f16[512,128]{1,0:T(8,128)(2,1)S(1)} %convert_element_type.44), channel_id=1, source_target_pairs={{0,16},{8,24},{16,0},{24,8},{1,17},{9,25},{17,1},{25,9},{2,18},{10... | collective-permute-start | bytes 393224 | tf_op jit(solution)/shard_map/ppermute | solution.py:521
  27.7 7.3 %collective-permute-start.10 = (f16[512,128]{1,0:T(8,128)(2,1)S(1)}, f16[512,128]{1,0:T(8,128)(2,1)S(1)}, u32[]{:S(2)}, u32[]{:S(2)}) collective-permute-start(f16[512,128]{1,0:T(8,128)(2,1)S(1)} %convert_element_type.42), channel_id=1, source_target_pairs={{0,8},{8,0},{16,24},{24,16},{1,9},{9,1},{17,25},{25,17},{2,10},{10... | collective-permute-start | bytes 393224 | tf_op jit(solution)/shard_map/ppermute | solution.py:521
  31.4 6.8 %collective-permute-start.6 = (f16[512,128]{1,0:T(8,128)(2,1)S(1)}, f16[512,128]{1,0:T(8,128)(2,1)S(1)}, u32[]{:S(2)}, u32[]{:S(2)}) collective-permute-start(f16[512,128]{1,0:T(8,128)(2,1)S(1)} %convert_element_type.40), channel_id=1, source_target_pairs={{0,24},{8,16},{16,8},{24,0},{1,25},{9,17},{17,9},{25,1},{2,26},{10... | collective-permute-start | bytes 393224 | tf_op jit(solution)/shard_map/ppermute | solution.py:521
  33.9 8.0 %collective-permute-start.5 = (f16[512,128]{1,0:T(8,128)(2,1)S(1)}, f16[512,128]{1,0:T(8,128)(2,1)S(1)}, u32[]{:S(2)}, u32[]{:S(2)}) collective-permute-start(f16[512,128]{1,0:T(8,128)(2,1)S(1)} %convert_element_type.38), channel_id=1, source_target_pairs={{0,16},{8,24},{16,0},{24,8},{1,17},{9,25},{17,1},{25,9},{2,18},{10... | collective-permute-start | bytes 393224 | tf_op jit(solution)/shard_map/ppermute | solution.py:521
  34.5 7.5 %collective-permute-start.4 = (f16[512,128]{1,0:T(8,128)(2,1)S(1)}, f16[512,128]{1,0:T(8,128)(2,1)S(1)}, u32[]{:S(2)}, u32[]{:S(2)}) collective-permute-start(f16[512,128]{1,0:T(8,128)(2,1)S(1)} %convert_element_type.36), channel_id=1, source_target_pairs={{0,8},{8,0},{16,24},{24,16},{1,9},{9,1},{17,25},{25,17},{2,10},{10... | collective-permute-start | bytes 393224 | tf_op jit(solution)/shard_map/ppermute | solution.py:521
  35.2 10.2 %collective-permute-start.15 = (bf16[528,128]{1,0:T(8,128)(2,1)S(1)}, bf16[528,128]{1,0:T(8,128)(2,1)S(1)}, u32[]{:S(2)}, u32[]{:S(2)}) collective-permute-start(bf16[528,128]{1,0:T(8,128)(2,1)S(1)} %soften.3.rest_0_), channel_id=1, source_target_pairs={{0,24},{8,16},{16,8},{24,0},{1,25},{9,17},{17,9},{25,1},{2,26},{10... | collective-permute-start | bytes 405512 | tf_op jit(solution)/shard_map/ppermute | solution.py:521
  37.7 10.9 %collective-permute-start.14 = (bf16[528,128]{1,0:T(8,128)(2,1)S(1)}, bf16[528,128]{1,0:T(8,128)(2,1)S(1)}, u32[]{:S(2)}, u32[]{:S(2)}) collective-permute-start(bf16[528,128]{1,0:T(8,128)(2,1)S(1)} %soften.3.rest_0_), channel_id=1, source_target_pairs={{0,16},{8,24},{16,0},{24,8},{1,17},{9,25},{17,1},{25,9},{2,18},{10... | collective-permute-start | bytes 405512 | tf_op jit(solution)/shard_map/ppermute | solution.py:521
  38.2 10.4 %collective-permute-start.13 = (bf16[528,128]{1,0:T(8,128)(2,1)S(1)}, bf16[528,128]{1,0:T(8,128)(2,1)S(1)}, u32[]{:S(2)}, u32[]{:S(2)}) collective-permute-start(bf16[528,128]{1,0:T(8,128)(2,1)S(1)} %soften.3.rest_0_), channel_id=1, source_target_pairs={{0,8},{8,0},{16,24},{24,16},{1,9},{9,1},{17,25},{25,17},{2,10},{10... | collective-permute-start | bytes 405512 | tf_op jit(solution)/shard_map/ppermute | solution.py:521
  42.1 9.8 %collective-permute-start.9 = (bf16[528,128]{1,0:T(8,128)(2,1)S(1)}, bf16[528,128]{1,0:T(8,128)(2,1)S(1)}, u32[]{:S(2)}, u32[]{:S(2)}) collective-permute-start(bf16[528,128]{1,0:T(8,128)(2,1)S(1)} %soften.2.rest_2_), channel_id=1, source_target_pairs={{0,24},{8,16},{16,8},{24,0},{1,25},{9,17},{17,9},{25,1},{2,26},{10... | collective-permute-start | bytes 405512 | tf_op jit(solution)/shard_map/ppermute | solution.py:521
  44.8 7.2 %collective-permute-start.8 = (bf16[528,128]{1,0:T(8,128)(2,1)S(1)}, bf16[528,128]{1,0:T(8,128)(2,1)S(1)}, u32[]{:S(2)}, u32[]{:S(2)}) collective-permute-start(bf16[528,128]{1,0:T(8,128)(2,1)S(1)} %soften.2.rest_2_), channel_id=1, source_target_pairs={{0,16},{8,24},{16,0},{24,8},{1,17},{9,25},{17,1},{25,9},{2,18},{10... | collective-permute-start | bytes 405512 | tf_op jit(solution)/shard_map/ppermute | solution.py:521
  45.5 6.5 %collective-permute-start.7 = (bf16[528,128]{1,0:T(8,128)(2,1)S(1)}, bf16[528,128]{1,0:T(8,128)(2,1)S(1)}, u32[]{:S(2)}, u32[]{:S(2)}) collective-permute-start(bf16[528,128]{1,0:T(8,128)(2,1)S(1)} %soften.2.rest_2_), channel_id=1, source_target_pairs={{0,8},{8,0},{16,24},{24,16},{1,9},{9,1},{17,25},{25,17},{2,10},{10... | collective-permute-start | bytes 405512 | tf_op jit(solution)/shard_map/ppermute | solution.py:521
  58.1 1.3 %collective-permute-start.16 = (f32[32,1024]{1,0:T(8,128)S(1)}, f32[32,1024]{1,0:T(8,128)S(1)}, u32[]{:S(2)}, u32[]{:S(2)}) collective-permute-start(f32[32,1024]{1,0:T(8,128)S(1)} %get-tuple-element.49), channel_id=1, source_target_pairs={{0,1},{1,0},{2,3},{3,2},{4,5},{5,4},{6,7},{7,6},{8,9},{9,8},{10,11... | collective-permute-start | bytes 393224 | tf_op jit(solution)/shard_map/ppermute | solution.py:521
  59.5 4.5 %collective-permute-start.17 = (f32[8,1024]{1,0:T(8,128)S(1)}, f32[8,1024]{1,0:T(8,128)S(1)}, u32[]{:S(2)}, u32[]{:S(2)}) collective-permute-start(f32[8,1024]{1,0:T(8,128)S(1)} %get-tuple-element.51), channel_id=1, source_target_pairs={{0,2},{1,3},{2,0},{3,1},{4,6},{5,7},{6,4},{7,5},{8,10},{9,11},{10,... | collective-permute-start | bytes 98312 | tf_op jit(solution)/shard_map/ppermute | solution.py:521
  59.6 4.9 %collective-permute-start.18 = (f32[8,1024]{1,0:T(8,128)S(1)}, f32[8,1024]{1,0:T(8,128)S(1)}, u32[]{:S(2)}, u32[]{:S(2)}) collective-permute-start(f32[8,1024]{1,0:T(8,128)S(1)} %get-tuple-element.52), channel_id=1, source_target_pairs={{0,4},{1,5},{2,6},{3,7},{4,0},{5,1},{6,2},{7,3},{8,12},{9,13},{10,... | collective-permute-start | bytes 98312 | tf_op jit(solution)/shard_map/ppermute | solution.py:521
  60.3 5.9 %collective-permute-start.19 = (f32[8,1024]{1,0:T(8,128)S(1)}, f32[8,1024]{1,0:T(8,128)S(1)}, u32[]{:S(2)}, u32[]{:S(2)}) collective-permute-start(f32[8,1024]{1,0:T(8,128)S(1)} %get-tuple-element.53), channel_id=1, source_target_pairs={{0,6},{1,7},{2,4},{3,5},{4,2},{5,3},{6,0},{7,1},{8,14},{9,15},{10,... | collective-permute-start | bytes 98312 | tf_op jit(solution)/shard_map/ppermute | solution.py:521

commit v5 on v4

--- a/solution.py
+++ b/solution.py
@@ -11,9 +11,9 @@
 f32, bf16 = jnp.float32, jnp.bfloat16
 VMEM = pl.BlockSpec(memory_space=pltpu.VMEM)
 SMEM = pl.BlockSpec(memory_space=pltpu.SMEM)
-HBM = pl.BlockSpec(memory_space=pltpu.HBM)
 LANES, ROWS = 128, 8
-START_MIB = 16
+PREPARE = 1 << 20
+EARLY = 20_000_000_000
 NN = (((1,), (0,)), ((), ()))
 NT = (((1,), (1,)), ((), ()))
 
@@ -52,45 +52,91 @@
     return VMEM if steps == 1 else pl.BlockSpec(shape, lambda i: (0,) * len(shape))
 
 
-def start_kernel(pack, pixels_in, turns_in, table_in, kind_in, names_in, *rest):
-    matrix, response_out, weighted, power_out, names = rest[:5]
-    pixels, turns, table, kind, response, done, sent = rest[5:]
-    moves = [
-        pltpu.make_async_copy(source, target, done.at[i])
-        for i, (source, target) in enumerate(
-            [(turns_in, turns), (table_in, table), (kind_in, kind), (names_in, names), (pixels_in, pixels)]
-        )
-    ]
-    for move in moves:
-        move.start()
-    turn_count, angles, _ = turns.shape
-    kinds, width = table.shape
+def turn_matrix(turns, i, pack, inside):
+    _, angles, width = turns.shape
     per = LANES // angles
-    tiles = width // LANES
+    wide = []
+    for j in range(pack):
+        turn = turns[i * pack + j]
+        turn = jnp.concatenate([jnp.concatenate([turn] * (LANES // width), axis=1)] * per, axis=0)
+        wide.append(jnp.where(inside, turn, jnp.zeros((), bf16)))
+    return jnp.concatenate(wide, axis=1)
+
+
+def same_cycle(angles):
     row = lax.broadcasted_iota(jnp.int32, (LANES, LANES), 0) // angles
     col = lax.broadcasted_iota(jnp.int32, (LANES, LANES), 1) // angles
-    zero = jnp.zeros((), bf16)
-    moves[0].wait()
-    moves[1].wait()
-    power = split(table[...] * table[...], 2)
-    power_out[...] = jnp.concatenate(power, axis=0)
+    return row == col
+
+
+def seed_kernel(out):
+    out[...] = lax.broadcasted_iota(jnp.int32, out.shape, 0)
+
+
+def seed():
+    return pl.pallas_call(
+        seed_kernel,
+        out_specs=VMEM,
+        out_shape=jax.ShapeDtypeStruct((LANES, 2 * LANES), jnp.int32),
+        name="seed",
+        **limits(4, EARLY, 0),
+    )()
+
+
+def start_kernel(numbers, own_in, pixels, turns, table, kind, names_in, weighted, power, names, own, turns2):
+    names[...] = names_in[...]
+    own[...] = own_in[...]
+    for i in range(turns.shape[0]):
+        turns2[i] = jnp.concatenate([turns[i]] * (LANES // turns.shape[2]), axis=1)
+    kinds, width = table.shape
+    power[...] = jnp.concatenate(split(table[...] * table[...], 2), axis=0)
+    table3 = jnp.concatenate(split(table[...], 3), axis=0)
+    count = pixels.shape[0]
+    rows = math.gcd(count, 256)
+    ids = numbers[:, :rows]
+    for i in range(count // rows):
+        at = slice(i * rows, (i + 1) * rows)
+        hit = jnp.where((ids % kinds == kind[:, at]) & (ids < 3 * kinds), 1.0, 0.0).T.astype(bf16)
+        factor = dot(hit[:, :3 * kinds], table3, NN)
+        weighted[at, :width] = (pixels[at, :].astype(f32) * factor).astype(bf16)
+        weighted[at, width:] = hit
+
+
+def start(particles, references, turns, table, kind, names):
+    count, pixels = particles.shape
+    kinds = table.shape[0]
+    return pl.pallas_call(
+        start_kernel,
+        in_specs=[VMEM] * 7,
+        out_specs=[VMEM] * 5,
+        out_shape=[
+            jax.ShapeDtypeStruct((count, pixels + LANES), bf16),
+            jax.ShapeDtypeStruct((2 * kinds, pixels), bf16),
+            jax.ShapeDtypeStruct(names.shape, jnp.int32),
+            jax.ShapeDtypeStruct(references.shape, bf16),
+            jax.ShapeDtypeStruct(turns.shape[:2] + (LANES,), bf16),
+        ],
+        name="start",
+        **limits(16, 1 << 20, 0),
+    )(seed(), references, particles, turns, table, kind, names)
+
+
+def prepare_kernel(pack, after, turns, power, matrix, response):
+    turn_count, angles, _ = turns.shape
+    kinds, width = power.shape[0] // 2, power.shape[1]
+    tiles = width // LANES
+    inside = same_cycle(angles)
     lhs = jnp.concatenate(
         [
-            jnp.concatenate([part[:, t * LANES:(t + 1) * LANES] for part in power], axis=1)
+            jnp.concatenate(
+                [power[k * kinds:(k + 1) * kinds, t * LANES:(t + 1) * LANES] for k in range(2)], axis=1
+            )
             for t in range(tiles)
         ],
         axis=0,
     )
-    steps = turn_count // pack
-    bands = math.gcd(steps, 4)
-    sends = []
-    for i in range(steps):
-        wide = []
-        for j in range(pack):
-            turn = turns[i * pack + j]
-            turn = jnp.concatenate([jnp.concatenate([turn] * per, axis=1)] * per, axis=0)
-            wide.append(jnp.where(row == col, turn, zero))
-        wide = jnp.concatenate(wide, axis=1)
+    for i in range(turn_count // pack):
+        wide = turn_matrix(turns, i, pack, inside)
         matrix[i * LANES:(i + 1) * LANES, :] = wide
         value = dot(lhs, jnp.concatenate([wide, wide], axis=0), NN).astype(bf16)
         for j in range(pack):
@@ -98,89 +144,35 @@
                 response[i * kinds:(i + 1) * kinds, j * width + t * LANES:j * width + (t + 1) * LANES] = value[
                     t * kinds:(t + 1) * kinds, j * LANES:(j + 1) * LANES
                 ]
-        if (i + 1) % (steps // bands) == 0:
-            band = len(sends)
-            at = pl.ds(band * (steps // bands) * kinds, steps // bands * kinds)
-            send = pltpu.make_async_copy(response.at[at, :], response_out.at[at, :], sent.at[band])
-            send.start()
-            sends.append(send)
-    for move in moves[2:]:
-        move.wait()
-    table3 = jnp.concatenate(split(table[...], 3), axis=0)
-    count = pixels.shape[0]
-    rows = math.gcd(count, 256)
-    ids = lax.broadcasted_iota(jnp.int32, (LANES, rows), 0)
-    for i in range(count // rows):
-        at = slice(i * rows, (i + 1) * rows)
-        hit = jnp.where((ids % kinds == kind[:, at]) & (ids < 3 * kinds), 1.0, 0.0).T.astype(bf16)
-        factor = dot(hit[:, :3 * kinds], table3, NN)
-        weighted[at, :width] = (pixels[at, :].astype(f32) * factor).astype(bf16)
-        weighted[at, width:] = hit
-    for send in sends:
-        send.wait()
-
-
-def start(particles, turns, table, kind, names, pack):
-    count, pixels = particles.shape
-    turn_count, angles, _ = turns.shape
-    kinds = table.shape[0]
+
+
+def prepare(turns, power, pack, after):
+    turn_count = turns.shape[0]
+    kinds, pixels = power.shape[0] // 2, power.shape[1]
     steps = turn_count // pack
     return pl.pallas_call(
-        functools.partial(start_kernel, pack),
-        in_specs=[HBM] * 5,
-        out_specs=[VMEM, HBM, VMEM, VMEM, VMEM],
+        functools.partial(prepare_kernel, pack),
+        in_specs=[VMEM] * 3,
+        out_specs=[VMEM] * 2,
         out_shape=[
             jax.ShapeDtypeStruct((steps * LANES, pack * LANES), bf16),
             jax.ShapeDtypeStruct((steps * kinds, pack * pixels), bf16),
-            jax.ShapeDtypeStruct((count, pixels + LANES), bf16),
-            jax.ShapeDtypeStruct((2 * kinds, pixels), bf16),
-            jax.ShapeDtypeStruct(names.shape, jnp.int32),
         ],
-        scratch_shapes=[
-            pltpu.VMEM(particles.shape, bf16),
-            pltpu.VMEM(turns.shape, bf16),
-            pltpu.VMEM(table.shape, f32),
-            pltpu.VMEM(kind.shape, jnp.int32),
-            pltpu.VMEM((steps * kinds, pack * pixels), bf16),
-            pltpu.SemaphoreType.DMA((5,)),
-            pltpu.SemaphoreType.DMA((4,)),
-        ],
-        name="start",
-        **limits(START_MIB, 1000000, 0),
-    )(particles, turns, table, kind, names)
-
-
-def stack_kernel(*refs):
-    out = refs[-1]
-    rows = refs[0].shape[0]
-    for i, ref in enumerate(refs[:-1]):
-        out[i * rows:(i + 1) * rows, :] = ref[...]
-
-
-def stack(blocks):
-    rows, columns = blocks[0].shape
-    return pl.pallas_call(
-        stack_kernel,
-        in_specs=[VMEM] * len(blocks),
-        out_specs=VMEM,
-        out_shape=jax.ShapeDtypeStruct((len(blocks) * rows, columns), blocks[0].dtype),
-        name="stack",
-        **limits(4, 20_000_000_000, 1 << 25),
-    )(*blocks)
-
-
-def rotate_kernel(groups, turn_count, power2, matrix, *rest):
+        name="prepare",
+        **limits(16, PREPARE, 0),
+    )(after, turns, power)
+
+
+def rotate_kernel(groups, pack, power2, turns, *rest):
     refs = rest[:-4]
     rotated, mean, center, energy = rest[-4:]
+    turn_count, angles, _ = turns.shape
+    inside_cycle = same_cycle(angles)
     kinds, pixels = power2.shape[0] // 2, power2.shape[1]
-    pack = matrix.shape[1] // LANES
     cpg = ROWS // pack
     tiles = pixels // LANES
     group_pairs = cpg * turn_count
-    source = [block[...].astype(f32) for block in refs]
-    if len(refs) > 1:
-        source = [part[i * cpg:(i + 1) * cpg, :] for i in range(groups // len(refs)) for part in source]
-    source = jnp.concatenate(source, axis=0)
+    source = jnp.concatenate([block[...].astype(f32) for block in refs], axis=0)
     line = lax.broadcasted_iota(jnp.int32, (ROWS, pixels), 0) // cpg
     copies = []
     for i in range(groups // pack):
@@ -203,7 +195,8 @@
         axis=0,
     ).astype(bf16)
     for s in range(turn_count // (2 * pack)):
-        value = dot(lhs, matrix[s * 2 * LANES:(s + 1) * 2 * LANES, :], NT)
+        both = [turn_matrix(turns, 2 * s + h, pack, inside_cycle) for h in range(2)]
+        value = dot(lhs, jnp.concatenate(both, axis=0), NT)
         for t in range(tiles):
             for g in range(groups):
                 at = (t * groups + g) * ROWS
@@ -236,16 +229,17 @@
         rotated[at, pixels:] = jnp.concatenate(parts + [blank], axis=0).T.astype(bf16)
 
 
-def rotate(refs, matrix, power2, turn_count, groups):
+def rotate(refs, turns, power2, pack, groups):
     kinds, pixels = power2.shape[0] // 2, power2.shape[1]
-    cpg = ROWS * LANES // matrix.shape[1]
+    turn_count = turns.shape[0]
+    cpg = ROWS // pack
     groups_all = sum(block.shape[0] for block in refs) // cpg
     steps = groups_all // groups
     pairs = groups * cpg * turn_count
     return pl.pallas_call(
-        functools.partial(rotate_kernel, groups, turn_count),
+        functools.partial(rotate_kernel, groups, pack),
         grid=(steps,),
-        in_specs=[same_spec(steps, power2.shape), same_spec(steps, matrix.shape)]
+        in_specs=[same_spec(steps, power2.shape), same_spec(steps, turns.shape)]
         + [block_spec(steps, (block.shape[0] // steps, pixels), 0) for block in refs],
         out_specs=[block_spec(steps, (pairs, pixels + LANES), 0), same_spec(steps, (1, LANES))],
         out_shape=[
@@ -255,7 +249,7 @@
         scratch_shapes=[pltpu.VMEM((kinds, 1), f32), pltpu.VMEM((kinds, pairs), f32)],
         name="rotate",
         **limits(12 if steps == 1 else 32, 8 * steps * pairs * pixels * 64, 2 * steps * pairs * pixels),
-    )(power2, matrix, *refs)
+    )(power2, turns, *refs)
 
 
 def score_kernel(groups, scale, begin, me, here, weighted, names, rotated, *rest):
@@ -535,15 +529,15 @@
     scale = 4.0 / math.sqrt(pixels * peers)
     me = lax.axis_index("cls").astype(jnp.int32).reshape(1)
     here = (lax.axis_index("dom") if paired else jnp.int32(0)).astype(jnp.int32).reshape(1)
+    weighted, power2, names, own_refs, turns2 = start(
+        particles, references, rotations, ctf_table, defocus.reshape(1, count), candidates.T
+    )
     if paired:
-        half = stack([references] + [swap(references, "dom", 2 * k) for k in range(1, owners // 2)])
-        refs = [half, swap(half, "dom", 1)]
+        line = [own_refs] + [swap(references, "dom", 2 * k) for k in range(1, owners // 2)]
+        refs = [half for block in line for half in (block, swap(references if block is own_refs else block, "dom", 1))]
     else:
         refs = [lax.all_gather(references, "dom", axis=0, tiled=True)]
-    matrix, response, weighted, power2, names = start(
-        particles, rotations, ctf_table, defocus.reshape(1, count), candidates.T, pack
-    )
-    rotated, mean = rotate(refs, matrix, power2, turn_count, groups)
+    rotated, mean = rotate(refs, turns2, power2, pack, groups)
     chunks = 2
     size = count // chunks
     blocks = []
@@ -554,6 +548,7 @@
             total = total + swap(cut[k].astype(jnp.float16), "cls", k).astype(f32)
         own = soften(total, mean)
         blocks.append([own] + [swap(own, "cls", k) for k in range(1, peers)])
+    matrix, response = prepare(turns2, power2, pack, blocks[0][0])
     parts = 2 if paired else 1
     out = []
     for c in range(chunks):

time: 67 us -> 63.4 us (0.946)
  Pallas kernels: 25.2 us -> 23.3 us
  waiting for transfers between devices: 13.7 us -> 12.3 us
  local copies, waits for them, and re-layouts: 0.72 us -> 0.03 us
    pallas_call x3 -> x4, Pallas kernels: 8.55 us -> 6.78 us  [the longest x1 4.46 us: rotate(): pl.pallas_call(functools.partial(rotate_kernel, groups, pack), grid=(step...]
    ppermute x20 -> x23, waiting for transfers between devices: 13.7 us -> 12.3 us  [swap(): lax.ppermute(x, axis, [(i, i ^ k) for i in range(lax.axis_size(axis))])]
    unnamed x12, local copies, waits for them, and re-layouts: 0.72 us -> 0.03 us
    ppermute x20 -> x23, starting transfers between devices: 26.1 us -> 26.4 us  [swap(): lax.ppermute(x, axis, [(i, i ^ k) for i in range(lax.axis_size(axis))])]
  transfers between devices with their start and end apart: 20 -> 23, of which waited for: 8 -> 10; matrix products, arithmetic and copies ran while one was open for 0% -> 0% of each run, Pallas kernels for 16% -> 14%
where the time goes in v5:
time: 63.4 us; the launch traced here: 63.2 us
  starting transfers between devices  26.4 us (42%)
  Pallas kernels  23.3 us (37%)
  waiting for transfers between devices  12.3 us (19%)
  between operations  0.9 us (1%)
    ppermute x23, starting transfers between devices, swap(): lax.ppermute(x, axis, [(i, i ^ k) for i in range(lax.axis_size(axis))])  26.4 us
    ppermute x23, waiting for transfers between devices, swap(): lax.ppermute(x, axis, [(i, i ^ k) for i in range(lax.axis_size(axis))])  12.3 us
    pallas_call x2, Pallas kernels, collect(): pl.pallas_call(functools.partial(collect_kernel, groups, parts, turn_coun...  9.39 us
    pallas_call x2, Pallas kernels, score(): pl.pallas_call(functools.partial(score_kernel, groups, scale, begin), gri...  6.22 us
    pallas_call x1, Pallas kernels, rotate(): pl.pallas_call(functools.partial(rotate_kernel, groups, pack), grid=(step...  4.46 us
    pallas_call x1, Pallas kernels, prepare(): pl.pallas_call(functools.partial(prepare_kernel, pack), in_specs=[VMEM] *...  1.5 us
  transfers between devices with their start and end apart: 23, of which 10 were waited for; matrix products, arithmetic and copies ran while one was open for 0% of the time, Pallas kernels for 14%

profile of v5, /device:TPU:0, one launch (start us, length us, event | category | flops | bytes accessed | tf_op | source)
XLA Modules:
  0.0 63.2 jit_solution(6802594407512327433)
XLA Ops:
  0.7 3.1 %collective-permute-start.1 = (bf16[4,1024]{1,0:T(4,128)(2,1)}, bf16[4,1024]{1,0:T(4,128)(2,1)S(1)}, u32[]{:S(2)}, u32[]{:S(2)}) collective-permute-start(bf16[4,1024]{1,0:T(4,128)(2,1)} %own_in.1), channel_id=1, source_target_pairs={{0,2},{1,3},{2,0},{3,1},{4,6},{5,7},{6,4},{7,5},{8,10},{9,11},{10,... | collective-permute-start | bytes 24584 | tf_op jit(solution)/shard_map/ppermute | solution.py:515
  3.8 2.5 %collective-permute-start.5 = (bf16[4,1024]{1,0:T(4,128)(2,1)}, bf16[4,1024]{1,0:T(4,128)(2,1)S(1)}, u32[]{:S(2)}, u32[]{:S(2)}) collective-permute-start(bf16[4,1024]{1,0:T(4,128)(2,1)} %own_in.1), channel_id=1, source_target_pairs={{0,6},{1,7},{2,4},{3,5},{4,2},{5,3},{6,0},{7,1},{8,14},{9,15},{10,... | collective-permute-start | bytes 24584 | tf_op jit(solution)/shard_map/ppermute | solution.py:515
  6.9 2.6 %collective-permute-done.5.rest_6_ = bf16[4,1024]{1,0:T(4,128)(2,1)S(1)} collective-permute-done((bf16[4,1024]{1,0:T(4,128)(2,1)}, bf16[4,1024]{1,0:T(4,128)(2,1)S(1)}, u32[]{:S(2)}, u32[]{:S(2)}) %collective-permute-start.5) | collective-permute-done | bytes 8224 | tf_op jit(solution)/shard_map/ppermute | solution.py:515
  9.5 1.5 %collective-permute-done.3.rest_4_ = bf16[4,1024]{1,0:T(4,128)(2,1)S(1)} collective-permute-done((bf16[4,1024]{1,0:T(4,128)(2,1)}, bf16[4,1024]{1,0:T(4,128)(2,1)S(1)}, u32[]{:S(2)}, u32[]{:S(2)}) %collective-permute-start.3) | collective-permute-done | bytes 8224 | tf_op jit(solution)/shard_map/ppermute | solution.py:515
  11.1 0.8 %start.1 = (bf16[1024,1152]{1,0:T(8,128)(2,1)S(1)}, bf16[64,1024]{1,0:T(8,128)(2,1)S(1)}, s32[2,1024]{1,0:T(2,128)S(1)}, bf16[4,1024]{1,0:T(4,128)(2,1)S(1)}, bf16[64,64,128]{2,1,0:T(8,128)(2,1)S(1)}) custom-call(s32[128,256]{1,0:T(8,128)S(1)} %seed.1.numbers, bf16[4,1024]{1,0:T(4,128)(2,1)S(1)} %copy-done.4, bf16[1024,1024]{1,0:T(8,128)(2,1)S(1)} %copy-done, ...), custom_call_target="tpu_custom_call" | custom-call | flops 1048576 | tf_op jit(solution)/shard_map/start/pallas_call | solution.py:108
  12.2 4.5 %rotate.1 = (bf16[2048,1152]{1,0:T(8,128)(2,1)S(1)}, f32[1,128]{1,0:T(1,128)S(1)}) custom-call(bf16[64,1024]{1,0:T(8,128)(2,1)S(1)} %get-tuple-element.34.power2.power, bf16[64,64,128]{2,1,0:T(8,128)(2,1)S(1)} %get-tuple-element.35.turns, bf16[4,1024]{1,0:T(4,128)(2,1)S(1)} %get-tuple-element.36.rest_0_, bf16[4,1024]{1,0:T(4,128)(2,1)S(1)} %collective-permute-done.rest_1_, ...), custom_call_target="tpu_custom_call" | custom-call | flops 1073741824 | bytes 4194304 | tf_op jit(solution)/shard_map/rotate/pallas_call | solution.py:239
  16.7 3.1 %score.2 = (f32[512,128]{1,0:T(8,128)S(1)}, f32[512,128]{1,0:T(8,128)S(1)}, f32[512,128]{1,0:T(8,128)S(1)}, f32[512,128]{1,0:T(8,128)S(1)}) custom-call(s32[1]{0:T(128)} %bitcast.me, s32[1]{0:T(128)} %bitcast.1.here, bf16[1024,1152]{1,0:T(8,128)(2,1)S(1)} %get-tuple-element.33.weighted, s32[2,1024]{1,0:T(2,128)S(1)} %get-tuple-element.32.names, ...), custom_call_target="tpu_custom_call" | custom-call | flops 2415919104 | bytes 4718592 | tf_op jit(solution)/shard_map/score/pallas_call | solution.py:288
  19.9 2.5 %collective-permute-start.9 = (f16[512,128]{1,0:T(8,128)(2,1)S(1)}, f16[512,128]{1,0:T(8,128)(2,1)S(1)}, u32[]{:S(2)}, u32[]{:S(2)}) collective-permute-start(f16[512,128]{1,0:T(8,128)(2,1)S(1)} %convert_element_type.40), channel_id=1, source_target_pairs={{0,24},{8,16},{16,8},{24,0},{1,25},{9,17},{17,9},{25,1},{2,26},{10... | collective-permute-start | bytes 393224 | tf_op jit(solution)/shard_map/ppermute | solution.py:515
  22.4 0.5 collective-permute-start.8
  22.9 0.5 collective-permute-start.7
  23.4 3.1 %score.3 = (f32[512,128]{1,0:T(8,128)S(1)}, f32[512,128]{1,0:T(8,128)S(1)}, f32[512,128]{1,0:T(8,128)S(1)}, f32[512,128]{1,0:T(8,128)S(1)}) custom-call(s32[1]{0:T(128)} %bitcast.me, s32[1]{0:T(128)} %bitcast.1.here, bf16[1024,1152]{1,0:T(8,128)(2,1)S(1)} %get-tuple-element.33.weighted, s32[2,1024]{1,0:T(2,128)S(1)} %get-tuple-element.32.names, ...), custom_call_target="tpu_custom_call" | custom-call | flops 2415919104 | bytes 4718592 | tf_op jit(solution)/shard_map/score/pallas_call | solution.py:288
  26.6 2.5 %collective-permute-start.12 = (f16[512,128]{1,0:T(8,128)(2,1)S(1)}, f16[512,128]{1,0:T(8,128)(2,1)S(1)}, u32[]{:S(2)}, u32[]{:S(2)}) collective-permute-start(f16[512,128]{1,0:T(8,128)(2,1)S(1)} %convert_element_type.46), channel_id=1, source_target_pairs={{0,24},{8,16},{16,8},{24,0},{1,25},{9,17},{17,9},{25,1},{2,26},{10... | collective-permute-start | bytes 393224 | tf_op jit(solution)/shard_map/ppermute | solution.py:515
  29.1 0.5 collective-permute-start.11
  29.6 0.5 collective-permute-start.10
  30.4 2.5 %collective-permute-start.18 = (bf16[528,128]{1,0:T(8,128)(2,1)S(1)}, bf16[528,128]{1,0:T(8,128)(2,1)S(1)}, u32[]{:S(2)}, u32[]{:S(2)}) collective-permute-start(bf16[528,128]{1,0:T(8,128)(2,1)S(1)} %soften.2.after.rest_0_), channel_id=1, source_target_pairs={{0,24},{8,16},{16,8},{24,0},{1,25},{9,17},{17,9},{25,1},{2,26},{10... | collective-permute-start | bytes 405512 | tf_op jit(solution)/shard_map/ppermute | solution.py:515
  32.9 0.5 collective-permute-start.17
  33.4 2.0 %collective-permute-start.16 = (bf16[528,128]{1,0:T(8,128)(2,1)S(1)}, bf16[528,128]{1,0:T(8,128)(2,1)S(1)}, u32[]{:S(2)}, u32[]{:S(2)}) collective-permute-start(bf16[528,128]{1,0:T(8,128)(2,1)S(1)} %soften.2.after.rest_0_), channel_id=1, source_target_pairs={{0,8},{8,0},{16,24},{24,16},{1,9},{9,1},{17,25},{25,17},{2,10},{10... | collective-permute-start | bytes 405512 | tf_op jit(solution)/shard_map/ppermute | solution.py:515
  35.5 1.9 %collective-permute-done.11 = f16[512,128]{1,0:T(8,128)(2,1)S(1)} collective-permute-done((f16[512,128]{1,0:T(8,128)(2,1)S(1)}, f16[512,128]{1,0:T(8,128)(2,1)S(1)}, u32[]{:S(2)}, u32[]{:S(2)}) %collective-permute-start.11) | collective-permute-done | bytes 131104 | tf_op jit(solution)/shard_map/ppermute | solution.py:515
  37.5 2.0 %collective-permute-start.15 = (bf16[528,128]{1,0:T(8,128)(2,1)S(1)}, bf16[528,128]{1,0:T(8,128)(2,1)S(1)}, u32[]{:S(2)}, u32[]{:S(2)}) collective-permute-start(bf16[528,128]{1,0:T(8,128)(2,1)S(1)} %soften.3.rest_2_), channel_id=1, source_target_pairs={{0,24},{8,16},{16,8},{24,0},{1,25},{9,17},{17,9},{25,1},{2,26},{10... | collective-permute-start | bytes 405512 | tf_op jit(solution)/shard_map/ppermute | solution.py:515
  39.6 1.2 %collective-permute-start.14 = (bf16[528,128]{1,0:T(8,128)(2,1)S(1)}, bf16[528,128]{1,0:T(8,128)(2,1)S(1)}, u32[]{:S(2)}, u32[]{:S(2)}) collective-permute-start(bf16[528,128]{1,0:T(8,128)(2,1)S(1)} %soften.3.rest_2_), channel_id=1, source_target_pairs={{0,16},{8,24},{16,0},{24,8},{1,17},{9,25},{17,1},{25,9},{2,18},{10... | collective-permute-start | bytes 405512 | tf_op jit(solution)/shard_map/ppermute | solution.py:515
  40.8 1.5 %prepare.1 = (bf16[4096,256]{1,0:T(8,128)(2,1)S(1)}, bf16[1024,2048]{1,0:T(8,128)(2,1)S(1)}) custom-call(bf16[528,128]{1,0:T(8,128)(2,1)S(1)} %soften.2.after.rest_0_, bf16[64,64,128]{2,1,0:T(8,128)(2,1)S(1)} %get-tuple-element.35.turns, bf16[64,1024]{1,0:T(8,128)(2,1)S(1)} %get-tuple-element.34.power2.power), custom_call_target="tpu_custom_call" | custom-call | flops 1048576 | tf_op jit(solution)/shard_map/prepare/pallas_call | solution.py:153
  42.7 0.6 %collective-permute-done.17.rest_2_ = bf16[528,128]{1,0:T(8,128)(2,1)S(1)} collective-permute-done((bf16[528,128]{1,0:T(8,128)(2,1)S(1)}, bf16[528,128]{1,0:T(8,128)(2,1)S(1)}, u32[]{:S(2)}, u32[]{:S(2)}) %collective-permute-start.17) | collective-permute-done | bytes 135200 | tf_op jit(solution)/shard_map/ppermute | solution.py:515
  43.3 3.3 %collect.2 = (f32[512,4096]{1,0:T(8,128)S(1)}, f32[64,1024]{1,0:T(8,128)S(1)}, f32[1,1024]{1,0:T(1,128)S(1)}) custom-call(s32[1]{0:T(128)} %bitcast.me, s32[1]{0:T(128)} %bitcast.1.here, s32[2,1024]{1,0:T(2,128)S(1)} %get-tuple-element.32.names, bf16[1024,1152]{1,0:T(8,128)(2,1)S(1)} %get-tuple-element.33.weighted, ...), custom_call_target="tpu_custom_call" | custom-call | flops 2415919104 | bytes 4194304 | tf_op jit(solution)/shard_map/collect/pallas_call | solution.py:455
  46.8 0.6 collective-permute-done.13.rest_3_
  47.4 6.1 %collect.3 = (f32[32,1024]{1,0:T(8,128)S(1)}, f32[32,1024]{1,0:T(8,128)S(1)}, f32[1,1024]{1,0:T(1,128)}) custom-call(s32[1]{0:T(128)} %bitcast.me, s32[1]{0:T(128)} %bitcast.1.here, s32[2,1024]{1,0:T(2,128)S(1)} %get-tuple-element.32.names, bf16[1024,1152]{1,0:T(8,128)(2,1)S(1)} %get-tuple-element.33.weighted, ...), custom_call_target="tpu_custom_call" | custom-call | flops 2415919104 | bytes 4194304 | tf_op jit(solution)/shard_map/collect/pallas_call | solution.py:455
  53.5 1.3 %collective-permute-done.19.right = f32[32,1024]{1,0:T(8,128)S(1)} collective-permute-done((f32[32,1024]{1,0:T(8,128)S(1)}, f32[32,1024]{1,0:T(8,128)S(1)}, u32[]{:S(2)}, u32[]{:S(2)}) %collective-permute-start.19) | collective-permute-done | bytes 131104 | tf_op jit(solution)/shard_map/ppermute | solution.py:515
  54.9 0.7 %collective-permute-start.20 = (f32[8,1024]{1,0:T(8,128)S(1)}, f32[8,1024]{1,0:T(8,128)S(1)}, u32[]{:S(2)}, u32[]{:S(2)}) collective-permute-start(f32[8,1024]{1,0:T(8,128)S(1)} %get-tuple-element.55), channel_id=1, source_target_pairs={{0,2},{1,3},{2,0},{3,1},{4,6},{5,7},{6,4},{7,5},{8,10},{9,11},{10,... | collective-permute-start | bytes 98312 | tf_op jit(solution)/shard_map/ppermute | solution.py:515
  55.6 1.2 %collective-permute-start.21 = (f32[8,1024]{1,0:T(8,128)S(1)}, f32[8,1024]{1,0:T(8,128)S(1)}, u32[]{:S(2)}, u32[]{:S(2)}) collective-permute-start(f32[8,1024]{1,0:T(8,128)S(1)} %get-tuple-element.56), channel_id=1, source_target_pairs={{0,4},{1,5},{2,6},{3,7},{4,0},{5,1},{6,2},{7,3},{8,12},{9,13},{10,... | collective-permute-start | bytes 98312 | tf_op jit(solution)/shard_map/ppermute | solution.py:515
  56.9 2.5 %collective-permute-start.22 = (f32[8,1024]{1,0:T(8,128)S(1)}, f32[8,1024]{1,0:T(8,128)S(1)}, u32[]{:S(2)}, u32[]{:S(2)}) collective-permute-start(f32[8,1024]{1,0:T(8,128)S(1)} %get-tuple-element.57), channel_id=1, source_target_pairs={{0,6},{1,7},{2,4},{3,5},{4,2},{5,3},{6,0},{7,1},{8,14},{9,15},{10,... | collective-permute-start | bytes 98312 | tf_op jit(solution)/shard_map/ppermute | solution.py:515
  59.4 1.1 %collective-permute-done.21.refs_2_ = f32[8,1024]{1,0:T(8,128)S(1)} collective-permute-done((f32[8,1024]{1,0:T(8,128)S(1)}, f32[8,1024]{1,0:T(8,128)S(1)}, u32[]{:S(2)}, u32[]{:S(2)}) %collective-permute-start.21) | collective-permute-done | bytes 32800 | tf_op jit(solution)/shard_map/ppermute | solution.py:515
  60.5 2.1 %collective-permute-done.22.refs_3_ = f32[8,1024]{1,0:T(8,128)S(1)} collective-permute-done((f32[8,1024]{1,0:T(8,128)S(1)}, f32[8,1024]{1,0:T(8,128)S(1)}, u32[]{:S(2)}, u32[]{:S(2)}) %collective-permute-start.22) | collective-permute-done | bytes 32800 | tf_op jit(solution)/shard_map/ppermute | solution.py:515
  62.6 0.6 finish.1
  (46 shorter events, 2.1 us)
Async XLA Ops:
  0.6 10.4 %copy-start.4 = (bf16[4,1024]{1,0:T(4,128)(2,1)S(1)}, bf16[4,1024]{1,0:T(4,128)(2,1)}, u32[]{:S(2)}) copy-start(bf16[4,1024]{1,0:T(4,128)(2,1)} %own_in.1) | copy-start | bytes 24580
  0.6 10.4 %copy-start.1 = (bf16[64,64,64]{2,1,0:T(8,128)(2,1)S(1)}, bf16[64,64,64]{2,1,0:T(8,128)(2,1)}, u32[]{:S(2)}) copy-start(bf16[64,64,64]{2,1,0:T(8,128)(2,1)} %turns.1) | copy-start | bytes 1572868
  0.7 10.4 %copy-start.2 = (f32[32,1024]{1,0:T(8,128)S(1)}, f32[32,1024]{1,0:T(8,128)}, u32[]{:S(2)}) copy-start(f32[32,1024]{1,0:T(8,128)} %table.1) | copy-start | bytes 393220
  0.7 10.4 %copy-start.5 = (s32[1024]{0:T(1024)S(1)}, s32[1024]{0:T(1024)}, u32[]{:S(2)}) copy-start(s32[1024]{0:T(1024)} %param.8) | copy-start | bytes 12292
  0.7 10.4 %copy-start.3 = (s32[1024,2]{0,1:T(2,128)S(1)}, s32[1024,2]{0,1:T(2,128)}, u32[]{:S(2)}) copy-start(s32[1024,2]{0,1:T(2,128)} %param.7) | copy-start | bytes 24580
  0.7 10.4 %copy-start = (bf16[1024,1024]{1,0:T(8,128)(2,1)S(1)}, bf16[1024,1024]{1,0:T(8,128)(2,1)}, u32[]{:S(2)}) copy-start(bf16[1024,1024]{1,0:T(8,128)(2,1)} %pixels.1) | copy-start | bytes 6291460
  0.7 5.7 %collective-permute-start.1 = (bf16[4,1024]{1,0:T(4,128)(2,1)}, bf16[4,1024]{1,0:T(4,128)(2,1)S(1)}, u32[]{:S(2)}, u32[]{:S(2)}) collective-permute-start(bf16[4,1024]{1,0:T(4,128)(2,1)} %own_in.1), channel_id=1, source_target_pairs={{0,2},{1,3},{2,0},{3,1},{4,6},{5,7},{6,4},{7,5},{8,10},{9,11},{10,... | collective-permute-start | bytes 24584 | tf_op jit(solution)/shard_map/ppermute | solution.py:515
  3.8 5.7 %collective-permute-start.5 = (bf16[4,1024]{1,0:T(4,128)(2,1)}, bf16[4,1024]{1,0:T(4,128)(2,1)S(1)}, u32[]{:S(2)}, u32[]{:S(2)}) collective-permute-start(bf16[4,1024]{1,0:T(4,128)(2,1)} %own_in.1), channel_id=1, source_target_pairs={{0,6},{1,7},{2,4},{3,5},{4,2},{5,3},{6,0},{7,1},{8,14},{9,15},{10,... | collective-permute-start | bytes 24584 | tf_op jit(solution)/shard_map/ppermute | solution.py:515
  6.3 4.8 %collective-permute-start.3 = (bf16[4,1024]{1,0:T(4,128)(2,1)}, bf16[4,1024]{1,0:T(4,128)(2,1)S(1)}, u32[]{:S(2)}, u32[]{:S(2)}) collective-permute-start(bf16[4,1024]{1,0:T(4,128)(2,1)} %own_in.1), channel_id=1, source_target_pairs={{0,4},{1,5},{2,6},{3,7},{4,0},{5,1},{6,2},{7,3},{8,12},{9,13},{10,... | collective-permute-start | bytes 24584 | tf_op jit(solution)/shard_map/ppermute | solution.py:515
  6.4 5.5 %collective-permute-start = (bf16[4,1024]{1,0:T(4,128)(2,1)}, bf16[4,1024]{1,0:T(4,128)(2,1)S(1)}, u32[]{:S(2)}, u32[]{:S(2)}) collective-permute-start(bf16[4,1024]{1,0:T(4,128)(2,1)} %own_in.1), channel_id=1, source_target_pairs={{0,1},{1,0},{2,3},{3,2},{4,5},{5,4},{6,7},{7,6},{8,9},{9,8},{10,11... | collective-permute-start | bytes 24584 | tf_op jit(solution)/shard_map/ppermute | solution.py:515
  6.4 5.5 %collective-permute-start.2 = (bf16[4,1024]{1,0:T(4,128)(2,1)S(1)}, bf16[4,1024]{1,0:T(4,128)(2,1)S(1)}, u32[]{:S(2)}, u32[]{:S(2)}) collective-permute-start(bf16[4,1024]{1,0:T(4,128)(2,1)S(1)} %collective-permute-done.1.rest_2_), channel_id=1, source_target_pairs={{0,1},{1,0},{2,3},{3,2},{4,5},{5,4},{6,7},{7,6},{8,9},{9,8},{10,11... | collective-permute-start | bytes 24584 | tf_op jit(solution)/shard_map/ppermute | solution.py:515
  9.5 2.4 %collective-permute-start.6 = (bf16[4,1024]{1,0:T(4,128)(2,1)S(1)}, bf16[4,1024]{1,0:T(4,128)(2,1)S(1)}, u32[]{:S(2)}, u32[]{:S(2)}) collective-permute-start(bf16[4,1024]{1,0:T(4,128)(2,1)S(1)} %collective-permute-done.5.rest_6_), channel_id=1, source_target_pairs={{0,1},{1,0},{2,3},{3,2},{4,5},{5,4},{6,7},{7,6},{8,9},{9,8},{10,11... | collective-permute-start | bytes 24584 | tf_op jit(solution)/shard_map/ppermute | solution.py:515
  11.0 1.2 %collective-permute-start.4 = (bf16[4,1024]{1,0:T(4,128)(2,1)S(1)}, bf16[4,1024]{1,0:T(4,128)(2,1)S(1)}, u32[]{:S(2)}, u32[]{:S(2)}) collective-permute-start(bf16[4,1024]{1,0:T(4,128)(2,1)S(1)} %collective-permute-done.3.rest_4_), channel_id=1, source_target_pairs={{0,1},{1,0},{2,3},{3,2},{4,5},{5,4},{6,7},{7,6},{8,9},{9,8},{10,11... | collective-permute-start | bytes 24584 | tf_op jit(solution)/shard_map/ppermute | solution.py:515
  19.9 9.8 %collective-permute-start.9 = (f16[512,128]{1,0:T(8,128)(2,1)S(1)}, f16[512,128]{1,0:T(8,128)(2,1)S(1)}, u32[]{:S(2)}, u32[]{:S(2)}) collective-permute-start(f16[512,128]{1,0:T(8,128)(2,1)S(1)} %convert_element_type.40), channel_id=1, source_target_pairs={{0,24},{8,16},{16,8},{24,0},{1,25},{9,17},{17,9},{25,1},{2,26},{10... | collective-permute-start | bytes 393224 | tf_op jit(solution)/shard_map/ppermute | solution.py:515
  22.4 7.8 %collective-permute-start.8 = (f16[512,128]{1,0:T(8,128)(2,1)S(1)}, f16[512,128]{1,0:T(8,128)(2,1)S(1)}, u32[]{:S(2)}, u32[]{:S(2)}) collective-permute-start(f16[512,128]{1,0:T(8,128)(2,1)S(1)} %convert_element_type.38), channel_id=1, source_target_pairs={{0,16},{8,24},{16,0},{24,8},{1,17},{9,25},{17,1},{25,9},{2,18},{10... | collective-permute-start | bytes 393224 | tf_op jit(solution)/shard_map/ppermute | solution.py:515
  22.9 7.3 %collective-permute-start.7 = (f16[512,128]{1,0:T(8,128)(2,1)S(1)}, f16[512,128]{1,0:T(8,128)(2,1)S(1)}, u32[]{:S(2)}, u32[]{:S(2)}) collective-permute-start(f16[512,128]{1,0:T(8,128)(2,1)S(1)} %convert_element_type.36), channel_id=1, source_target_pairs={{0,8},{8,0},{16,24},{24,16},{1,9},{9,1},{17,25},{25,17},{2,10},{10... | collective-permute-start | bytes 393224 | tf_op jit(solution)/shard_map/ppermute | solution.py:515
  26.6 6.8 %collective-permute-start.12 = (f16[512,128]{1,0:T(8,128)(2,1)S(1)}, f16[512,128]{1,0:T(8,128)(2,1)S(1)}, u32[]{:S(2)}, u32[]{:S(2)}) collective-permute-start(f16[512,128]{1,0:T(8,128)(2,1)S(1)} %convert_element_type.46), channel_id=1, source_target_pairs={{0,24},{8,16},{16,8},{24,0},{1,25},{9,17},{17,9},{25,1},{2,26},{10... | collective-permute-start | bytes 393224 | tf_op jit(solution)/shard_map/ppermute | solution.py:515
  29.1 8.2 %collective-permute-start.11 = (f16[512,128]{1,0:T(8,128)(2,1)S(1)}, f16[512,128]{1,0:T(8,128)(2,1)S(1)}, u32[]{:S(2)}, u32[]{:S(2)}) collective-permute-start(f16[512,128]{1,0:T(8,128)(2,1)S(1)} %convert_element_type.44), channel_id=1, source_target_pairs={{0,16},{8,24},{16,0},{24,8},{1,17},{9,25},{17,1},{25,9},{2,18},{10... | collective-permute-start | bytes 393224 | tf_op jit(solution)/shard_map/ppermute | solution.py:515
  29.6 7.7 %collective-permute-start.10 = (f16[512,128]{1,0:T(8,128)(2,1)S(1)}, f16[512,128]{1,0:T(8,128)(2,1)S(1)}, u32[]{:S(2)}, u32[]{:S(2)}) collective-permute-start(f16[512,128]{1,0:T(8,128)(2,1)S(1)} %convert_element_type.42), channel_id=1, source_target_pairs={{0,8},{8,0},{16,24},{24,16},{1,9},{9,1},{17,25},{25,17},{2,10},{10... | collective-permute-start | bytes 393224 | tf_op jit(solution)/shard_map/ppermute | solution.py:515
  30.4 11.9 %collective-permute-start.18 = (bf16[528,128]{1,0:T(8,128)(2,1)S(1)}, bf16[528,128]{1,0:T(8,128)(2,1)S(1)}, u32[]{:S(2)}, u32[]{:S(2)}) collective-permute-start(bf16[528,128]{1,0:T(8,128)(2,1)S(1)} %soften.2.after.rest_0_), channel_id=1, source_target_pairs={{0,24},{8,16},{16,8},{24,0},{1,25},{9,17},{17,9},{25,1},{2,26},{10... | collective-permute-start | bytes 405512 | tf_op jit(solution)/shard_map/ppermute | solution.py:515
  32.9 10.4 %collective-permute-start.17 = (bf16[528,128]{1,0:T(8,128)(2,1)S(1)}, bf16[528,128]{1,0:T(8,128)(2,1)S(1)}, u32[]{:S(2)}, u32[]{:S(2)}) collective-permute-start(bf16[528,128]{1,0:T(8,128)(2,1)S(1)} %soften.2.after.rest_0_), channel_id=1, source_target_pairs={{0,16},{8,24},{16,0},{24,8},{1,17},{9,25},{17,1},{25,9},{2,18},{10... | collective-permute-start | bytes 405512 | tf_op jit(solution)/shard_map/ppermute | solution.py:515
  33.4 9.9 %collective-permute-start.16 = (bf16[528,128]{1,0:T(8,128)(2,1)S(1)}, bf16[528,128]{1,0:T(8,128)(2,1)S(1)}, u32[]{:S(2)}, u32[]{:S(2)}) collective-permute-start(bf16[528,128]{1,0:T(8,128)(2,1)S(1)} %soften.2.after.rest_0_), channel_id=1, source_target_pairs={{0,8},{8,0},{16,24},{24,16},{1,9},{9,1},{17,25},{25,17},{2,10},{10... | collective-permute-start | bytes 405512 | tf_op jit(solution)/shard_map/ppermute | solution.py:515
  37.5 9.1 %collective-permute-start.15 = (bf16[528,128]{1,0:T(8,128)(2,1)S(1)}, bf16[528,128]{1,0:T(8,128)(2,1)S(1)}, u32[]{:S(2)}, u32[]{:S(2)}) collective-permute-start(bf16[528,128]{1,0:T(8,128)(2,1)S(1)} %soften.3.rest_2_), channel_id=1, source_target_pairs={{0,24},{8,16},{16,8},{24,0},{1,25},{9,17},{17,9},{25,1},{2,26},{10... | collective-permute-start | bytes 405512 | tf_op jit(solution)/shard_map/ppermute | solution.py:515
  39.6 7.2 %collective-permute-start.14 = (bf16[528,128]{1,0:T(8,128)(2,1)S(1)}, bf16[528,128]{1,0:T(8,128)(2,1)S(1)}, u32[]{:S(2)}, u32[]{:S(2)}) collective-permute-start(bf16[528,128]{1,0:T(8,128)(2,1)S(1)} %soften.3.rest_2_), channel_id=1, source_target_pairs={{0,16},{8,24},{16,0},{24,8},{1,17},{9,25},{17,1},{25,9},{2,18},{10... | collective-permute-start | bytes 405512 | tf_op jit(solution)/shard_map/ppermute | solution.py:515
  42.3 5.1 %collective-permute-start.13 = (bf16[528,128]{1,0:T(8,128)(2,1)S(1)}, bf16[528,128]{1,0:T(8,128)(2,1)S(1)}, u32[]{:S(2)}, u32[]{:S(2)}) collective-permute-start(bf16[528,128]{1,0:T(8,128)(2,1)S(1)} %soften.3.rest_2_), channel_id=1, source_target_pairs={{0,8},{8,0},{16,24},{24,16},{1,9},{9,1},{17,25},{25,17},{2,10},{10... | collective-permute-start | bytes 405512 | tf_op jit(solution)/shard_map/ppermute | solution.py:515
  53.5 1.3 %collective-permute-start.19 = (f32[32,1024]{1,0:T(8,128)S(1)}, f32[32,1024]{1,0:T(8,128)S(1)}, u32[]{:S(2)}, u32[]{:S(2)}) collective-permute-start(f32[32,1024]{1,0:T(8,128)S(1)} %get-tuple-element.53), channel_id=1, source_target_pairs={{0,1},{1,0},{2,3},{3,2},{4,5},{5,4},{6,7},{7,6},{8,9},{9,8},{10,11... | collective-permute-start | bytes 393224 | tf_op jit(solution)/shard_map/ppermute | solution.py:515
  54.9 4.5 %collective-permute-start.20 = (f32[8,1024]{1,0:T(8,128)S(1)}, f32[8,1024]{1,0:T(8,128)S(1)}, u32[]{:S(2)}, u32[]{:S(2)}) collective-permute-start(f32[8,1024]{1,0:T(8,128)S(1)} %get-tuple-element.55), channel_id=1, source_target_pairs={{0,2},{1,3},{2,0},{3,1},{4,6},{5,7},{6,4},{7,5},{8,10},{9,11},{10,... | collective-permute-start | bytes 98312 | tf_op jit(solution)/shard_map/ppermute | solution.py:515
  55.6 4.8 %collective-permute-start.21 = (f32[8,1024]{1,0:T(8,128)S(1)}, f32[8,1024]{1,0:T(8,128)S(1)}, u32[]{:S(2)}, u32[]{:S(2)}) collective-permute-start(f32[8,1024]{1,0:T(8,128)S(1)} %get-tuple-element.56), channel_id=1, source_target_pairs={{0,4},{1,5},{2,6},{3,7},{4,0},{5,1},{6,2},{7,3},{8,12},{9,13},{10,... | collective-permute-start | bytes 98312 | tf_op jit(solution)/shard_map/ppermute | solution.py:515
  56.9 5.7 %collective-permute-start.22 = (f32[8,1024]{1,0:T(8,128)S(1)}, f32[8,1024]{1,0:T(8,128)S(1)}, u32[]{:S(2)}, u32[]{:S(2)}) collective-permute-start(f32[8,1024]{1,0:T(8,128)S(1)} %get-tuple-element.57), channel_id=1, source_target_pairs={{0,6},{1,7},{2,4},{3,5},{4,2},{5,3},{6,0},{7,1},{8,14},{9,15},{10,... | collective-permute-start | bytes 98312 | tf_op jit(solution)/shard_map/ppermute | solution.py:515

commit v6 on v5

--- a/solution.py
+++ b/solution.py
@@ -12,7 +12,7 @@
 VMEM = pl.BlockSpec(memory_space=pltpu.VMEM)
 SMEM = pl.BlockSpec(memory_space=pltpu.SMEM)
 LANES, ROWS = 128, 8
-PREPARE = 1 << 20
+PREPARE = 4_000_000_000
 EARLY = 20_000_000_000
 NN = (((1,), (0,)), ((), ()))
 NT = (((1,), (1,)), ((), ()))
@@ -121,7 +121,8 @@
     )(seed(), references, particles, turns, table, kind, names)
 
 
-def prepare_kernel(pack, after, turns, power, matrix, response):
+def prepare_kernel(pack, after, turns, power, matrix, response, sign):
+    sign[...] = jnp.zeros_like(sign)
     turn_count, angles, _ = turns.shape
     kinds, width = power.shape[0] // 2, power.shape[1]
     tiles = width // LANES
@@ -153,10 +154,11 @@
     return pl.pallas_call(
         functools.partial(prepare_kernel, pack),
         in_specs=[VMEM] * 3,
-        out_specs=[VMEM] * 2,
+        out_specs=[VMEM] * 3,
         out_shape=[
             jax.ShapeDtypeStruct((steps * LANES, pack * LANES), bf16),
             jax.ShapeDtypeStruct((steps * kinds, pack * pixels), bf16),
+            jax.ShapeDtypeStruct((ROWS, LANES), f32),
         ],
         name="prepare",
         **limits(16, PREPARE, 0),
@@ -222,11 +224,11 @@
 
     spread = lax.broadcasted_iota(jnp.int32, (kinds, LANES), 0) == lax.broadcasted_iota(jnp.int32, (kinds, LANES), 1)
     mean[...] = jnp.sum(jnp.where(spread, center[...], 0.0), axis=0, keepdims=True)
-    blank = jnp.zeros((LANES - 3 * kinds, LANES), f32)
+    blank = jnp.zeros((LANES, LANES - 2 * kinds), bf16)
     for i in range(pairs // LANES):
         at = slice(i * LANES, (i + 1) * LANES)
-        parts = [part.astype(f32) for part in split(energy[:, at] - center[...], 3)]
-        rotated[at, pixels:] = jnp.concatenate(parts + [blank], axis=0).T.astype(bf16)
+        parts = jnp.concatenate(split(energy[:, at] - center[...], 2), axis=0).T
+        rotated[at, pixels:] = jnp.concatenate([parts, blank], axis=1)
 
 
 def rotate(refs, turns, power2, pack, groups):
@@ -303,7 +305,8 @@
     )(me, here, weighted, names, rotated)
 
 
-def soften_kernel(scores, mean, out):
+def soften_kernel(scores, mean, *rest):
+    out = rest[-1]
     value = scores[...]
     rows, share = value.shape
     top = jnp.max(value, axis=0, keepdims=True)
@@ -320,16 +323,16 @@
     out[rows:, :] = tail.astype(bf16)
 
 
-def soften(scores, mean):
+def soften(scores, mean, *after):
     rows, share = scores.shape
     return pl.pallas_call(
         soften_kernel,
-        in_specs=[VMEM, VMEM],
+        in_specs=[VMEM] * (2 + len(after)),
         out_specs=VMEM,
         out_shape=jax.ShapeDtypeStruct((rows + 2 * ROWS, share), bf16),
         name="soften",
         **limits(8, 4 * rows * share, 6 * rows * share, rows * share),
-    )(scores, mean)
+    )(scores, mean, *after)
 
 
 def collect_kernel(groups, parts, turn_count, kinds, scale, begin, peers, first, last, me, here, names, weighted, *rest):
@@ -371,6 +374,10 @@
         if not first:
             logs[:, :begin] = before[2][:, :begin]
 
+    halves = 2 if groups % 4 == 0 else 1
+    span = groups // halves
+    row_of = lambda t, g: ((g // span * tiles + t) * span + g % span) * ROWS
+    totals = []
     zero = jnp.zeros((), bf16)
     for g in range(0, groups, 2):
         dense = []
@@ -389,7 +396,7 @@
                     for q in range(2)
                 ]
                 pair = jnp.concatenate(pair, axis=0)
-                at = slice((t * groups + g) * ROWS, (t * groups + g + 2) * ROWS)
+                at = slice(row_of(t, g), row_of(t, g) + 2 * ROWS)
                 if not first:
                     pair = pair + before[0][at, lanes]
                 lhs[at, lanes] = pair.astype(lhs.dtype)
@@ -397,11 +404,13 @@
                 by_kind[(g + q) * ROWS:(g + q + 1) * ROWS, i * kinds:(i + 1) * kinds] = value[
                     q * pairs + i * ROWS:q * pairs + (i + 1) * ROWS, pixels:pixels + kinds
                 ]
+        if last and (g + 2) % span == 0:
+            at = slice(len(totals) * tiles * span * ROWS, (len(totals) + 1) * tiles * span * ROWS)
+            totals.append(dot(lhs[at, :], matrix[...], NN))
     if not last:
         if not first:
             by_kind[...] = by_kind[...] + before[1][...]
         return
-    total = dot(lhs[...], matrix[...], NN)
     light = by_kind[...] if first else by_kind[...] + before[1][...]
     heavy = dot(jnp.concatenate(split(light, 2), axis=0), response[...], NN)
     heavy = heavy[:groups * ROWS] + heavy[groups * ROWS:]
@@ -417,8 +426,8 @@
         part, to = g % parts, slice(g // parts * ROWS, (g // parts + 1) * ROWS)
         for t in range(tiles):
             lanes = slice(t * LANES, (t + 1) * LANES)
-            at = slice((t * groups + g) * ROWS, (t * groups + g + 1) * ROWS)
-            top = fold([total[at, j * LANES:(j + 1) * LANES] for j in range(pack)])
+            at = slice((t * span + g % span) * ROWS, (t * span + g % span + 1) * ROWS)
+            top = fold([totals[g // span][at, j * LANES:(j + 1) * LANES] for j in range(pack)])
             at = slice(g * ROWS, (g + 1) * ROWS)
             low = fold(
                 [heavy[at, j * pixels + t * LANES:j * pixels + (t + 1) * LANES] for j in range(pack)]
@@ -540,15 +549,16 @@
     rotated, mean = rotate(refs, turns2, power2, pack, groups)
     chunks = 2
     size = count // chunks
-    blocks = []
+    blocks, signs = [], []
     for c in range(chunks):
         cut = score(c * size, size, weighted, names, rotated, me, here, peers, group_pairs, groups, scale)
         total = cut[0]
         for k in range(1, peers):
             total = total + swap(cut[k].astype(jnp.float16), "cls", k).astype(f32)
-        own = soften(total, mean)
+        own = soften(total, mean, *signs)
+        if c == 0:
+            matrix, response, *signs = prepare(turns2, power2, pack, own)
         blocks.append([own] + [swap(own, "cls", k) for k in range(1, peers)])
-    matrix, response = prepare(turns2, power2, pack, blocks[0][0])
     parts = 2 if paired else 1
     out = []
     for c in range(chunks):

time: 63.4 us -> 61.9 us (0.976)
  starting transfers between devices: 26.4 us -> 24.9 us
  waiting for transfers between devices: 12.3 us -> 13.3 us
  Pallas kernels: 23.3 us -> 22.4 us
    ppermute x23, starting transfers between devices: 26.4 us -> 24.9 us  [swap(): lax.ppermute(x, axis, [(i, i ^ k) for i in range(lax.axis_size(axis))])]
    ppermute x23, waiting for transfers between devices: 12.3 us -> 13.3 us  [swap(): lax.ppermute(x, axis, [(i, i ^ k) for i in range(lax.axis_size(axis))])]
    pallas_call x2, Pallas kernels: 9.39 us -> 8.69 us  [collect(): pl.pallas_call(functools.partial(collect_kernel, groups, parts, turn_coun...]
  transfers between devices with their start and end apart: 23 -> 23, of which waited for: 10 -> 10; matrix products, arithmetic and copies ran while one was open for 0% -> 0% of each run, Pallas kernels for 14% -> 15%
where the time goes in v6:
time: 61.9 us; the launch traced here: 61.8 us
  starting transfers between devices  24.9 us (40%)
  Pallas kernels  22.4 us (36%)
  waiting for transfers between devices  13.3 us (21%)
  between operations  0.9 us (1%)
    ppermute x23, starting transfers between devices, swap(): lax.ppermute(x, axis, [(i, i ^ k) for i in range(lax.axis_size(axis))])  24.9 us
    ppermute x23, waiting for transfers between devices, swap(): lax.ppermute(x, axis, [(i, i ^ k) for i in range(lax.axis_size(axis))])  13.3 us
    pallas_call x2, Pallas kernels, collect(): pl.pallas_call(functools.partial(collect_kernel, groups, parts, turn_coun...  8.69 us
    pallas_call x2, Pallas kernels, score(): pl.pallas_call(functools.partial(score_kernel, groups, scale, begin), gri...  6.22 us
    pallas_call x1, Pallas kernels, rotate(): pl.pallas_call(functools.partial(rotate_kernel, groups, pack), grid=(step...  4.23 us
    pallas_call x1, Pallas kernels, prepare(): pl.pallas_call(functools.partial(prepare_kernel, pack), in_specs=[VMEM] *...  1.49 us
  transfers between devices with their start and end apart: 23, of which 10 were waited for; matrix products, arithmetic and copies ran while one was open for 0% of the time, Pallas kernels for 15%

profile of v6, /device:TPU:0, one launch (start us, length us, event | category | flops | bytes accessed | tf_op | source)
XLA Modules:
  0.0 61.8 jit_solution(6634461409968145795)
XLA Ops:
  0.7 3.1 %collective-permute-start.1 = (bf16[4,1024]{1,0:T(4,128)(2,1)}, bf16[4,1024]{1,0:T(4,128)(2,1)S(1)}, u32[]{:S(2)}, u32[]{:S(2)}) collective-permute-start(bf16[4,1024]{1,0:T(4,128)(2,1)} %own_in.1), channel_id=1, source_target_pairs={{0,2},{1,3},{2,0},{3,1},{4,6},{5,7},{6,4},{7,5},{8,10},{9,11},{10,... | collective-permute-start | bytes 24584 | tf_op jit(solution)/shard_map/ppermute | solution.py:524
  3.8 2.5 %collective-permute-start.5 = (bf16[4,1024]{1,0:T(4,128)(2,1)}, bf16[4,1024]{1,0:T(4,128)(2,1)S(1)}, u32[]{:S(2)}, u32[]{:S(2)}) collective-permute-start(bf16[4,1024]{1,0:T(4,128)(2,1)} %own_in.1), channel_id=1, source_target_pairs={{0,6},{1,7},{2,4},{3,5},{4,2},{5,3},{6,0},{7,1},{8,14},{9,15},{10,... | collective-permute-start | bytes 24584 | tf_op jit(solution)/shard_map/ppermute | solution.py:524
  6.4 0.5 collective-permute-start.2
  6.9 2.6 %collective-permute-done.5.rest_6_ = bf16[4,1024]{1,0:T(4,128)(2,1)S(1)} collective-permute-done((bf16[4,1024]{1,0:T(4,128)(2,1)}, bf16[4,1024]{1,0:T(4,128)(2,1)S(1)}, u32[]{:S(2)}, u32[]{:S(2)}) %collective-permute-start.5) | collective-permute-done | bytes 8224 | tf_op jit(solution)/shard_map/ppermute | solution.py:524
  9.5 1.5 %collective-permute-done.3.rest_4_ = bf16[4,1024]{1,0:T(4,128)(2,1)S(1)} collective-permute-done((bf16[4,1024]{1,0:T(4,128)(2,1)}, bf16[4,1024]{1,0:T(4,128)(2,1)S(1)}, u32[]{:S(2)}, u32[]{:S(2)}) %collective-permute-start.3) | collective-permute-done | bytes 8224 | tf_op jit(solution)/shard_map/ppermute | solution.py:524
  11.1 0.8 %start.1 = (bf16[1024,1152]{1,0:T(8,128)(2,1)S(1)}, bf16[64,1024]{1,0:T(8,128)(2,1)S(1)}, s32[2,1024]{1,0:T(2,128)S(1)}, bf16[4,1024]{1,0:T(4,128)(2,1)S(1)}, bf16[64,64,128]{2,1,0:T(8,128)(2,1)S(1)}) custom-call(s32[128,256]{1,0:T(8,128)S(1)} %seed.1.numbers, bf16[4,1024]{1,0:T(4,128)(2,1)S(1)} %copy-done.4, bf16[1024,1024]{1,0:T(8,128)(2,1)S(1)} %copy-done, ...), custom_call_target="tpu_custom_call" | custom-call | flops 1048576 | tf_op jit(solution)/shard_map/start/pallas_call | solution.py:108
  12.2 4.2 %rotate.1 = (bf16[2048,1152]{1,0:T(8,128)(2,1)S(1)}, f32[1,128]{1,0:T(1,128)S(1)}) custom-call(bf16[64,1024]{1,0:T(8,128)(2,1)S(1)} %get-tuple-element.35.power2.power, bf16[64,64,128]{2,1,0:T(8,128)(2,1)S(1)} %get-tuple-element.36.turns, bf16[4,1024]{1,0:T(4,128)(2,1)S(1)} %get-tuple-element.37.rest_0_, bf16[4,1024]{1,0:T(4,128)(2,1)S(1)} %collective-permute-done.rest_1_, ...), custom_call_target="tpu_custom_call" | custom-call | flops 1073741824 | bytes 4194304 | tf_op jit(solution)/shard_map/rotate/pallas_call | solution.py:241
  16.4 3.1 %score.2 = (f32[512,128]{1,0:T(8,128)S(1)}, f32[512,128]{1,0:T(8,128)S(1)}, f32[512,128]{1,0:T(8,128)S(1)}, f32[512,128]{1,0:T(8,128)S(1)}) custom-call(s32[1]{0:T(128)} %bitcast.me, s32[1]{0:T(128)} %bitcast.1.here, bf16[1024,1152]{1,0:T(8,128)(2,1)S(1)} %get-tuple-element.34.weighted, s32[2,1024]{1,0:T(2,128)S(1)} %get-tuple-element.33.names, ...), custom_call_target="tpu_custom_call" | custom-call | flops 2415919104 | bytes 4718592 | tf_op jit(solution)/shard_map/score/pallas_call | solution.py:290
  19.6 2.5 %collective-permute-start.9 = (f16[512,128]{1,0:T(8,128)(2,1)S(1)}, f16[512,128]{1,0:T(8,128)(2,1)S(1)}, u32[]{:S(2)}, u32[]{:S(2)}) collective-permute-start(f16[512,128]{1,0:T(8,128)(2,1)S(1)} %convert_element_type.40), channel_id=1, source_target_pairs={{0,24},{8,16},{16,8},{24,0},{1,25},{9,17},{17,9},{25,1},{2,26},{10... | collective-permute-start | bytes 393224 | tf_op jit(solution)/shard_map/ppermute | solution.py:524
  22.1 0.5 collective-permute-start.8
  22.7 0.5 collective-permute-start.7
  23.2 3.1 %score.3 = (f32[512,128]{1,0:T(8,128)S(1)}, f32[512,128]{1,0:T(8,128)S(1)}, f32[512,128]{1,0:T(8,128)S(1)}, f32[512,128]{1,0:T(8,128)S(1)}) custom-call(s32[1]{0:T(128)} %bitcast.me, s32[1]{0:T(128)} %bitcast.1.here, bf16[1024,1152]{1,0:T(8,128)(2,1)S(1)} %get-tuple-element.34.weighted, s32[2,1024]{1,0:T(2,128)S(1)} %get-tuple-element.33.names, ...), custom_call_target="tpu_custom_call" | custom-call | flops 2415919104 | bytes 4718592 | tf_op jit(solution)/shard_map/score/pallas_call | solution.py:290
  26.4 2.5 %collective-permute-start.12 = (f16[512,128]{1,0:T(8,128)(2,1)S(1)}, f16[512,128]{1,0:T(8,128)(2,1)S(1)}, u32[]{:S(2)}, u32[]{:S(2)}) collective-permute-start(f16[512,128]{1,0:T(8,128)(2,1)S(1)} %convert_element_type.46), channel_id=1, source_target_pairs={{0,24},{8,16},{16,8},{24,0},{1,25},{9,17},{17,9},{25,1},{2,26},{10... | collective-permute-start | bytes 393224 | tf_op jit(solution)/shard_map/ppermute | solution.py:524
  28.9 0.5 collective-permute-start.11
  29.4 0.5 collective-permute-start.10
  30.2 2.5 %collective-permute-start.18 = (bf16[528,128]{1,0:T(8,128)(2,1)S(1)}, bf16[528,128]{1,0:T(8,128)(2,1)S(1)}, u32[]{:S(2)}, u32[]{:S(2)}) collective-permute-start(bf16[528,128]{1,0:T(8,128)(2,1)S(1)} %soften.2.after.rest_0_), channel_id=1, source_target_pairs={{0,24},{8,16},{16,8},{24,0},{1,25},{9,17},{17,9},{25,1},{2,26},{10... | collective-permute-start | bytes 405512 | tf_op jit(solution)/shard_map/ppermute | solution.py:524
  32.7 0.5 collective-permute-start.17
  33.2 1.5 %prepare.1 = (bf16[4096,256]{1,0:T(8,128)(2,1)S(1)}, bf16[1024,2048]{1,0:T(8,128)(2,1)S(1)}, f32[8,128]{1,0:T(8,128)S(1)}) custom-call(bf16[528,128]{1,0:T(8,128)(2,1)S(1)} %soften.2.after.rest_0_, bf16[64,64,128]{2,1,0:T(8,128)(2,1)S(1)} %get-tuple-element.36.turns, bf16[64,1024]{1,0:T(8,128)(2,1)S(1)} %get-tuple-element.35.power2.power), custom_call_target="tpu_custom_call" | custom-call | flops 4000000000 | tf_op jit(solution)/shard_map/prepare/pallas_call | solution.py:154
  34.7 0.6 collective-permute-start.16
  35.3 1.8 %collective-permute-done.11 = f16[512,128]{1,0:T(8,128)(2,1)S(1)} collective-permute-done((f16[512,128]{1,0:T(8,128)(2,1)S(1)}, f16[512,128]{1,0:T(8,128)(2,1)S(1)}, u32[]{:S(2)}, u32[]{:S(2)}) %collective-permute-start.11) | collective-permute-done | bytes 131104 | tf_op jit(solution)/shard_map/ppermute | solution.py:524
  37.4 2.0 %collective-permute-start.15 = (bf16[528,128]{1,0:T(8,128)(2,1)S(1)}, bf16[528,128]{1,0:T(8,128)(2,1)S(1)}, u32[]{:S(2)}, u32[]{:S(2)}) collective-permute-start(bf16[528,128]{1,0:T(8,128)(2,1)S(1)} %soften.3.rest_2_), channel_id=1, source_target_pairs={{0,24},{8,16},{16,8},{24,0},{1,25},{9,17},{17,9},{25,1},{2,26},{10... | collective-permute-start | bytes 405512 | tf_op jit(solution)/shard_map/ppermute | solution.py:524
  39.4 1.2 %collective-permute-start.14 = (bf16[528,128]{1,0:T(8,128)(2,1)S(1)}, bf16[528,128]{1,0:T(8,128)(2,1)S(1)}, u32[]{:S(2)}, u32[]{:S(2)}) collective-permute-start(bf16[528,128]{1,0:T(8,128)(2,1)S(1)} %soften.3.rest_2_), channel_id=1, source_target_pairs={{0,16},{8,24},{16,0},{24,8},{1,17},{9,25},{17,1},{25,9},{2,18},{10... | collective-permute-start | bytes 405512 | tf_op jit(solution)/shard_map/ppermute | solution.py:524
  40.9 2.2 %collective-permute-done.17.rest_2_ = bf16[528,128]{1,0:T(8,128)(2,1)S(1)} collective-permute-done((bf16[528,128]{1,0:T(8,128)(2,1)S(1)}, bf16[528,128]{1,0:T(8,128)(2,1)S(1)}, u32[]{:S(2)}, u32[]{:S(2)}) %collective-permute-start.17) | collective-permute-done | bytes 135200 | tf_op jit(solution)/shard_map/ppermute | solution.py:524
  43.1 3.3 %collect.2 = (f32[512,4096]{1,0:T(8,128)S(1)}, f32[64,1024]{1,0:T(8,128)S(1)}, f32[1,1024]{1,0:T(1,128)S(1)}) custom-call(s32[1]{0:T(128)} %bitcast.me, s32[1]{0:T(128)} %bitcast.1.here, s32[2,1024]{1,0:T(2,128)S(1)} %get-tuple-element.33.names, bf16[1024,1152]{1,0:T(8,128)(2,1)S(1)} %get-tuple-element.34.weighted, ...), custom_call_target="tpu_custom_call" | custom-call | flops 2415919104 | bytes 4194304 | tf_op jit(solution)/shard_map/collect/pallas_call | solution.py:464
  46.7 5.4 %collect.3 = (f32[32,1024]{1,0:T(8,128)S(1)}, f32[32,1024]{1,0:T(8,128)S(1)}, f32[1,1024]{1,0:T(1,128)}) custom-call(s32[1]{0:T(128)} %bitcast.me, s32[1]{0:T(128)} %bitcast.1.here, s32[2,1024]{1,0:T(2,128)S(1)} %get-tuple-element.33.names, bf16[1024,1152]{1,0:T(8,128)(2,1)S(1)} %get-tuple-element.34.weighted, ...), custom_call_target="tpu_custom_call" | custom-call | flops 2415919104 | bytes 4194304 | tf_op jit(solution)/shard_map/collect/pallas_call | solution.py:464
  52.1 1.3 %collective-permute-done.19.right = f32[32,1024]{1,0:T(8,128)S(1)} collective-permute-done((f32[32,1024]{1,0:T(8,128)S(1)}, f32[32,1024]{1,0:T(8,128)S(1)}, u32[]{:S(2)}, u32[]{:S(2)}) %collective-permute-start.19) | collective-permute-done | bytes 131104 | tf_op jit(solution)/shard_map/ppermute | solution.py:524
  53.4 0.8 %collective-permute-start.20 = (f32[8,1024]{1,0:T(8,128)S(1)}, f32[8,1024]{1,0:T(8,128)S(1)}, u32[]{:S(2)}, u32[]{:S(2)}) collective-permute-start(f32[8,1024]{1,0:T(8,128)S(1)} %get-tuple-element.57), channel_id=1, source_target_pairs={{0,2},{1,3},{2,0},{3,1},{4,6},{5,7},{6,4},{7,5},{8,10},{9,11},{10,... | collective-permute-start | bytes 98312 | tf_op jit(solution)/shard_map/ppermute | solution.py:524
  54.2 1.2 %collective-permute-start.21 = (f32[8,1024]{1,0:T(8,128)S(1)}, f32[8,1024]{1,0:T(8,128)S(1)}, u32[]{:S(2)}, u32[]{:S(2)}) collective-permute-start(f32[8,1024]{1,0:T(8,128)S(1)} %get-tuple-element.58), channel_id=1, source_target_pairs={{0,4},{1,5},{2,6},{3,7},{4,0},{5,1},{6,2},{7,3},{8,12},{9,13},{10,... | collective-permute-start | bytes 98312 | tf_op jit(solution)/shard_map/ppermute | solution.py:524
  55.4 2.5 %collective-permute-start.22 = (f32[8,1024]{1,0:T(8,128)S(1)}, f32[8,1024]{1,0:T(8,128)S(1)}, u32[]{:S(2)}, u32[]{:S(2)}) collective-permute-start(f32[8,1024]{1,0:T(8,128)S(1)} %get-tuple-element.59), channel_id=1, source_target_pairs={{0,6},{1,7},{2,4},{3,5},{4,2},{5,3},{6,0},{7,1},{8,14},{9,15},{10,... | collective-permute-start | bytes 98312 | tf_op jit(solution)/shard_map/ppermute | solution.py:524
  57.9 1.1 %collective-permute-done.21.refs_2_ = f32[8,1024]{1,0:T(8,128)S(1)} collective-permute-done((f32[8,1024]{1,0:T(8,128)S(1)}, f32[8,1024]{1,0:T(8,128)S(1)}, u32[]{:S(2)}, u32[]{:S(2)}) %collective-permute-start.21) | collective-permute-done | bytes 32800 | tf_op jit(solution)/shard_map/ppermute | solution.py:524
  59.0 2.1 %collective-permute-done.22.refs_3_ = f32[8,1024]{1,0:T(8,128)S(1)} collective-permute-done((f32[8,1024]{1,0:T(8,128)S(1)}, f32[8,1024]{1,0:T(8,128)S(1)}, u32[]{:S(2)}, u32[]{:S(2)}) %collective-permute-start.22) | collective-permute-done | bytes 32800 | tf_op jit(solution)/shard_map/ppermute | solution.py:524
  61.1 0.6 finish.1
  (46 shorter events, 1.6 us)
Async XLA Ops:
  0.6 10.4 %copy-start.4 = (bf16[4,1024]{1,0:T(4,128)(2,1)S(1)}, bf16[4,1024]{1,0:T(4,128)(2,1)}, u32[]{:S(2)}) copy-start(bf16[4,1024]{1,0:T(4,128)(2,1)} %own_in.1) | copy-start | bytes 24580
  0.6 10.4 %copy-start.1 = (bf16[64,64,64]{2,1,0:T(8,128)(2,1)S(1)}, bf16[64,64,64]{2,1,0:T(8,128)(2,1)}, u32[]{:S(2)}) copy-start(bf16[64,64,64]{2,1,0:T(8,128)(2,1)} %turns.1) | copy-start | bytes 1572868
  0.7 10.4 %copy-start.2 = (f32[32,1024]{1,0:T(8,128)S(1)}, f32[32,1024]{1,0:T(8,128)}, u32[]{:S(2)}) copy-start(f32[32,1024]{1,0:T(8,128)} %table.1) | copy-start | bytes 393220
  0.7 10.4 %copy-start.5 = (s32[1024]{0:T(1024)S(1)}, s32[1024]{0:T(1024)}, u32[]{:S(2)}) copy-start(s32[1024]{0:T(1024)} %param.8) | copy-start | bytes 12292
  0.7 10.4 %copy-start.3 = (s32[1024,2]{0,1:T(2,128)S(1)}, s32[1024,2]{0,1:T(2,128)}, u32[]{:S(2)}) copy-start(s32[1024,2]{0,1:T(2,128)} %param.7) | copy-start | bytes 24580
  0.7 10.4 %copy-start = (bf16[1024,1024]{1,0:T(8,128)(2,1)S(1)}, bf16[1024,1024]{1,0:T(8,128)(2,1)}, u32[]{:S(2)}) copy-start(bf16[1024,1024]{1,0:T(8,128)(2,1)} %pixels.1) | copy-start | bytes 6291460
  0.7 5.7 %collective-permute-start.1 = (bf16[4,1024]{1,0:T(4,128)(2,1)}, bf16[4,1024]{1,0:T(4,128)(2,1)S(1)}, u32[]{:S(2)}, u32[]{:S(2)}) collective-permute-start(bf16[4,1024]{1,0:T(4,128)(2,1)} %own_in.1), channel_id=1, source_target_pairs={{0,2},{1,3},{2,0},{3,1},{4,6},{5,7},{6,4},{7,5},{8,10},{9,11},{10,... | collective-permute-start | bytes 24584 | tf_op jit(solution)/shard_map/ppermute | solution.py:524
  3.8 5.7 %collective-permute-start.5 = (bf16[4,1024]{1,0:T(4,128)(2,1)}, bf16[4,1024]{1,0:T(4,128)(2,1)S(1)}, u32[]{:S(2)}, u32[]{:S(2)}) collective-permute-start(bf16[4,1024]{1,0:T(4,128)(2,1)} %own_in.1), channel_id=1, source_target_pairs={{0,6},{1,7},{2,4},{3,5},{4,2},{5,3},{6,0},{7,1},{8,14},{9,15},{10,... | collective-permute-start | bytes 24584 | tf_op jit(solution)/shard_map/ppermute | solution.py:524
  6.3 4.8 %collective-permute-start.3 = (bf16[4,1024]{1,0:T(4,128)(2,1)}, bf16[4,1024]{1,0:T(4,128)(2,1)S(1)}, u32[]{:S(2)}, u32[]{:S(2)}) collective-permute-start(bf16[4,1024]{1,0:T(4,128)(2,1)} %own_in.1), channel_id=1, source_target_pairs={{0,4},{1,5},{2,6},{3,7},{4,0},{5,1},{6,2},{7,3},{8,12},{9,13},{10,... | collective-permute-start | bytes 24584 | tf_op jit(solution)/shard_map/ppermute | solution.py:524
  6.4 5.5 %collective-permute-start = (bf16[4,1024]{1,0:T(4,128)(2,1)}, bf16[4,1024]{1,0:T(4,128)(2,1)S(1)}, u32[]{:S(2)}, u32[]{:S(2)}) collective-permute-start(bf16[4,1024]{1,0:T(4,128)(2,1)} %own_in.1), channel_id=1, source_target_pairs={{0,1},{1,0},{2,3},{3,2},{4,5},{5,4},{6,7},{7,6},{8,9},{9,8},{10,11... | collective-permute-start | bytes 24584 | tf_op jit(solution)/shard_map/ppermute | solution.py:524
  6.4 5.5 %collective-permute-start.2 = (bf16[4,1024]{1,0:T(4,128)(2,1)S(1)}, bf16[4,1024]{1,0:T(4,128)(2,1)S(1)}, u32[]{:S(2)}, u32[]{:S(2)}) collective-permute-start(bf16[4,1024]{1,0:T(4,128)(2,1)S(1)} %collective-permute-done.1.rest_2_), channel_id=1, source_target_pairs={{0,1},{1,0},{2,3},{3,2},{4,5},{5,4},{6,7},{7,6},{8,9},{9,8},{10,11... | collective-permute-start | bytes 24584 | tf_op jit(solution)/shard_map/ppermute | solution.py:524
  9.5 2.4 %collective-permute-start.6 = (bf16[4,1024]{1,0:T(4,128)(2,1)S(1)}, bf16[4,1024]{1,0:T(4,128)(2,1)S(1)}, u32[]{:S(2)}, u32[]{:S(2)}) collective-permute-start(bf16[4,1024]{1,0:T(4,128)(2,1)S(1)} %collective-permute-done.5.rest_6_), channel_id=1, source_target_pairs={{0,1},{1,0},{2,3},{3,2},{4,5},{5,4},{6,7},{7,6},{8,9},{9,8},{10,11... | collective-permute-start | bytes 24584 | tf_op jit(solution)/shard_map/ppermute | solution.py:524
  11.0 1.2 %collective-permute-start.4 = (bf16[4,1024]{1,0:T(4,128)(2,1)S(1)}, bf16[4,1024]{1,0:T(4,128)(2,1)S(1)}, u32[]{:S(2)}, u32[]{:S(2)}) collective-permute-start(bf16[4,1024]{1,0:T(4,128)(2,1)S(1)} %collective-permute-done.3.rest_4_), channel_id=1, source_target_pairs={{0,1},{1,0},{2,3},{3,2},{4,5},{5,4},{6,7},{7,6},{8,9},{9,8},{10,11... | collective-permute-start | bytes 24584 | tf_op jit(solution)/shard_map/ppermute | solution.py:524
  19.6 9.8 %collective-permute-start.9 = (f16[512,128]{1,0:T(8,128)(2,1)S(1)}, f16[512,128]{1,0:T(8,128)(2,1)S(1)}, u32[]{:S(2)}, u32[]{:S(2)}) collective-permute-start(f16[512,128]{1,0:T(8,128)(2,1)S(1)} %convert_element_type.40), channel_id=1, source_target_pairs={{0,24},{8,16},{16,8},{24,0},{1,25},{9,17},{17,9},{25,1},{2,26},{10... | collective-permute-start | bytes 393224 | tf_op jit(solution)/shard_map/ppermute | solution.py:524
  22.1 7.8 %collective-permute-start.8 = (f16[512,128]{1,0:T(8,128)(2,1)S(1)}, f16[512,128]{1,0:T(8,128)(2,1)S(1)}, u32[]{:S(2)}, u32[]{:S(2)}) collective-permute-start(f16[512,128]{1,0:T(8,128)(2,1)S(1)} %convert_element_type.38), channel_id=1, source_target_pairs={{0,16},{8,24},{16,0},{24,8},{1,17},{9,25},{17,1},{25,9},{2,18},{10... | collective-permute-start | bytes 393224 | tf_op jit(solution)/shard_map/ppermute | solution.py:524
  22.7 7.3 %collective-permute-start.7 = (f16[512,128]{1,0:T(8,128)(2,1)S(1)}, f16[512,128]{1,0:T(8,128)(2,1)S(1)}, u32[]{:S(2)}, u32[]{:S(2)}) collective-permute-start(f16[512,128]{1,0:T(8,128)(2,1)S(1)} %convert_element_type.36), channel_id=1, source_target_pairs={{0,8},{8,0},{16,24},{24,16},{1,9},{9,1},{17,25},{25,17},{2,10},{10... | collective-permute-start | bytes 393224 | tf_op jit(solution)/shard_map/ppermute | solution.py:524
  26.4 8.3 %collective-permute-start.12 = (f16[512,128]{1,0:T(8,128)(2,1)S(1)}, f16[512,128]{1,0:T(8,128)(2,1)S(1)}, u32[]{:S(2)}, u32[]{:S(2)}) collective-permute-start(f16[512,128]{1,0:T(8,128)(2,1)S(1)} %convert_element_type.46), channel_id=1, source_target_pairs={{0,24},{8,16},{16,8},{24,0},{1,25},{9,17},{17,9},{25,1},{2,26},{10... | collective-permute-start | bytes 393224 | tf_op jit(solution)/shard_map/ppermute | solution.py:524
  28.9 8.2 %collective-permute-start.11 = (f16[512,128]{1,0:T(8,128)(2,1)S(1)}, f16[512,128]{1,0:T(8,128)(2,1)S(1)}, u32[]{:S(2)}, u32[]{:S(2)}) collective-permute-start(f16[512,128]{1,0:T(8,128)(2,1)S(1)} %convert_element_type.44), channel_id=1, source_target_pairs={{0,16},{8,24},{16,0},{24,8},{1,17},{9,25},{17,1},{25,9},{2,18},{10... | collective-permute-start | bytes 393224 | tf_op jit(solution)/shard_map/ppermute | solution.py:524
  29.4 7.7 %collective-permute-start.10 = (f16[512,128]{1,0:T(8,128)(2,1)S(1)}, f16[512,128]{1,0:T(8,128)(2,1)S(1)}, u32[]{:S(2)}, u32[]{:S(2)}) collective-permute-start(f16[512,128]{1,0:T(8,128)(2,1)S(1)} %convert_element_type.42), channel_id=1, source_target_pairs={{0,8},{8,0},{16,24},{24,16},{1,9},{9,1},{17,25},{25,17},{2,10},{10... | collective-permute-start | bytes 393224 | tf_op jit(solution)/shard_map/ppermute | solution.py:524
  30.2 10.4 %collective-permute-start.18 = (bf16[528,128]{1,0:T(8,128)(2,1)S(1)}, bf16[528,128]{1,0:T(8,128)(2,1)S(1)}, u32[]{:S(2)}, u32[]{:S(2)}) collective-permute-start(bf16[528,128]{1,0:T(8,128)(2,1)S(1)} %soften.2.after.rest_0_), channel_id=1, source_target_pairs={{0,24},{8,16},{16,8},{24,0},{1,25},{9,17},{17,9},{25,1},{2,26},{10... | collective-permute-start | bytes 405512 | tf_op jit(solution)/shard_map/ppermute | solution.py:524
  32.7 10.4 %collective-permute-start.17 = (bf16[528,128]{1,0:T(8,128)(2,1)S(1)}, bf16[528,128]{1,0:T(8,128)(2,1)S(1)}, u32[]{:S(2)}, u32[]{:S(2)}) collective-permute-start(bf16[528,128]{1,0:T(8,128)(2,1)S(1)} %soften.2.after.rest_0_), channel_id=1, source_target_pairs={{0,16},{8,24},{16,0},{24,8},{1,17},{9,25},{17,1},{25,9},{2,18},{10... | collective-permute-start | bytes 405512 | tf_op jit(solution)/shard_map/ppermute | solution.py:524
  34.7 8.4 %collective-permute-start.16 = (bf16[528,128]{1,0:T(8,128)(2,1)S(1)}, bf16[528,128]{1,0:T(8,128)(2,1)S(1)}, u32[]{:S(2)}, u32[]{:S(2)}) collective-permute-start(bf16[528,128]{1,0:T(8,128)(2,1)S(1)} %soften.2.after.rest_0_), channel_id=1, source_target_pairs={{0,8},{8,0},{16,24},{24,16},{1,9},{9,1},{17,25},{25,17},{2,10},{10... | collective-permute-start | bytes 405512 | tf_op jit(solution)/shard_map/ppermute | solution.py:524
  37.4 9.0 %collective-permute-start.15 = (bf16[528,128]{1,0:T(8,128)(2,1)S(1)}, bf16[528,128]{1,0:T(8,128)(2,1)S(1)}, u32[]{:S(2)}, u32[]{:S(2)}) collective-permute-start(bf16[528,128]{1,0:T(8,128)(2,1)S(1)} %soften.3.rest_2_), channel_id=1, source_target_pairs={{0,24},{8,16},{16,8},{24,0},{1,25},{9,17},{17,9},{25,1},{2,26},{10... | collective-permute-start | bytes 405512 | tf_op jit(solution)/shard_map/ppermute | solution.py:524
  39.4 7.2 %collective-permute-start.14 = (bf16[528,128]{1,0:T(8,128)(2,1)S(1)}, bf16[528,128]{1,0:T(8,128)(2,1)S(1)}, u32[]{:S(2)}, u32[]{:S(2)}) collective-permute-start(bf16[528,128]{1,0:T(8,128)(2,1)S(1)} %soften.3.rest_2_), channel_id=1, source_target_pairs={{0,16},{8,24},{16,0},{24,8},{1,17},{9,25},{17,1},{25,9},{2,18},{10... | collective-permute-start | bytes 405512 | tf_op jit(solution)/shard_map/ppermute | solution.py:524
  40.6 6.1 %collective-permute-start.13 = (bf16[528,128]{1,0:T(8,128)(2,1)S(1)}, bf16[528,128]{1,0:T(8,128)(2,1)S(1)}, u32[]{:S(2)}, u32[]{:S(2)}) collective-permute-start(bf16[528,128]{1,0:T(8,128)(2,1)S(1)} %soften.3.rest_2_), channel_id=1, source_target_pairs={{0,8},{8,0},{16,24},{24,16},{1,9},{9,1},{17,25},{25,17},{2,10},{10... | collective-permute-start | bytes 405512 | tf_op jit(solution)/shard_map/ppermute | solution.py:524
  52.1 1.3 %collective-permute-start.19 = (f32[32,1024]{1,0:T(8,128)S(1)}, f32[32,1024]{1,0:T(8,128)S(1)}, u32[]{:S(2)}, u32[]{:S(2)}) collective-permute-start(f32[32,1024]{1,0:T(8,128)S(1)} %get-tuple-element.55), channel_id=1, source_target_pairs={{0,1},{1,0},{2,3},{3,2},{4,5},{5,4},{6,7},{7,6},{8,9},{9,8},{10,11... | collective-permute-start | bytes 393224 | tf_op jit(solution)/shard_map/ppermute | solution.py:524
  53.4 4.5 %collective-permute-start.20 = (f32[8,1024]{1,0:T(8,128)S(1)}, f32[8,1024]{1,0:T(8,128)S(1)}, u32[]{:S(2)}, u32[]{:S(2)}) collective-permute-start(f32[8,1024]{1,0:T(8,128)S(1)} %get-tuple-element.57), channel_id=1, source_target_pairs={{0,2},{1,3},{2,0},{3,1},{4,6},{5,7},{6,4},{7,5},{8,10},{9,11},{10,... | collective-permute-start | bytes 98312 | tf_op jit(solution)/shard_map/ppermute | solution.py:524
  54.2 4.8 %collective-permute-start.21 = (f32[8,1024]{1,0:T(8,128)S(1)}, f32[8,1024]{1,0:T(8,128)S(1)}, u32[]{:S(2)}, u32[]{:S(2)}) collective-permute-start(f32[8,1024]{1,0:T(8,128)S(1)} %get-tuple-element.58), channel_id=1, source_target_pairs={{0,4},{1,5},{2,6},{3,7},{4,0},{5,1},{6,2},{7,3},{8,12},{9,13},{10,... | collective-permute-start | bytes 98312 | tf_op jit(solution)/shard_map/ppermute | solution.py:524
  55.4 5.7 %collective-permute-start.22 = (f32[8,1024]{1,0:T(8,128)S(1)}, f32[8,1024]{1,0:T(8,128)S(1)}, u32[]{:S(2)}, u32[]{:S(2)}) collective-permute-start(f32[8,1024]{1,0:T(8,128)S(1)} %get-tuple-element.59), channel_id=1, source_target_pairs={{0,6},{1,7},{2,4},{3,5},{4,2},{5,3},{6,0},{7,1},{8,14},{9,15},{10,... | collective-permute-start | bytes 98312 | tf_op jit(solution)/shard_map/ppermute | solution.py:524

commit v7 on v6

--- a/solution.py
+++ b/solution.py
@@ -568,7 +568,7 @@
         )
     if paired:
         pieces = add_cut(out[0], swap(out[1], "dom", 1), owners // 2)
-        pieces = [pieces[0]] + [swap(pieces[k], "dom", 2 * k) for k in range(1, owners // 2)]
+        pieces = [pieces[0]] + [swap(pieces[k], "dom", 2 * k) for k in reversed(range(1, owners // 2))]
     else:
         pieces = [lax.psum_scatter(out[0], "dom", scatter_dimension=0, tiled=True)]
     class_sums, class_weights = finish(pieces, cpg)

time: 61.9 us -> 61.1 us (0.987)
  waiting for transfers between devices: 13.3 us -> 12.5 us
    ppermute x23, waiting for transfers between devices: 13.3 us -> 12.5 us  [swap(): lax.ppermute(x, axis, [(i, i ^ k) for i in range(lax.axis_size(axis))])]
  transfers between devices with their start and end apart: 23 -> 23, of which waited for: 10 -> 11; matrix products, arithmetic and copies ran while one was open for 0% -> 0% of each run, Pallas kernels for 15% -> 15%
where the time goes in v7:
time: 61.1 us; the launch traced here: 61 us
  starting transfers between devices  24.9 us (41%)
  Pallas kernels  22.4 us (37%)
  waiting for transfers between devices  12.5 us (20%)
  between operations  0.9 us (1%)
    ppermute x23, starting transfers between devices, swap(): lax.ppermute(x, axis, [(i, i ^ k) for i in range(lax.axis_size(axis))])  24.9 us
    ppermute x23, waiting for transfers between devices, swap(): lax.ppermute(x, axis, [(i, i ^ k) for i in range(lax.axis_size(axis))])  12.5 us
    pallas_call x2, Pallas kernels, collect(): pl.pallas_call(functools.partial(collect_kernel, groups, parts, turn_coun...  8.69 us
    pallas_call x2, Pallas kernels, score(): pl.pallas_call(functools.partial(score_kernel, groups, scale, begin), gri...  6.22 us
    pallas_call x1, Pallas kernels, rotate(): pl.pallas_call(functools.partial(rotate_kernel, groups, pack), grid=(step...  4.23 us
    pallas_call x1, Pallas kernels, prepare(): pl.pallas_call(functools.partial(prepare_kernel, pack), in_specs=[VMEM] *...  1.49 us
  transfers between devices with their start and end apart: 23, of which 11 were waited for; matrix products, arithmetic and copies ran while one was open for 0% of the time, Pallas kernels for 15%

profile of v7, /device:TPU:0, one launch (start us, length us, event | category | flops | bytes accessed | tf_op | source)
XLA Modules:
  0.0 61.0 jit_solution(12856372089970928754)
XLA Ops:
  0.7 3.1 %collective-permute-start.1 = (bf16[4,1024]{1,0:T(4,128)(2,1)}, bf16[4,1024]{1,0:T(4,128)(2,1)S(1)}, u32[]{:S(2)}, u32[]{:S(2)}) collective-permute-start(bf16[4,1024]{1,0:T(4,128)(2,1)} %own_in.1), channel_id=1, source_target_pairs={{0,2},{1,3},{2,0},{3,1},{4,6},{5,7},{6,4},{7,5},{8,10},{9,11},{10,... | collective-permute-start | bytes 24584 | tf_op jit(solution)/shard_map/ppermute | solution.py:524
  3.8 2.5 %collective-permute-start.5 = (bf16[4,1024]{1,0:T(4,128)(2,1)}, bf16[4,1024]{1,0:T(4,128)(2,1)S(1)}, u32[]{:S(2)}, u32[]{:S(2)}) collective-permute-start(bf16[4,1024]{1,0:T(4,128)(2,1)} %own_in.1), channel_id=1, source_target_pairs={{0,6},{1,7},{2,4},{3,5},{4,2},{5,3},{6,0},{7,1},{8,14},{9,15},{10,... | collective-permute-start | bytes 24584 | tf_op jit(solution)/shard_map/ppermute | solution.py:524
  6.4 0.5 collective-permute-start.2
  6.9 2.6 %collective-permute-done.5.rest_6_ = bf16[4,1024]{1,0:T(4,128)(2,1)S(1)} collective-permute-done((bf16[4,1024]{1,0:T(4,128)(2,1)}, bf16[4,1024]{1,0:T(4,128)(2,1)S(1)}, u32[]{:S(2)}, u32[]{:S(2)}) %collective-permute-start.5) | collective-permute-done | bytes 8224 | tf_op jit(solution)/shard_map/ppermute | solution.py:524
  9.5 1.5 %collective-permute-done.3.rest_4_ = bf16[4,1024]{1,0:T(4,128)(2,1)S(1)} collective-permute-done((bf16[4,1024]{1,0:T(4,128)(2,1)}, bf16[4,1024]{1,0:T(4,128)(2,1)S(1)}, u32[]{:S(2)}, u32[]{:S(2)}) %collective-permute-start.3) | collective-permute-done | bytes 8224 | tf_op jit(solution)/shard_map/ppermute | solution.py:524
  11.1 0.8 %start.1 = (bf16[1024,1152]{1,0:T(8,128)(2,1)S(1)}, bf16[64,1024]{1,0:T(8,128)(2,1)S(1)}, s32[2,1024]{1,0:T(2,128)S(1)}, bf16[4,1024]{1,0:T(4,128)(2,1)S(1)}, bf16[64,64,128]{2,1,0:T(8,128)(2,1)S(1)}) custom-call(s32[128,256]{1,0:T(8,128)S(1)} %seed.1.numbers, bf16[4,1024]{1,0:T(4,128)(2,1)S(1)} %copy-done.4, bf16[1024,1024]{1,0:T(8,128)(2,1)S(1)} %copy-done, ...), custom_call_target="tpu_custom_call" | custom-call | flops 1048576 | tf_op jit(solution)/shard_map/start/pallas_call | solution.py:108
  12.2 4.2 %rotate.1 = (bf16[2048,1152]{1,0:T(8,128)(2,1)S(1)}, f32[1,128]{1,0:T(1,128)S(1)}) custom-call(bf16[64,1024]{1,0:T(8,128)(2,1)S(1)} %get-tuple-element.35.power2.power, bf16[64,64,128]{2,1,0:T(8,128)(2,1)S(1)} %get-tuple-element.36.turns, bf16[4,1024]{1,0:T(4,128)(2,1)S(1)} %get-tuple-element.37.rest_0_, bf16[4,1024]{1,0:T(4,128)(2,1)S(1)} %collective-permute-done.rest_1_, ...), custom_call_target="tpu_custom_call" | custom-call | flops 1073741824 | bytes 4194304 | tf_op jit(solution)/shard_map/rotate/pallas_call | solution.py:241
  16.4 3.1 %score.2 = (f32[512,128]{1,0:T(8,128)S(1)}, f32[512,128]{1,0:T(8,128)S(1)}, f32[512,128]{1,0:T(8,128)S(1)}, f32[512,128]{1,0:T(8,128)S(1)}) custom-call(s32[1]{0:T(128)} %bitcast.me, s32[1]{0:T(128)} %bitcast.1.here, bf16[1024,1152]{1,0:T(8,128)(2,1)S(1)} %get-tuple-element.34.weighted, s32[2,1024]{1,0:T(2,128)S(1)} %get-tuple-element.33.names, ...), custom_call_target="tpu_custom_call" | custom-call | flops 2415919104 | bytes 4718592 | tf_op jit(solution)/shard_map/score/pallas_call | solution.py:290
  19.6 2.5 %collective-permute-start.9 = (f16[512,128]{1,0:T(8,128)(2,1)S(1)}, f16[512,128]{1,0:T(8,128)(2,1)S(1)}, u32[]{:S(2)}, u32[]{:S(2)}) collective-permute-start(f16[512,128]{1,0:T(8,128)(2,1)S(1)} %convert_element_type.40), channel_id=1, source_target_pairs={{0,24},{8,16},{16,8},{24,0},{1,25},{9,17},{17,9},{25,1},{2,26},{10... | collective-permute-start | bytes 393224 | tf_op jit(solution)/shard_map/ppermute | solution.py:524
  22.1 0.5 collective-permute-start.8
  22.7 0.5 collective-permute-start.7
  23.2 3.1 %score.3 = (f32[512,128]{1,0:T(8,128)S(1)}, f32[512,128]{1,0:T(8,128)S(1)}, f32[512,128]{1,0:T(8,128)S(1)}, f32[512,128]{1,0:T(8,128)S(1)}) custom-call(s32[1]{0:T(128)} %bitcast.me, s32[1]{0:T(128)} %bitcast.1.here, bf16[1024,1152]{1,0:T(8,128)(2,1)S(1)} %get-tuple-element.34.weighted, s32[2,1024]{1,0:T(2,128)S(1)} %get-tuple-element.33.names, ...), custom_call_target="tpu_custom_call" | custom-call | flops 2415919104 | bytes 4718592 | tf_op jit(solution)/shard_map/score/pallas_call | solution.py:290
  26.4 2.5 %collective-permute-start.12 = (f16[512,128]{1,0:T(8,128)(2,1)S(1)}, f16[512,128]{1,0:T(8,128)(2,1)S(1)}, u32[]{:S(2)}, u32[]{:S(2)}) collective-permute-start(f16[512,128]{1,0:T(8,128)(2,1)S(1)} %convert_element_type.46), channel_id=1, source_target_pairs={{0,24},{8,16},{16,8},{24,0},{1,25},{9,17},{17,9},{25,1},{2,26},{10... | collective-permute-start | bytes 393224 | tf_op jit(solution)/shard_map/ppermute | solution.py:524
  28.9 0.5 collective-permute-start.11
  29.4 0.5 collective-permute-start.10
  30.2 2.5 %collective-permute-start.18 = (bf16[528,128]{1,0:T(8,128)(2,1)S(1)}, bf16[528,128]{1,0:T(8,128)(2,1)S(1)}, u32[]{:S(2)}, u32[]{:S(2)}) collective-permute-start(bf16[528,128]{1,0:T(8,128)(2,1)S(1)} %soften.2.after.rest_0_), channel_id=1, source_target_pairs={{0,24},{8,16},{16,8},{24,0},{1,25},{9,17},{17,9},{25,1},{2,26},{10... | collective-permute-start | bytes 405512 | tf_op jit(solution)/shard_map/ppermute | solution.py:524
  32.7 0.5 collective-permute-start.17
  33.2 1.5 %prepare.1 = (bf16[4096,256]{1,0:T(8,128)(2,1)S(1)}, bf16[1024,2048]{1,0:T(8,128)(2,1)S(1)}, f32[8,128]{1,0:T(8,128)S(1)}) custom-call(bf16[528,128]{1,0:T(8,128)(2,1)S(1)} %soften.2.after.rest_0_, bf16[64,64,128]{2,1,0:T(8,128)(2,1)S(1)} %get-tuple-element.36.turns, bf16[64,1024]{1,0:T(8,128)(2,1)S(1)} %get-tuple-element.35.power2.power), custom_call_target="tpu_custom_call" | custom-call | flops 4000000000 | tf_op jit(solution)/shard_map/prepare/pallas_call | solution.py:154
  34.7 0.6 %collective-permute-start.16 = (bf16[528,128]{1,0:T(8,128)(2,1)S(1)}, bf16[528,128]{1,0:T(8,128)(2,1)S(1)}, u32[]{:S(2)}, u32[]{:S(2)}) collective-permute-start(bf16[528,128]{1,0:T(8,128)(2,1)S(1)} %soften.2.after.rest_0_), channel_id=1, source_target_pairs={{0,8},{8,0},{16,24},{24,16},{1,9},{9,1},{17,25},{25,17},{2,10},{10... | collective-permute-start | bytes 405512 | tf_op jit(solution)/shard_map/ppermute | solution.py:524
  35.3 1.8 %collective-permute-done.11 = f16[512,128]{1,0:T(8,128)(2,1)S(1)} collective-permute-done((f16[512,128]{1,0:T(8,128)(2,1)S(1)}, f16[512,128]{1,0:T(8,128)(2,1)S(1)}, u32[]{:S(2)}, u32[]{:S(2)}) %collective-permute-start.11) | collective-permute-done | bytes 131104 | tf_op jit(solution)/shard_map/ppermute | solution.py:524
  37.4 2.0 %collective-permute-start.15 = (bf16[528,128]{1,0:T(8,128)(2,1)S(1)}, bf16[528,128]{1,0:T(8,128)(2,1)S(1)}, u32[]{:S(2)}, u32[]{:S(2)}) collective-permute-start(bf16[528,128]{1,0:T(8,128)(2,1)S(1)} %soften.3.rest_2_), channel_id=1, source_target_pairs={{0,24},{8,16},{16,8},{24,0},{1,25},{9,17},{17,9},{25,1},{2,26},{10... | collective-permute-start | bytes 405512 | tf_op jit(solution)/shard_map/ppermute | solution.py:524
  39.4 1.2 %collective-permute-start.14 = (bf16[528,128]{1,0:T(8,128)(2,1)S(1)}, bf16[528,128]{1,0:T(8,128)(2,1)S(1)}, u32[]{:S(2)}, u32[]{:S(2)}) collective-permute-start(bf16[528,128]{1,0:T(8,128)(2,1)S(1)} %soften.3.rest_2_), channel_id=1, source_target_pairs={{0,16},{8,24},{16,0},{24,8},{1,17},{9,25},{17,1},{25,9},{2,18},{10... | collective-permute-start | bytes 405512 | tf_op jit(solution)/shard_map/ppermute | solution.py:524
  40.9 2.2 %collective-permute-done.17.rest_2_ = bf16[528,128]{1,0:T(8,128)(2,1)S(1)} collective-permute-done((bf16[528,128]{1,0:T(8,128)(2,1)S(1)}, bf16[528,128]{1,0:T(8,128)(2,1)S(1)}, u32[]{:S(2)}, u32[]{:S(2)}) %collective-permute-start.17) | collective-permute-done | bytes 135200 | tf_op jit(solution)/shard_map/ppermute | solution.py:524
  43.1 3.3 %collect.2 = (f32[512,4096]{1,0:T(8,128)S(1)}, f32[64,1024]{1,0:T(8,128)S(1)}, f32[1,1024]{1,0:T(1,128)S(1)}) custom-call(s32[1]{0:T(128)} %bitcast.me, s32[1]{0:T(128)} %bitcast.1.here, s32[2,1024]{1,0:T(2,128)S(1)} %get-tuple-element.33.names, bf16[1024,1152]{1,0:T(8,128)(2,1)S(1)} %get-tuple-element.34.weighted, ...), custom_call_target="tpu_custom_call" | custom-call | flops 2415919104 | bytes 4194304 | tf_op jit(solution)/shard_map/collect/pallas_call | solution.py:464
  46.7 5.4 %collect.3 = (f32[32,1024]{1,0:T(8,128)S(1)}, f32[32,1024]{1,0:T(8,128)S(1)}, f32[1,1024]{1,0:T(1,128)}) custom-call(s32[1]{0:T(128)} %bitcast.me, s32[1]{0:T(128)} %bitcast.1.here, s32[2,1024]{1,0:T(2,128)S(1)} %get-tuple-element.33.names, bf16[1024,1152]{1,0:T(8,128)(2,1)S(1)} %get-tuple-element.34.weighted, ...), custom_call_target="tpu_custom_call" | custom-call | flops 2415919104 | bytes 4194304 | tf_op jit(solution)/shard_map/collect/pallas_call | solution.py:464
  52.1 1.3 %collective-permute-done.19.right = f32[32,1024]{1,0:T(8,128)S(1)} collective-permute-done((f32[32,1024]{1,0:T(8,128)S(1)}, f32[32,1024]{1,0:T(8,128)S(1)}, u32[]{:S(2)}, u32[]{:S(2)}) %collective-permute-start.19) | collective-permute-done | bytes 131104 | tf_op jit(solution)/shard_map/ppermute | solution.py:524
  53.4 1.4 %collective-permute-start.20 = (f32[8,1024]{1,0:T(8,128)S(1)}, f32[8,1024]{1,0:T(8,128)S(1)}, u32[]{:S(2)}, u32[]{:S(2)}) collective-permute-start(f32[8,1024]{1,0:T(8,128)S(1)} %get-tuple-element.57), channel_id=1, source_target_pairs={{0,6},{1,7},{2,4},{3,5},{4,2},{5,3},{6,0},{7,1},{8,14},{9,15},{10,... | collective-permute-start | bytes 98312 | tf_op jit(solution)/shard_map/ppermute | solution.py:524
  54.9 0.8 %collective-permute-start.21 = (f32[8,1024]{1,0:T(8,128)S(1)}, f32[8,1024]{1,0:T(8,128)S(1)}, u32[]{:S(2)}, u32[]{:S(2)}) collective-permute-start(f32[8,1024]{1,0:T(8,128)S(1)} %get-tuple-element.58), channel_id=1, source_target_pairs={{0,4},{1,5},{2,6},{3,7},{4,0},{5,1},{6,2},{7,3},{8,12},{9,13},{10,... | collective-permute-start | bytes 98312 | tf_op jit(solution)/shard_map/ppermute | solution.py:524
  55.7 2.2 %collective-permute-start.22 = (f32[8,1024]{1,0:T(8,128)S(1)}, f32[8,1024]{1,0:T(8,128)S(1)}, u32[]{:S(2)}, u32[]{:S(2)}) collective-permute-start(f32[8,1024]{1,0:T(8,128)S(1)} %get-tuple-element.59), channel_id=1, source_target_pairs={{0,2},{1,3},{2,0},{3,1},{4,6},{5,7},{6,4},{7,5},{8,10},{9,11},{10,... | collective-permute-start | bytes 98312 | tf_op jit(solution)/shard_map/ppermute | solution.py:524
  57.9 1.3 %collective-permute-done.20.refs_1_ = f32[8,1024]{1,0:T(8,128)S(1)} collective-permute-done((f32[8,1024]{1,0:T(8,128)S(1)}, f32[8,1024]{1,0:T(8,128)S(1)}, u32[]{:S(2)}, u32[]{:S(2)}) %collective-permute-start.20) | collective-permute-done | bytes 32800 | tf_op jit(solution)/shard_map/ppermute | solution.py:524
  59.2 1.0 %collective-permute-done.21.refs_2_ = f32[8,1024]{1,0:T(8,128)S(1)} collective-permute-done((f32[8,1024]{1,0:T(8,128)S(1)}, f32[8,1024]{1,0:T(8,128)S(1)}, u32[]{:S(2)}, u32[]{:S(2)}) %collective-permute-start.21) | collective-permute-done | bytes 32800 | tf_op jit(solution)/shard_map/ppermute | solution.py:524
  60.3 0.6 %finish.1 = (bf16[4,1024]{1,0:T(4,128)(2,1)}, f32[4,1024]{1,0:T(4,128)}) custom-call(f32[8,1024]{1,0:T(8,128)S(1)} %get-tuple-element.56.refs_0_, f32[8,1024]{1,0:T(8,128)S(1)} %collective-permute-done.20.refs_1_, f32[8,1024]{1,0:T(8,128)S(1)} %collective-permute-done.21.refs_2_, f32[8,1024]{1,0:T(8,128)S(1)} %collective-permute-done.22.refs_3_), custom_call_target="tpu_custom_call" | custom-call | flops 8192 | bytes 98304 | tf_op jit(solution)/shard_map/finish/pallas_call | solution.py:513
  (46 shorter events, 1.8 us)
Async XLA Ops:
  0.6 10.4 %copy-start.4 = (bf16[4,1024]{1,0:T(4,128)(2,1)S(1)}, bf16[4,1024]{1,0:T(4,128)(2,1)}, u32[]{:S(2)}) copy-start(bf16[4,1024]{1,0:T(4,128)(2,1)} %own_in.1) | copy-start | bytes 24580
  0.6 10.4 %copy-start.1 = (bf16[64,64,64]{2,1,0:T(8,128)(2,1)S(1)}, bf16[64,64,64]{2,1,0:T(8,128)(2,1)}, u32[]{:S(2)}) copy-start(bf16[64,64,64]{2,1,0:T(8,128)(2,1)} %turns.1) | copy-start | bytes 1572868
  0.7 10.4 %copy-start.2 = (f32[32,1024]{1,0:T(8,128)S(1)}, f32[32,1024]{1,0:T(8,128)}, u32[]{:S(2)}) copy-start(f32[32,1024]{1,0:T(8,128)} %table.1) | copy-start | bytes 393220
  0.7 10.4 %copy-start.5 = (s32[1024]{0:T(1024)S(1)}, s32[1024]{0:T(1024)}, u32[]{:S(2)}) copy-start(s32[1024]{0:T(1024)} %param.8) | copy-start | bytes 12292
  0.7 10.4 %copy-start.3 = (s32[1024,2]{0,1:T(2,128)S(1)}, s32[1024,2]{0,1:T(2,128)}, u32[]{:S(2)}) copy-start(s32[1024,2]{0,1:T(2,128)} %param.7) | copy-start | bytes 24580
  0.7 10.4 %copy-start = (bf16[1024,1024]{1,0:T(8,128)(2,1)S(1)}, bf16[1024,1024]{1,0:T(8,128)(2,1)}, u32[]{:S(2)}) copy-start(bf16[1024,1024]{1,0:T(8,128)(2,1)} %pixels.1) | copy-start | bytes 6291460
  0.7 5.7 %collective-permute-start.1 = (bf16[4,1024]{1,0:T(4,128)(2,1)}, bf16[4,1024]{1,0:T(4,128)(2,1)S(1)}, u32[]{:S(2)}, u32[]{:S(2)}) collective-permute-start(bf16[4,1024]{1,0:T(4,128)(2,1)} %own_in.1), channel_id=1, source_target_pairs={{0,2},{1,3},{2,0},{3,1},{4,6},{5,7},{6,4},{7,5},{8,10},{9,11},{10,... | collective-permute-start | bytes 24584 | tf_op jit(solution)/shard_map/ppermute | solution.py:524
  3.8 5.7 %collective-permute-start.5 = (bf16[4,1024]{1,0:T(4,128)(2,1)}, bf16[4,1024]{1,0:T(4,128)(2,1)S(1)}, u32[]{:S(2)}, u32[]{:S(2)}) collective-permute-start(bf16[4,1024]{1,0:T(4,128)(2,1)} %own_in.1), channel_id=1, source_target_pairs={{0,6},{1,7},{2,4},{3,5},{4,2},{5,3},{6,0},{7,1},{8,14},{9,15},{10,... | collective-permute-start | bytes 24584 | tf_op jit(solution)/shard_map/ppermute | solution.py:524
  6.3 4.8 %collective-permute-start.3 = (bf16[4,1024]{1,0:T(4,128)(2,1)}, bf16[4,1024]{1,0:T(4,128)(2,1)S(1)}, u32[]{:S(2)}, u32[]{:S(2)}) collective-permute-start(bf16[4,1024]{1,0:T(4,128)(2,1)} %own_in.1), channel_id=1, source_target_pairs={{0,4},{1,5},{2,6},{3,7},{4,0},{5,1},{6,2},{7,3},{8,12},{9,13},{10,... | collective-permute-start | bytes 24584 | tf_op jit(solution)/shard_map/ppermute | solution.py:524
  6.4 5.5 %collective-permute-start = (bf16[4,1024]{1,0:T(4,128)(2,1)}, bf16[4,1024]{1,0:T(4,128)(2,1)S(1)}, u32[]{:S(2)}, u32[]{:S(2)}) collective-permute-start(bf16[4,1024]{1,0:T(4,128)(2,1)} %own_in.1), channel_id=1, source_target_pairs={{0,1},{1,0},{2,3},{3,2},{4,5},{5,4},{6,7},{7,6},{8,9},{9,8},{10,11... | collective-permute-start | bytes 24584 | tf_op jit(solution)/shard_map/ppermute | solution.py:524
  6.4 5.5 %collective-permute-start.2 = (bf16[4,1024]{1,0:T(4,128)(2,1)S(1)}, bf16[4,1024]{1,0:T(4,128)(2,1)S(1)}, u32[]{:S(2)}, u32[]{:S(2)}) collective-permute-start(bf16[4,1024]{1,0:T(4,128)(2,1)S(1)} %collective-permute-done.1.rest_2_), channel_id=1, source_target_pairs={{0,1},{1,0},{2,3},{3,2},{4,5},{5,4},{6,7},{7,6},{8,9},{9,8},{10,11... | collective-permute-start | bytes 24584 | tf_op jit(solution)/shard_map/ppermute | solution.py:524
  9.5 2.4 %collective-permute-start.6 = (bf16[4,1024]{1,0:T(4,128)(2,1)S(1)}, bf16[4,1024]{1,0:T(4,128)(2,1)S(1)}, u32[]{:S(2)}, u32[]{:S(2)}) collective-permute-start(bf16[4,1024]{1,0:T(4,128)(2,1)S(1)} %collective-permute-done.5.rest_6_), channel_id=1, source_target_pairs={{0,1},{1,0},{2,3},{3,2},{4,5},{5,4},{6,7},{7,6},{8,9},{9,8},{10,11... | collective-permute-start | bytes 24584 | tf_op jit(solution)/shard_map/ppermute | solution.py:524
  11.0 1.2 %collective-permute-start.4 = (bf16[4,1024]{1,0:T(4,128)(2,1)S(1)}, bf16[4,1024]{1,0:T(4,128)(2,1)S(1)}, u32[]{:S(2)}, u32[]{:S(2)}) collective-permute-start(bf16[4,1024]{1,0:T(4,128)(2,1)S(1)} %collective-permute-done.3.rest_4_), channel_id=1, source_target_pairs={{0,1},{1,0},{2,3},{3,2},{4,5},{5,4},{6,7},{7,6},{8,9},{9,8},{10,11... | collective-permute-start | bytes 24584 | tf_op jit(solution)/shard_map/ppermute | solution.py:524
  19.6 9.8 %collective-permute-start.9 = (f16[512,128]{1,0:T(8,128)(2,1)S(1)}, f16[512,128]{1,0:T(8,128)(2,1)S(1)}, u32[]{:S(2)}, u32[]{:S(2)}) collective-permute-start(f16[512,128]{1,0:T(8,128)(2,1)S(1)} %convert_element_type.40), channel_id=1, source_target_pairs={{0,24},{8,16},{16,8},{24,0},{1,25},{9,17},{17,9},{25,1},{2,26},{10... | collective-permute-start | bytes 393224 | tf_op jit(solution)/shard_map/ppermute | solution.py:524
  22.1 7.8 %collective-permute-start.8 = (f16[512,128]{1,0:T(8,128)(2,1)S(1)}, f16[512,128]{1,0:T(8,128)(2,1)S(1)}, u32[]{:S(2)}, u32[]{:S(2)}) collective-permute-start(f16[512,128]{1,0:T(8,128)(2,1)S(1)} %convert_element_type.38), channel_id=1, source_target_pairs={{0,16},{8,24},{16,0},{24,8},{1,17},{9,25},{17,1},{25,9},{2,18},{10... | collective-permute-start | bytes 393224 | tf_op jit(solution)/shard_map/ppermute | solution.py:524
  22.7 7.3 %collective-permute-start.7 = (f16[512,128]{1,0:T(8,128)(2,1)S(1)}, f16[512,128]{1,0:T(8,128)(2,1)S(1)}, u32[]{:S(2)}, u32[]{:S(2)}) collective-permute-start(f16[512,128]{1,0:T(8,128)(2,1)S(1)} %convert_element_type.36), channel_id=1, source_target_pairs={{0,8},{8,0},{16,24},{24,16},{1,9},{9,1},{17,25},{25,17},{2,10},{10... | collective-permute-start | bytes 393224 | tf_op jit(solution)/shard_map/ppermute | solution.py:524
  26.4 8.3 %collective-permute-start.12 = (f16[512,128]{1,0:T(8,128)(2,1)S(1)}, f16[512,128]{1,0:T(8,128)(2,1)S(1)}, u32[]{:S(2)}, u32[]{:S(2)}) collective-permute-start(f16[512,128]{1,0:T(8,128)(2,1)S(1)} %convert_element_type.46), channel_id=1, source_target_pairs={{0,24},{8,16},{16,8},{24,0},{1,25},{9,17},{17,9},{25,1},{2,26},{10... | collective-permute-start | bytes 393224 | tf_op jit(solution)/shard_map/ppermute | solution.py:524
  28.9 8.2 %collective-permute-start.11 = (f16[512,128]{1,0:T(8,128)(2,1)S(1)}, f16[512,128]{1,0:T(8,128)(2,1)S(1)}, u32[]{:S(2)}, u32[]{:S(2)}) collective-permute-start(f16[512,128]{1,0:T(8,128)(2,1)S(1)} %convert_element_type.44), channel_id=1, source_target_pairs={{0,16},{8,24},{16,0},{24,8},{1,17},{9,25},{17,1},{25,9},{2,18},{10... | collective-permute-start | bytes 393224 | tf_op jit(solution)/shard_map/ppermute | solution.py:524
  29.4 7.7 %collective-permute-start.10 = (f16[512,128]{1,0:T(8,128)(2,1)S(1)}, f16[512,128]{1,0:T(8,128)(2,1)S(1)}, u32[]{:S(2)}, u32[]{:S(2)}) collective-permute-start(f16[512,128]{1,0:T(8,128)(2,1)S(1)} %convert_element_type.42), channel_id=1, source_target_pairs={{0,8},{8,0},{16,24},{24,16},{1,9},{9,1},{17,25},{25,17},{2,10},{10... | collective-permute-start | bytes 393224 | tf_op jit(solution)/shard_map/ppermute | solution.py:524
  30.2 10.4 %collective-permute-start.18 = (bf16[528,128]{1,0:T(8,128)(2,1)S(1)}, bf16[528,128]{1,0:T(8,128)(2,1)S(1)}, u32[]{:S(2)}, u32[]{:S(2)}) collective-permute-start(bf16[528,128]{1,0:T(8,128)(2,1)S(1)} %soften.2.after.rest_0_), channel_id=1, source_target_pairs={{0,24},{8,16},{16,8},{24,0},{1,25},{9,17},{17,9},{25,1},{2,26},{10... | collective-permute-start | bytes 405512 | tf_op jit(solution)/shard_map/ppermute | solution.py:524
  32.7 10.4 %collective-permute-start.17 = (bf16[528,128]{1,0:T(8,128)(2,1)S(1)}, bf16[528,128]{1,0:T(8,128)(2,1)S(1)}, u32[]{:S(2)}, u32[]{:S(2)}) collective-permute-start(bf16[528,128]{1,0:T(8,128)(2,1)S(1)} %soften.2.after.rest_0_), channel_id=1, source_target_pairs={{0,16},{8,24},{16,0},{24,8},{1,17},{9,25},{17,1},{25,9},{2,18},{10... | collective-permute-start | bytes 405512 | tf_op jit(solution)/shard_map/ppermute | solution.py:524
  34.7 8.4 %collective-permute-start.16 = (bf16[528,128]{1,0:T(8,128)(2,1)S(1)}, bf16[528,128]{1,0:T(8,128)(2,1)S(1)}, u32[]{:S(2)}, u32[]{:S(2)}) collective-permute-start(bf16[528,128]{1,0:T(8,128)(2,1)S(1)} %soften.2.after.rest_0_), channel_id=1, source_target_pairs={{0,8},{8,0},{16,24},{24,16},{1,9},{9,1},{17,25},{25,17},{2,10},{10... | collective-permute-start | bytes 405512 | tf_op jit(solution)/shard_map/ppermute | solution.py:524
  37.4 9.0 %collective-permute-start.15 = (bf16[528,128]{1,0:T(8,128)(2,1)S(1)}, bf16[528,128]{1,0:T(8,128)(2,1)S(1)}, u32[]{:S(2)}, u32[]{:S(2)}) collective-permute-start(bf16[528,128]{1,0:T(8,128)(2,1)S(1)} %soften.3.rest_2_), channel_id=1, source_target_pairs={{0,24},{8,16},{16,8},{24,0},{1,25},{9,17},{17,9},{25,1},{2,26},{10... | collective-permute-start | bytes 405512 | tf_op jit(solution)/shard_map/ppermute | solution.py:524
  39.4 7.2 %collective-permute-start.14 = (bf16[528,128]{1,0:T(8,128)(2,1)S(1)}, bf16[528,128]{1,0:T(8,128)(2,1)S(1)}, u32[]{:S(2)}, u32[]{:S(2)}) collective-permute-start(bf16[528,128]{1,0:T(8,128)(2,1)S(1)} %soften.3.rest_2_), channel_id=1, source_target_pairs={{0,16},{8,24},{16,0},{24,8},{1,17},{9,25},{17,1},{25,9},{2,18},{10... | collective-permute-start | bytes 405512 | tf_op jit(solution)/shard_map/ppermute | solution.py:524
  40.6 6.1 %collective-permute-start.13 = (bf16[528,128]{1,0:T(8,128)(2,1)S(1)}, bf16[528,128]{1,0:T(8,128)(2,1)S(1)}, u32[]{:S(2)}, u32[]{:S(2)}) collective-permute-start(bf16[528,128]{1,0:T(8,128)(2,1)S(1)} %soften.3.rest_2_), channel_id=1, source_target_pairs={{0,8},{8,0},{16,24},{24,16},{1,9},{9,1},{17,25},{25,17},{2,10},{10... | collective-permute-start | bytes 405512 | tf_op jit(solution)/shard_map/ppermute | solution.py:524
  52.1 1.3 %collective-permute-start.19 = (f32[32,1024]{1,0:T(8,128)S(1)}, f32[32,1024]{1,0:T(8,128)S(1)}, u32[]{:S(2)}, u32[]{:S(2)}) collective-permute-start(f32[32,1024]{1,0:T(8,128)S(1)} %get-tuple-element.55), channel_id=1, source_target_pairs={{0,1},{1,0},{2,3},{3,2},{4,5},{5,4},{6,7},{7,6},{8,9},{9,8},{10,11... | collective-permute-start | bytes 393224 | tf_op jit(solution)/shard_map/ppermute | solution.py:524
  53.4 5.8 %collective-permute-start.20 = (f32[8,1024]{1,0:T(8,128)S(1)}, f32[8,1024]{1,0:T(8,128)S(1)}, u32[]{:S(2)}, u32[]{:S(2)}) collective-permute-start(f32[8,1024]{1,0:T(8,128)S(1)} %get-tuple-element.57), channel_id=1, source_target_pairs={{0,6},{1,7},{2,4},{3,5},{4,2},{5,3},{6,0},{7,1},{8,14},{9,15},{10,... | collective-permute-start | bytes 98312 | tf_op jit(solution)/shard_map/ppermute | solution.py:524
  54.9 5.3 %collective-permute-start.21 = (f32[8,1024]{1,0:T(8,128)S(1)}, f32[8,1024]{1,0:T(8,128)S(1)}, u32[]{:S(2)}, u32[]{:S(2)}) collective-permute-start(f32[8,1024]{1,0:T(8,128)S(1)} %get-tuple-element.58), channel_id=1, source_target_pairs={{0,4},{1,5},{2,6},{3,7},{4,0},{5,1},{6,2},{7,3},{8,12},{9,13},{10,... | collective-permute-start | bytes 98312 | tf_op jit(solution)/shard_map/ppermute | solution.py:524
  55.7 4.7 %collective-permute-start.22 = (f32[8,1024]{1,0:T(8,128)S(1)}, f32[8,1024]{1,0:T(8,128)S(1)}, u32[]{:S(2)}, u32[]{:S(2)}) collective-permute-start(f32[8,1024]{1,0:T(8,128)S(1)} %get-tuple-element.59), channel_id=1, source_target_pairs={{0,2},{1,3},{2,0},{3,1},{4,6},{5,7},{6,4},{7,5},{8,10},{9,11},{10,... | collective-permute-start | bytes 98312 | tf_op jit(solution)/shard_map/ppermute | solution.py:524

commit v8 on v7

--- a/solution.py
+++ b/solution.py
@@ -568,7 +568,7 @@
         )
     if paired:
         pieces = add_cut(out[0], swap(out[1], "dom", 1), owners // 2)
-        pieces = [pieces[0]] + [swap(pieces[k], "dom", 2 * k) for k in reversed(range(1, owners // 2))]
+        pieces = [pieces[0]] + [swap(pieces[k], "dom", 2 * k) for k in [owners // 2 - 1, *range(1, owners // 2 - 1)]]
     else:
         pieces = [lax.psum_scatter(out[0], "dom", scatter_dimension=0, tiled=True)]
     class_sums, class_weights = finish(pieces, cpg)

time: 61.1 us -> 60.9 us (level)
  no operation moved by 1% of the time
where the time goes in v8:
time: 60.9 us; the launch traced here: 60.7 us
  starting transfers between devices  24.9 us (41%)
  Pallas kernels  22.4 us (37%)
  waiting for transfers between devices  12.2 us (20%)
  between operations  0.9 us (1%)
    ppermute x23, starting transfers between devices, swap(): lax.ppermute(x, axis, [(i, i ^ k) for i in range(lax.axis_size(axis))])  24.9 us
    ppermute x23, waiting for transfers between devices, swap(): lax.ppermute(x, axis, [(i, i ^ k) for i in range(lax.axis_size(axis))])  12.2 us
    pallas_call x2, Pallas kernels, collect(): pl.pallas_call(functools.partial(collect_kernel, groups, parts, turn_coun...  8.69 us
    pallas_call x2, Pallas kernels, score(): pl.pallas_call(functools.partial(score_kernel, groups, scale, begin), gri...  6.22 us
    pallas_call x1, Pallas kernels, rotate(): pl.pallas_call(functools.partial(rotate_kernel, groups, pack), grid=(step...  4.23 us
    pallas_call x1, Pallas kernels, prepare(): pl.pallas_call(functools.partial(prepare_kernel, pack), in_specs=[VMEM] *...  1.49 us
  transfers between devices with their start and end apart: 23, of which 11 were waited for; matrix products, arithmetic and copies ran while one was open for 0% of the time, Pallas kernels for 15%

profile of v8, /device:TPU:0, one launch (start us, length us, event | category | flops | bytes accessed | tf_op | source)
XLA Modules:
  0.0 60.7 jit_solution(2212530359261622157)
XLA Ops:
  0.7 3.1 %collective-permute-start.1 = (bf16[4,1024]{1,0:T(4,128)(2,1)}, bf16[4,1024]{1,0:T(4,128)(2,1)S(1)}, u32[]{:S(2)}, u32[]{:S(2)}) collective-permute-start(bf16[4,1024]{1,0:T(4,128)(2,1)} %own_in.1), channel_id=1, source_target_pairs={{0,2},{1,3},{2,0},{3,1},{4,6},{5,7},{6,4},{7,5},{8,10},{9,11},{10,... | collective-permute-start | bytes 24584 | tf_op jit(solution)/shard_map/ppermute | solution.py:524
  3.8 2.5 %collective-permute-start.5 = (bf16[4,1024]{1,0:T(4,128)(2,1)}, bf16[4,1024]{1,0:T(4,128)(2,1)S(1)}, u32[]{:S(2)}, u32[]{:S(2)}) collective-permute-start(bf16[4,1024]{1,0:T(4,128)(2,1)} %own_in.1), channel_id=1, source_target_pairs={{0,6},{1,7},{2,4},{3,5},{4,2},{5,3},{6,0},{7,1},{8,14},{9,15},{10,... | collective-permute-start | bytes 24584 | tf_op jit(solution)/shard_map/ppermute | solution.py:524
  6.4 0.5 collective-permute-start.2
  6.9 2.6 %collective-permute-done.5.rest_6_ = bf16[4,1024]{1,0:T(4,128)(2,1)S(1)} collective-permute-done((bf16[4,1024]{1,0:T(4,128)(2,1)}, bf16[4,1024]{1,0:T(4,128)(2,1)S(1)}, u32[]{:S(2)}, u32[]{:S(2)}) %collective-permute-start.5) | collective-permute-done | bytes 8224 | tf_op jit(solution)/shard_map/ppermute | solution.py:524
  9.5 1.5 %collective-permute-done.3.rest_4_ = bf16[4,1024]{1,0:T(4,128)(2,1)S(1)} collective-permute-done((bf16[4,1024]{1,0:T(4,128)(2,1)}, bf16[4,1024]{1,0:T(4,128)(2,1)S(1)}, u32[]{:S(2)}, u32[]{:S(2)}) %collective-permute-start.3) | collective-permute-done | bytes 8224 | tf_op jit(solution)/shard_map/ppermute | solution.py:524
  11.1 0.8 %start.1 = (bf16[1024,1152]{1,0:T(8,128)(2,1)S(1)}, bf16[64,1024]{1,0:T(8,128)(2,1)S(1)}, s32[2,1024]{1,0:T(2,128)S(1)}, bf16[4,1024]{1,0:T(4,128)(2,1)S(1)}, bf16[64,64,128]{2,1,0:T(8,128)(2,1)S(1)}) custom-call(s32[128,256]{1,0:T(8,128)S(1)} %seed.1.numbers, bf16[4,1024]{1,0:T(4,128)(2,1)S(1)} %copy-done.4, bf16[1024,1024]{1,0:T(8,128)(2,1)S(1)} %copy-done, ...), custom_call_target="tpu_custom_call" | custom-call | flops 1048576 | tf_op jit(solution)/shard_map/start/pallas_call | solution.py:108
  12.2 4.2 %rotate.1 = (bf16[2048,1152]{1,0:T(8,128)(2,1)S(1)}, f32[1,128]{1,0:T(1,128)S(1)}) custom-call(bf16[64,1024]{1,0:T(8,128)(2,1)S(1)} %get-tuple-element.35.power2.power, bf16[64,64,128]{2,1,0:T(8,128)(2,1)S(1)} %get-tuple-element.36.turns, bf16[4,1024]{1,0:T(4,128)(2,1)S(1)} %get-tuple-element.37.rest_0_, bf16[4,1024]{1,0:T(4,128)(2,1)S(1)} %collective-permute-done.rest_1_, ...), custom_call_target="tpu_custom_call" | custom-call | flops 1073741824 | bytes 4194304 | tf_op jit(solution)/shard_map/rotate/pallas_call | solution.py:241
  16.4 3.1 %score.2 = (f32[512,128]{1,0:T(8,128)S(1)}, f32[512,128]{1,0:T(8,128)S(1)}, f32[512,128]{1,0:T(8,128)S(1)}, f32[512,128]{1,0:T(8,128)S(1)}) custom-call(s32[1]{0:T(128)} %bitcast.me, s32[1]{0:T(128)} %bitcast.1.here, bf16[1024,1152]{1,0:T(8,128)(2,1)S(1)} %get-tuple-element.34.weighted, s32[2,1024]{1,0:T(2,128)S(1)} %get-tuple-element.33.names, ...), custom_call_target="tpu_custom_call" | custom-call | flops 2415919104 | bytes 4718592 | tf_op jit(solution)/shard_map/score/pallas_call | solution.py:290
  19.6 2.5 %collective-permute-start.9 = (f16[512,128]{1,0:T(8,128)(2,1)S(1)}, f16[512,128]{1,0:T(8,128)(2,1)S(1)}, u32[]{:S(2)}, u32[]{:S(2)}) collective-permute-start(f16[512,128]{1,0:T(8,128)(2,1)S(1)} %convert_element_type.40), channel_id=1, source_target_pairs={{0,24},{8,16},{16,8},{24,0},{1,25},{9,17},{17,9},{25,1},{2,26},{10... | collective-permute-start | bytes 393224 | tf_op jit(solution)/shard_map/ppermute | solution.py:524
  22.1 0.5 collective-permute-start.8
  22.7 0.5 collective-permute-start.7
  23.2 3.1 %score.3 = (f32[512,128]{1,0:T(8,128)S(1)}, f32[512,128]{1,0:T(8,128)S(1)}, f32[512,128]{1,0:T(8,128)S(1)}, f32[512,128]{1,0:T(8,128)S(1)}) custom-call(s32[1]{0:T(128)} %bitcast.me, s32[1]{0:T(128)} %bitcast.1.here, bf16[1024,1152]{1,0:T(8,128)(2,1)S(1)} %get-tuple-element.34.weighted, s32[2,1024]{1,0:T(2,128)S(1)} %get-tuple-element.33.names, ...), custom_call_target="tpu_custom_call" | custom-call | flops 2415919104 | bytes 4718592 | tf_op jit(solution)/shard_map/score/pallas_call | solution.py:290
  26.4 2.5 %collective-permute-start.12 = (f16[512,128]{1,0:T(8,128)(2,1)S(1)}, f16[512,128]{1,0:T(8,128)(2,1)S(1)}, u32[]{:S(2)}, u32[]{:S(2)}) collective-permute-start(f16[512,128]{1,0:T(8,128)(2,1)S(1)} %convert_element_type.46), channel_id=1, source_target_pairs={{0,24},{8,16},{16,8},{24,0},{1,25},{9,17},{17,9},{25,1},{2,26},{10... | collective-permute-start | bytes 393224 | tf_op jit(solution)/shard_map/ppermute | solution.py:524
  28.9 0.5 collective-permute-start.11
  29.4 0.5 collective-permute-start.10
  30.2 2.5 %collective-permute-start.18 = (bf16[528,128]{1,0:T(8,128)(2,1)S(1)}, bf16[528,128]{1,0:T(8,128)(2,1)S(1)}, u32[]{:S(2)}, u32[]{:S(2)}) collective-permute-start(bf16[528,128]{1,0:T(8,128)(2,1)S(1)} %soften.2.after.rest_0_), channel_id=1, source_target_pairs={{0,24},{8,16},{16,8},{24,0},{1,25},{9,17},{17,9},{25,1},{2,26},{10... | collective-permute-start | bytes 405512 | tf_op jit(solution)/shard_map/ppermute | solution.py:524
  32.7 0.5 collective-permute-start.17
  33.2 1.5 %prepare.1 = (bf16[4096,256]{1,0:T(8,128)(2,1)S(1)}, bf16[1024,2048]{1,0:T(8,128)(2,1)S(1)}, f32[8,128]{1,0:T(8,128)S(1)}) custom-call(bf16[528,128]{1,0:T(8,128)(2,1)S(1)} %soften.2.after.rest_0_, bf16[64,64,128]{2,1,0:T(8,128)(2,1)S(1)} %get-tuple-element.36.turns, bf16[64,1024]{1,0:T(8,128)(2,1)S(1)} %get-tuple-element.35.power2.power), custom_call_target="tpu_custom_call" | custom-call | flops 4000000000 | tf_op jit(solution)/shard_map/prepare/pallas_call | solution.py:154
  34.7 0.6 %collective-permute-start.16 = (bf16[528,128]{1,0:T(8,128)(2,1)S(1)}, bf16[528,128]{1,0:T(8,128)(2,1)S(1)}, u32[]{:S(2)}, u32[]{:S(2)}) collective-permute-start(bf16[528,128]{1,0:T(8,128)(2,1)S(1)} %soften.2.after.rest_0_), channel_id=1, source_target_pairs={{0,8},{8,0},{16,24},{24,16},{1,9},{9,1},{17,25},{25,17},{2,10},{10... | collective-permute-start | bytes 405512 | tf_op jit(solution)/shard_map/ppermute | solution.py:524
  35.3 1.8 %collective-permute-done.11 = f16[512,128]{1,0:T(8,128)(2,1)S(1)} collective-permute-done((f16[512,128]{1,0:T(8,128)(2,1)S(1)}, f16[512,128]{1,0:T(8,128)(2,1)S(1)}, u32[]{:S(2)}, u32[]{:S(2)}) %collective-permute-start.11) | collective-permute-done | bytes 131104 | tf_op jit(solution)/shard_map/ppermute | solution.py:524
  37.4 2.0 %collective-permute-start.15 = (bf16[528,128]{1,0:T(8,128)(2,1)S(1)}, bf16[528,128]{1,0:T(8,128)(2,1)S(1)}, u32[]{:S(2)}, u32[]{:S(2)}) collective-permute-start(bf16[528,128]{1,0:T(8,128)(2,1)S(1)} %soften.3.rest_2_), channel_id=1, source_target_pairs={{0,24},{8,16},{16,8},{24,0},{1,25},{9,17},{17,9},{25,1},{2,26},{10... | collective-permute-start | bytes 405512 | tf_op jit(solution)/shard_map/ppermute | solution.py:524
  39.4 1.2 %collective-permute-start.14 = (bf16[528,128]{1,0:T(8,128)(2,1)S(1)}, bf16[528,128]{1,0:T(8,128)(2,1)S(1)}, u32[]{:S(2)}, u32[]{:S(2)}) collective-permute-start(bf16[528,128]{1,0:T(8,128)(2,1)S(1)} %soften.3.rest_2_), channel_id=1, source_target_pairs={{0,16},{8,24},{16,0},{24,8},{1,17},{9,25},{17,1},{25,9},{2,18},{10... | collective-permute-start | bytes 405512 | tf_op jit(solution)/shard_map/ppermute | solution.py:524
  40.6 0.3 collective-permute-start.13
  40.9 2.2 %collective-permute-done.17.rest_2_ = bf16[528,128]{1,0:T(8,128)(2,1)S(1)} collective-permute-done((bf16[528,128]{1,0:T(8,128)(2,1)S(1)}, bf16[528,128]{1,0:T(8,128)(2,1)S(1)}, u32[]{:S(2)}, u32[]{:S(2)}) %collective-permute-start.17) | collective-permute-done | bytes 135200 | tf_op jit(solution)/shard_map/ppermute | solution.py:524
  43.1 3.3 %collect.2 = (f32[512,4096]{1,0:T(8,128)S(1)}, f32[64,1024]{1,0:T(8,128)S(1)}, f32[1,1024]{1,0:T(1,128)S(1)}) custom-call(s32[1]{0:T(128)} %bitcast.me, s32[1]{0:T(128)} %bitcast.1.here, s32[2,1024]{1,0:T(2,128)S(1)} %get-tuple-element.33.names, bf16[1024,1152]{1,0:T(8,128)(2,1)S(1)} %get-tuple-element.34.weighted, ...), custom_call_target="tpu_custom_call" | custom-call | flops 2415919104 | bytes 4194304 | tf_op jit(solution)/shard_map/collect/pallas_call | solution.py:464
  46.7 5.4 %collect.3 = (f32[32,1024]{1,0:T(8,128)S(1)}, f32[32,1024]{1,0:T(8,128)S(1)}, f32[1,1024]{1,0:T(1,128)}) custom-call(s32[1]{0:T(128)} %bitcast.me, s32[1]{0:T(128)} %bitcast.1.here, s32[2,1024]{1,0:T(2,128)S(1)} %get-tuple-element.33.names, bf16[1024,1152]{1,0:T(8,128)(2,1)S(1)} %get-tuple-element.34.weighted, ...), custom_call_target="tpu_custom_call" | custom-call | flops 2415919104 | bytes 4194304 | tf_op jit(solution)/shard_map/collect/pallas_call | solution.py:464
  52.1 1.3 %collective-permute-done.19.right = f32[32,1024]{1,0:T(8,128)S(1)} collective-permute-done((f32[32,1024]{1,0:T(8,128)S(1)}, f32[32,1024]{1,0:T(8,128)S(1)}, u32[]{:S(2)}, u32[]{:S(2)}) %collective-permute-start.19) | collective-permute-done | bytes 131104 | tf_op jit(solution)/shard_map/ppermute | solution.py:524
  53.4 1.4 %collective-permute-start.20 = (f32[8,1024]{1,0:T(8,128)S(1)}, f32[8,1024]{1,0:T(8,128)S(1)}, u32[]{:S(2)}, u32[]{:S(2)}) collective-permute-start(f32[8,1024]{1,0:T(8,128)S(1)} %get-tuple-element.57), channel_id=1, source_target_pairs={{0,6},{1,7},{2,4},{3,5},{4,2},{5,3},{6,0},{7,1},{8,14},{9,15},{10,... | collective-permute-start | bytes 98312 | tf_op jit(solution)/shard_map/ppermute | solution.py:524
  54.9 3.0 %collective-permute-start.22 = (f32[8,1024]{1,0:T(8,128)S(1)}, f32[8,1024]{1,0:T(8,128)S(1)}, u32[]{:S(2)}, u32[]{:S(2)}) collective-permute-start(f32[8,1024]{1,0:T(8,128)S(1)} %get-tuple-element.59), channel_id=1, source_target_pairs={{0,4},{1,5},{2,6},{3,7},{4,0},{5,1},{6,2},{7,3},{8,12},{9,13},{10,... | collective-permute-start | bytes 98312 | tf_op jit(solution)/shard_map/ppermute | solution.py:524
  57.9 1.4 %collective-permute-done.20.refs_1_ = f32[8,1024]{1,0:T(8,128)S(1)} collective-permute-done((f32[8,1024]{1,0:T(8,128)S(1)}, f32[8,1024]{1,0:T(8,128)S(1)}, u32[]{:S(2)}, u32[]{:S(2)}) %collective-permute-start.20) | collective-permute-done | bytes 32800 | tf_op jit(solution)/shard_map/ppermute | solution.py:524
  59.4 0.7 %collective-permute-done.22.refs_3_ = f32[8,1024]{1,0:T(8,128)S(1)} collective-permute-done((f32[8,1024]{1,0:T(8,128)S(1)}, f32[8,1024]{1,0:T(8,128)S(1)}, u32[]{:S(2)}, u32[]{:S(2)}) %collective-permute-start.22) | collective-permute-done | bytes 32800 | tf_op jit(solution)/shard_map/ppermute | solution.py:524
  60.1 0.6 %finish.1 = (bf16[4,1024]{1,0:T(4,128)(2,1)}, f32[4,1024]{1,0:T(4,128)}) custom-call(f32[8,1024]{1,0:T(8,128)S(1)} %get-tuple-element.56.refs_0_, f32[8,1024]{1,0:T(8,128)S(1)} %collective-permute-done.20.refs_1_, f32[8,1024]{1,0:T(8,128)S(1)} %collective-permute-done.21.refs_2_, f32[8,1024]{1,0:T(8,128)S(1)} %collective-permute-done.22.refs_3_), custom_call_target="tpu_custom_call" | custom-call | flops 8192 | bytes 98304 | tf_op jit(solution)/shard_map/finish/pallas_call | solution.py:513
  (46 shorter events, 1.5 us)
Async XLA Ops:
  0.6 10.4 %copy-start.4 = (bf16[4,1024]{1,0:T(4,128)(2,1)S(1)}, bf16[4,1024]{1,0:T(4,128)(2,1)}, u32[]{:S(2)}) copy-start(bf16[4,1024]{1,0:T(4,128)(2,1)} %own_in.1) | copy-start | bytes 24580
  0.6 10.4 %copy-start.1 = (bf16[64,64,64]{2,1,0:T(8,128)(2,1)S(1)}, bf16[64,64,64]{2,1,0:T(8,128)(2,1)}, u32[]{:S(2)}) copy-start(bf16[64,64,64]{2,1,0:T(8,128)(2,1)} %turns.1) | copy-start | bytes 1572868
  0.7 10.4 %copy-start.2 = (f32[32,1024]{1,0:T(8,128)S(1)}, f32[32,1024]{1,0:T(8,128)}, u32[]{:S(2)}) copy-start(f32[32,1024]{1,0:T(8,128)} %table.1) | copy-start | bytes 393220
  0.7 10.4 %copy-start.5 = (s32[1024]{0:T(1024)S(1)}, s32[1024]{0:T(1024)}, u32[]{:S(2)}) copy-start(s32[1024]{0:T(1024)} %param.8) | copy-start | bytes 12292
  0.7 10.4 %copy-start.3 = (s32[1024,2]{0,1:T(2,128)S(1)}, s32[1024,2]{0,1:T(2,128)}, u32[]{:S(2)}) copy-start(s32[1024,2]{0,1:T(2,128)} %param.7) | copy-start | bytes 24580
  0.7 10.4 %copy-start = (bf16[1024,1024]{1,0:T(8,128)(2,1)S(1)}, bf16[1024,1024]{1,0:T(8,128)(2,1)}, u32[]{:S(2)}) copy-start(bf16[1024,1024]{1,0:T(8,128)(2,1)} %pixels.1) | copy-start | bytes 6291460
  0.7 5.7 %collective-permute-start.1 = (bf16[4,1024]{1,0:T(4,128)(2,1)}, bf16[4,1024]{1,0:T(4,128)(2,1)S(1)}, u32[]{:S(2)}, u32[]{:S(2)}) collective-permute-start(bf16[4,1024]{1,0:T(4,128)(2,1)} %own_in.1), channel_id=1, source_target_pairs={{0,2},{1,3},{2,0},{3,1},{4,6},{5,7},{6,4},{7,5},{8,10},{9,11},{10,... | collective-permute-start | bytes 24584 | tf_op jit(solution)/shard_map/ppermute | solution.py:524
  3.8 5.7 %collective-permute-start.5 = (bf16[4,1024]{1,0:T(4,128)(2,1)}, bf16[4,1024]{1,0:T(4,128)(2,1)S(1)}, u32[]{:S(2)}, u32[]{:S(2)}) collective-permute-start(bf16[4,1024]{1,0:T(4,128)(2,1)} %own_in.1), channel_id=1, source_target_pairs={{0,6},{1,7},{2,4},{3,5},{4,2},{5,3},{6,0},{7,1},{8,14},{9,15},{10,... | collective-permute-start | bytes 24584 | tf_op jit(solution)/shard_map/ppermute | solution.py:524
  6.3 4.8 %collective-permute-start.3 = (bf16[4,1024]{1,0:T(4,128)(2,1)}, bf16[4,1024]{1,0:T(4,128)(2,1)S(1)}, u32[]{:S(2)}, u32[]{:S(2)}) collective-permute-start(bf16[4,1024]{1,0:T(4,128)(2,1)} %own_in.1), channel_id=1, source_target_pairs={{0,4},{1,5},{2,6},{3,7},{4,0},{5,1},{6,2},{7,3},{8,12},{9,13},{10,... | collective-permute-start | bytes 24584 | tf_op jit(solution)/shard_map/ppermute | solution.py:524
  6.4 5.5 %collective-permute-start = (bf16[4,1024]{1,0:T(4,128)(2,1)}, bf16[4,1024]{1,0:T(4,128)(2,1)S(1)}, u32[]{:S(2)}, u32[]{:S(2)}) collective-permute-start(bf16[4,1024]{1,0:T(4,128)(2,1)} %own_in.1), channel_id=1, source_target_pairs={{0,1},{1,0},{2,3},{3,2},{4,5},{5,4},{6,7},{7,6},{8,9},{9,8},{10,11... | collective-permute-start | bytes 24584 | tf_op jit(solution)/shard_map/ppermute | solution.py:524
  6.4 5.5 %collective-permute-start.2 = (bf16[4,1024]{1,0:T(4,128)(2,1)S(1)}, bf16[4,1024]{1,0:T(4,128)(2,1)S(1)}, u32[]{:S(2)}, u32[]{:S(2)}) collective-permute-start(bf16[4,1024]{1,0:T(4,128)(2,1)S(1)} %collective-permute-done.1.rest_2_), channel_id=1, source_target_pairs={{0,1},{1,0},{2,3},{3,2},{4,5},{5,4},{6,7},{7,6},{8,9},{9,8},{10,11... | collective-permute-start | bytes 24584 | tf_op jit(solution)/shard_map/ppermute | solution.py:524
  9.5 2.4 %collective-permute-start.6 = (bf16[4,1024]{1,0:T(4,128)(2,1)S(1)}, bf16[4,1024]{1,0:T(4,128)(2,1)S(1)}, u32[]{:S(2)}, u32[]{:S(2)}) collective-permute-start(bf16[4,1024]{1,0:T(4,128)(2,1)S(1)} %collective-permute-done.5.rest_6_), channel_id=1, source_target_pairs={{0,1},{1,0},{2,3},{3,2},{4,5},{5,4},{6,7},{7,6},{8,9},{9,8},{10,11... | collective-permute-start | bytes 24584 | tf_op jit(solution)/shard_map/ppermute | solution.py:524
  11.0 1.2 %collective-permute-start.4 = (bf16[4,1024]{1,0:T(4,128)(2,1)S(1)}, bf16[4,1024]{1,0:T(4,128)(2,1)S(1)}, u32[]{:S(2)}, u32[]{:S(2)}) collective-permute-start(bf16[4,1024]{1,0:T(4,128)(2,1)S(1)} %collective-permute-done.3.rest_4_), channel_id=1, source_target_pairs={{0,1},{1,0},{2,3},{3,2},{4,5},{5,4},{6,7},{7,6},{8,9},{9,8},{10,11... | collective-permute-start | bytes 24584 | tf_op jit(solution)/shard_map/ppermute | solution.py:524
  19.6 9.8 %collective-permute-start.9 = (f16[512,128]{1,0:T(8,128)(2,1)S(1)}, f16[512,128]{1,0:T(8,128)(2,1)S(1)}, u32[]{:S(2)}, u32[]{:S(2)}) collective-permute-start(f16[512,128]{1,0:T(8,128)(2,1)S(1)} %convert_element_type.40), channel_id=1, source_target_pairs={{0,24},{8,16},{16,8},{24,0},{1,25},{9,17},{17,9},{25,1},{2,26},{10... | collective-permute-start | bytes 393224 | tf_op jit(solution)/shard_map/ppermute | solution.py:524
  22.1 7.8 %collective-permute-start.8 = (f16[512,128]{1,0:T(8,128)(2,1)S(1)}, f16[512,128]{1,0:T(8,128)(2,1)S(1)}, u32[]{:S(2)}, u32[]{:S(2)}) collective-permute-start(f16[512,128]{1,0:T(8,128)(2,1)S(1)} %convert_element_type.38), channel_id=1, source_target_pairs={{0,16},{8,24},{16,0},{24,8},{1,17},{9,25},{17,1},{25,9},{2,18},{10... | collective-permute-start | bytes 393224 | tf_op jit(solution)/shard_map/ppermute | solution.py:524
  22.7 7.3 %collective-permute-start.7 = (f16[512,128]{1,0:T(8,128)(2,1)S(1)}, f16[512,128]{1,0:T(8,128)(2,1)S(1)}, u32[]{:S(2)}, u32[]{:S(2)}) collective-permute-start(f16[512,128]{1,0:T(8,128)(2,1)S(1)} %convert_element_type.36), channel_id=1, source_target_pairs={{0,8},{8,0},{16,24},{24,16},{1,9},{9,1},{17,25},{25,17},{2,10},{10... | collective-permute-start | bytes 393224 | tf_op jit(solution)/shard_map/ppermute | solution.py:524
  26.4 8.3 %collective-permute-start.12 = (f16[512,128]{1,0:T(8,128)(2,1)S(1)}, f16[512,128]{1,0:T(8,128)(2,1)S(1)}, u32[]{:S(2)}, u32[]{:S(2)}) collective-permute-start(f16[512,128]{1,0:T(8,128)(2,1)S(1)} %convert_element_type.46), channel_id=1, source_target_pairs={{0,24},{8,16},{16,8},{24,0},{1,25},{9,17},{17,9},{25,1},{2,26},{10... | collective-permute-start | bytes 393224 | tf_op jit(solution)/shard_map/ppermute | solution.py:524
  28.9 8.2 %collective-permute-start.11 = (f16[512,128]{1,0:T(8,128)(2,1)S(1)}, f16[512,128]{1,0:T(8,128)(2,1)S(1)}, u32[]{:S(2)}, u32[]{:S(2)}) collective-permute-start(f16[512,128]{1,0:T(8,128)(2,1)S(1)} %convert_element_type.44), channel_id=1, source_target_pairs={{0,16},{8,24},{16,0},{24,8},{1,17},{9,25},{17,1},{25,9},{2,18},{10... | collective-permute-start | bytes 393224 | tf_op jit(solution)/shard_map/ppermute | solution.py:524
  29.4 7.7 %collective-permute-start.10 = (f16[512,128]{1,0:T(8,128)(2,1)S(1)}, f16[512,128]{1,0:T(8,128)(2,1)S(1)}, u32[]{:S(2)}, u32[]{:S(2)}) collective-permute-start(f16[512,128]{1,0:T(8,128)(2,1)S(1)} %convert_element_type.42), channel_id=1, source_target_pairs={{0,8},{8,0},{16,24},{24,16},{1,9},{9,1},{17,25},{25,17},{2,10},{10... | collective-permute-start | bytes 393224 | tf_op jit(solution)/shard_map/ppermute | solution.py:524
  30.2 10.4 %collective-permute-start.18 = (bf16[528,128]{1,0:T(8,128)(2,1)S(1)}, bf16[528,128]{1,0:T(8,128)(2,1)S(1)}, u32[]{:S(2)}, u32[]{:S(2)}) collective-permute-start(bf16[528,128]{1,0:T(8,128)(2,1)S(1)} %soften.2.after.rest_0_), channel_id=1, source_target_pairs={{0,24},{8,16},{16,8},{24,0},{1,25},{9,17},{17,9},{25,1},{2,26},{10... | collective-permute-start | bytes 405512 | tf_op jit(solution)/shard_map/ppermute | solution.py:524
  32.7 10.4 %collective-permute-start.17 = (bf16[528,128]{1,0:T(8,128)(2,1)S(1)}, bf16[528,128]{1,0:T(8,128)(2,1)S(1)}, u32[]{:S(2)}, u32[]{:S(2)}) collective-permute-start(bf16[528,128]{1,0:T(8,128)(2,1)S(1)} %soften.2.after.rest_0_), channel_id=1, source_target_pairs={{0,16},{8,24},{16,0},{24,8},{1,17},{9,25},{17,1},{25,9},{2,18},{10... | collective-permute-start | bytes 405512 | tf_op jit(solution)/shard_map/ppermute | solution.py:524
  34.7 8.4 %collective-permute-start.16 = (bf16[528,128]{1,0:T(8,128)(2,1)S(1)}, bf16[528,128]{1,0:T(8,128)(2,1)S(1)}, u32[]{:S(2)}, u32[]{:S(2)}) collective-permute-start(bf16[528,128]{1,0:T(8,128)(2,1)S(1)} %soften.2.after.rest_0_), channel_id=1, source_target_pairs={{0,8},{8,0},{16,24},{24,16},{1,9},{9,1},{17,25},{25,17},{2,10},{10... | collective-permute-start | bytes 405512 | tf_op jit(solution)/shard_map/ppermute | solution.py:524
  37.4 9.0 %collective-permute-start.15 = (bf16[528,128]{1,0:T(8,128)(2,1)S(1)}, bf16[528,128]{1,0:T(8,128)(2,1)S(1)}, u32[]{:S(2)}, u32[]{:S(2)}) collective-permute-start(bf16[528,128]{1,0:T(8,128)(2,1)S(1)} %soften.3.rest_2_), channel_id=1, source_target_pairs={{0,24},{8,16},{16,8},{24,0},{1,25},{9,17},{17,9},{25,1},{2,26},{10... | collective-permute-start | bytes 405512 | tf_op jit(solution)/shard_map/ppermute | solution.py:524
  39.4 7.2 %collective-permute-start.14 = (bf16[528,128]{1,0:T(8,128)(2,1)S(1)}, bf16[528,128]{1,0:T(8,128)(2,1)S(1)}, u32[]{:S(2)}, u32[]{:S(2)}) collective-permute-start(bf16[528,128]{1,0:T(8,128)(2,1)S(1)} %soften.3.rest_2_), channel_id=1, source_target_pairs={{0,16},{8,24},{16,0},{24,8},{1,17},{9,25},{17,1},{25,9},{2,18},{10... | collective-permute-start | bytes 405512 | tf_op jit(solution)/shard_map/ppermute | solution.py:524
  40.6 6.1 %collective-permute-start.13 = (bf16[528,128]{1,0:T(8,128)(2,1)S(1)}, bf16[528,128]{1,0:T(8,128)(2,1)S(1)}, u32[]{:S(2)}, u32[]{:S(2)}) collective-permute-start(bf16[528,128]{1,0:T(8,128)(2,1)S(1)} %soften.3.rest_2_), channel_id=1, source_target_pairs={{0,8},{8,0},{16,24},{24,16},{1,9},{9,1},{17,25},{25,17},{2,10},{10... | collective-permute-start | bytes 405512 | tf_op jit(solution)/shard_map/ppermute | solution.py:524
  52.1 1.3 %collective-permute-start.19 = (f32[32,1024]{1,0:T(8,128)S(1)}, f32[32,1024]{1,0:T(8,128)S(1)}, u32[]{:S(2)}, u32[]{:S(2)}) collective-permute-start(f32[32,1024]{1,0:T(8,128)S(1)} %get-tuple-element.55), channel_id=1, source_target_pairs={{0,1},{1,0},{2,3},{3,2},{4,5},{5,4},{6,7},{7,6},{8,9},{9,8},{10,11... | collective-permute-start | bytes 393224 | tf_op jit(solution)/shard_map/ppermute | solution.py:524
  53.4 5.8 %collective-permute-start.20 = (f32[8,1024]{1,0:T(8,128)S(1)}, f32[8,1024]{1,0:T(8,128)S(1)}, u32[]{:S(2)}, u32[]{:S(2)}) collective-permute-start(f32[8,1024]{1,0:T(8,128)S(1)} %get-tuple-element.57), channel_id=1, source_target_pairs={{0,6},{1,7},{2,4},{3,5},{4,2},{5,3},{6,0},{7,1},{8,14},{9,15},{10,... | collective-permute-start | bytes 98312 | tf_op jit(solution)/shard_map/ppermute | solution.py:524
  54.9 4.6 %collective-permute-start.21 = (f32[8,1024]{1,0:T(8,128)S(1)}, f32[8,1024]{1,0:T(8,128)S(1)}, u32[]{:S(2)}, u32[]{:S(2)}) collective-permute-start(f32[8,1024]{1,0:T(8,128)S(1)} %get-tuple-element.58), channel_id=1, source_target_pairs={{0,2},{1,3},{2,0},{3,1},{4,6},{5,7},{6,4},{7,5},{8,10},{9,11},{10,... | collective-permute-start | bytes 98312 | tf_op jit(solution)/shard_map/ppermute | solution.py:524
  54.9 5.2 %collective-permute-start.22 = (f32[8,1024]{1,0:T(8,128)S(1)}, f32[8,1024]{1,0:T(8,128)S(1)}, u32[]{:S(2)}, u32[]{:S(2)}) collective-permute-start(f32[8,1024]{1,0:T(8,128)S(1)} %get-tuple-element.59), channel_id=1, source_target_pairs={{0,4},{1,5},{2,6},{3,7},{4,0},{5,1},{6,2},{7,3},{8,12},{9,13},{10,... | collective-permute-start | bytes 98312 | tf_op jit(solution)/shard_map/ppermute | solution.py:524
